TPU v7x, 32 devices: a whole 2x2x4 slice. The times are simulated.
32 devices in a mesh: wide: 16 (over z, y, core), narrow: 2 (over x).
Axes of the slice: x: 2, y: 2, z: 4, core: 2. Of those that a mesh axis runs over, the one named last changes fastest.
Arguments:
- signal_samples: float32 [512, 512], P(('wide', 'narrow')), may hold values from -9 to 9
- present_mask: int32 [512, 512], P(('wide', 'narrow')), may hold values 0 or 1
- embedder_inner_matrix: bfloat16 [32, 1536], replicated, may hold values from -1 to 1
- embedder_inner_offset: float32 [1536], replicated, may hold values from -3 to 3
- embedder_final_matrix: bfloat16 [1536, 384], replicated, may hold values from -0.15625 to 0.15625
- embedder_shortcut_matrix: bfloat16 [32, 384], replicated, may hold values from -1 to 1
- embedder_final_offset: float32 [384], replicated, may hold values from -3 to 3
- mixer_prescale_factor: float32 [384], replicated, may hold values from 0.1 to 1.9
- probe_matrix: bfloat16 [384, 512], replicated, may hold values from -0.3125 to 0.3125
- address_matrix: bfloat16 [384, 512], replicated, may hold values from -0.3125 to 0.3125
- content_matrix: bfloat16 [384, 512], replicated, may hold values from -0.3125 to 0.3125
- mixer_merge_matrix: bfloat16 [512, 384], replicated, may hold values from -0.75 to 0.75
- perceptron_prescale_factor: float32 [384], replicated, may hold values from 0.1 to 1.9
- expand_matrix: bfloat16 [384, 1536], replicated, may hold values from -0.3125 to 0.3125
- contract_matrix: bfloat16 [1536, 384], replicated, may hold values from -0.15625 to 0.15625
- readout_inner_matrix: bfloat16 [384, 1536], replicated, may hold values from -0.3125 to 0.3125
- readout_inner_offset: float32 [1536], replicated, may hold values from -3 to 3
- readout_horizon_matrix: bfloat16 [1536, 576], P(None, 'narrow'), may hold values from -0.15625 to 0.15625
- readout_shortcut_matrix: bfloat16 [384, 576], P(None, 'narrow'), may hold values from -0.3125 to 0.3125
- readout_offset: bfloat16 [576], P('narrow'), may hold values from -3 to 3
- prediction_cotangent: float32 [16384, 576], P('wide', 'narrow'), may hold values from -6 to 6
Outputs:
- prediction_native: float32 [16384, 576], P('wide', 'narrow')
- series_grad: float32 [512, 512], P(('wide', 'narrow'))
- grad_tok_in_w: float32 [32, 1536], replicated
- grad_tok_in_b: float32 [1536], replicated
- grad_tok_out_w: float32 [1536, 384], replicated
- grad_tok_skip_w: float32 [32, 384], replicated
- grad_tok_out_b: float32 [384], replicated
- grad_norm1_gain: float32 [384], replicated
- grad_w_query: float32 [384, 512], replicated
- grad_w_key: float32 [384, 512], replicated
- grad_w_value: float32 [384, 512], replicated
- grad_w_out: float32 [512, 384], replicated
- grad_norm2_gain: float32 [384], replicated
- grad_w_up: float32 [384, 1536], replicated
- grad_w_down: float32 [1536, 384], replicated
- grad_head_in_w: float32 [384, 1536], replicated
- grad_head_in_b: float32 [1536], replicated
- grad_head_out_w: float32 [1536, 576], P(None, 'narrow')
- grad_head_skip_w: float32 [384, 576], P(None, 'narrow')
- grad_head_out_b: float32 [576], P('narrow')
All inputs are finite; a program needn't handle non-finite values. No bound on the sum of `present_mask` on one device may be relied on, other than what follows from the above.
Results may differ from a plain program's by a relative error of at most 0.017.
Values may be sent and summed in bfloat16 or wider, within the bound.
No kernel may reach another device: no remote copies, remote signals or barrier semaphores. Data moves between devices by JAX's collectives and lax.ppermute only.
A program may use at most 192 MiB of HBM per device.

v0:
```python
import functools

import jax
import jax.numpy as jnp
from jax import lax
from jax.experimental import pallas as pl
from jax.experimental.pallas import tpu as pltpu
from jax.sharding import PartitionSpec as P

HEADS = 8
HEAD_DIM = 64
EPS = 1e-06
SCALE = HEAD_DIM ** (-0.5)
bf = jnp.bfloat16
f32 = jnp.float32
TILE = 384
AXES = ("wide", "narrow")
MIB = 1 << 20


def dot(a, b):
    return lax.dot_general(a, b, (((1,), (0,)), ((), ())), preferred_element_type=f32)


def dot_nt(a, b):
    return lax.dot_general(a, b, (((1,), (1,)), ((), ())), preferred_element_type=f32)


def dot_tn(a, b):
    return lax.dot_general(a, b, (((0,), (0,)), ((), ())), preferred_element_type=f32)


class Chain:
    def __init__(self):
        self.last = None

    def __call__(self, kernel, outs, args, scratch=(), limit=16, raw=()):
        vmem = pl.BlockSpec(memory_space=pltpu.VMEM)
        hbm = pl.BlockSpec(memory_space=pl.ANY)
        args, raw = list(args), [pltpu.with_memory_space_constraint(v, pltpu.HBM) for v in raw]
        deps = [] if self.last is None or any(a is self.last for a in args) else [self.last]
        n, d = len(args) + len(raw), len(deps)

        def body(*refs):
            kernel(*refs[:n], *refs[n + d:])

        name = getattr(kernel, "__name__", None) or kernel.func.__name__
        res = list(pl.pallas_call(
            body,
            name=name,
            out_shape=[jax.ShapeDtypeStruct(s, d) for s, d in outs],
            in_specs=[vmem] * len(args) + [pl.BlockSpec(memory_space=pltpu.HBM)] * len(raw) + [hbm] * d,
            out_specs=[vmem] * len(outs),
            scratch_shapes=list(scratch),
            cost_estimate=pl.CostEstimate(flops=1000, bytes_accessed=1000, transcendentals=0),
            compiler_params=pltpu.CompilerParams(vmem_limit_bytes=limit * MIB),
        )(*args, *raw, *deps))
        self.last = min(res, key=lambda r: r.size)
        return res


def silu_parts(v):
    s = 0.5 * jnp.tanh(0.5 * v) + 0.5
    h = v * s
    return h, s + h * (1.0 - s)


def iota(shape, dim):
    return lax.broadcasted_iota(jnp.int32, shape, dim)


def series_stats(samples, observed, patch):
    first = jnp.where(iota(samples.shape, 1) < patch, observed, 0.0)
    count = jnp.maximum(jnp.sum(first, axis=1, keepdims=True), 1.0)
    center = jnp.sum(first * samples, axis=1, keepdims=True) / count
    offset = samples - center
    spread = jnp.sum(first * offset * offset, axis=1, keepdims=True) / count
    sigma = jnp.sqrt(jnp.maximum(spread, 1.0))
    return first, count, center, offset, spread, sigma


def rms(v):
    return lax.rsqrt(jnp.mean(v * v, axis=-1, keepdims=True) + EPS)


def norm_back(g, v, gain):
    r = rms(v)
    u = v * r
    w = g * gain
    grad_gain = jnp.sum(g * u, axis=0, keepdims=True)
    return r * (w - u * jnp.mean(w * u, axis=-1, keepdims=True)), grad_gain


def token_row(v, rows):
    series = v.shape[0]
    own = iota((series, rows), 1) // (rows // series) == iota((series, rows), 0)
    return jnp.sum(jnp.where(own, v, 0.0), axis=0, keepdims=True)


def series_column(v, series):
    rows = v.shape[1]
    own = iota((series, rows), 1) // (rows // series) == iota((series, rows), 0)
    return jnp.sum(jnp.where(own, v, 0.0), axis=1, keepdims=True)


def me_of(masks, count):
    index = lax.axis_index("wide") * count + lax.axis_index("narrow")
    out = jnp.int32(0)
    for m in masks:
        out = out * 2 + (index // m) % 2
    return out


def prepare_kernel(count, rows, bias, cot, whz, wrs, *refs):
    cots, (own, mine, short) = refs[:count - 1], refs[count - 1:count + 2]
    wide_cots, half, shortcut, sems = refs[count + 2:]
    narrow = lax.axis_index("narrow")
    core = lax.axis_index("wide") % 2
    width, dim = half.shape[1], shortcut.shape[1]

    def tokens(r):
        return cot.at[:, pl.ds(pl.multiple_of((narrow ^ r) * rows, 128), rows)]

    copies = [
        pltpu.make_async_copy(whz.at[:, pl.ds(pl.multiple_of(core * width, 128), width)], half, sems.at[0]),
        pltpu.make_async_copy(wrs, shortcut, sems.at[1]),
        pltpu.make_async_copy(tokens(0), own, sems.at[2]),
    ] + [pltpu.make_async_copy(tokens(r), wide_cots.at[r - 1], sems.at[2 + r]) for r in range(1, count)]
    for c in copies:
        c.start()
    for c in copies[:2]:
        c.wait()
    short[:, :dim] = shortcut[...]
    short[:, dim:] = dot_tn(bias[...].astype(f32)[None, :].astype(bf), jnp.ones((1, 128), bf)).astype(bf)
    mine[:, :width] = half[...]
    part = (dim + 128) // 2
    mine[:, width:] = short[:, pl.ds(pl.multiple_of(core * part, 128), part)]
    for c in copies[2:]:
        c.wait()
    for r in range(1, count):
        cots[r - 1][...] = wide_cots[r - 1].astype(bf)


def gate_kernel(v, out):
    out[...] = v[...]


def tokens_kernel(patch, *refs):
    samples, mask, bi, bfin, gain = refs[:5]
    hbm = refs[5:16]
    patches, hid, dhid, embed, normed, qkv, sigma_row, center_row = refs[16:24]
    vmem, sems = refs[24:35], refs[35]
    copies = [pltpu.make_async_copy(h, v, sems.at[i]) for i, (h, v) in enumerate(zip(hbm, vmem))]
    for c in copies:
        c.start()
    wi, wfin, wskip, wq, wk, wv = vmem[:6]
    series, points = samples.shape
    tokens = points // patch
    rows = series * tokens
    observed = mask[...].astype(f32)
    _, _, center, offset, _, sigma = series_stats(samples[...], observed, patch)
    sigma_row[...] = token_row(sigma, rows)
    center_row[...] = token_row(center, rows)
    scaled = (observed * offset / sigma).astype(bf)
    spread_rows = (iota((rows, series), 0) // tokens == iota((rows, series), 1)).astype(f32).astype(bf)
    own = (iota((rows, points), 1) // patch == iota((rows, points), 0) % tokens).astype(f32)
    col = iota((points, 2 * patch), 0) % patch
    lane = iota((points, 2 * patch), 1)
    fold_s = (col == lane).astype(f32).astype(bf)
    fold_o = (col + patch == lane).astype(f32).astype(bf)
    es = (dot(spread_rows, scaled) * own).astype(bf)
    eo = (dot(spread_rows, observed.astype(bf)) * own).astype(bf)
    p = (dot(es, fold_s) + dot(eo, fold_o)).astype(bf)
    patches[...] = p
    for c in copies[:3]:
        c.wait()
    acc = dot(p, wskip[...]) + bfin[...][None, :]
    for j in range(0, wi.shape[1], TILE):
        t = slice(j, j + TILE)
        h, d = silu_parts(dot(p, wi[:, t]) + bi[t][None, :])
        h = h.astype(bf)
        hid[:, t] = h
        dhid[:, t] = d.astype(bf)
        acc = acc + dot(h, wfin[t, :])
    embed[...] = acc
    n = (acc * rms(acc) * gain[...][None, :]).astype(bf)
    normed[...] = n
    inner = wq.shape[1]
    for i, w in enumerate((wq, wk, wv)):
        copies[3 + i].wait()
        qkv[:, i * inner:(i + 1) * inner] = dot(n, w[...]).astype(bf)
    for c in copies[6:]:
        c.wait()


def block_mask():
    return (iota((128, 256), 0) // 32 == iota((128, 256), 1) // 64).astype(f32).astype(bf)


def spread_heads(v, keep):
    return jnp.concatenate([v] * 4, axis=0) * keep


def pick_heads(v):
    head = iota((32, 256), 1) // 64
    out = v[0:32]
    for h in range(1, 4):
        out = jnp.where(head == h, v[32 * h:32 * h + 32], out)
    return out


def pairs(rows):
    for i in range(rows // 16):
        yield i, slice(32 * (i // 2), 32 * (i // 2) + 32), 256 * (i % 2)


def attend_kernel(qkv, probs, mixed):
    keep = block_mask()
    inner = HEADS * HEAD_DIM
    rows = qkv.shape[0]
    for i, s, c in pairs(rows):
        q = spread_heads(qkv[s, c:c + 256], keep)
        probs[i] = dot_nt(qkv[s, inner + c:inner + c + 256], q)
    for i in range(0, rows // 16, 4):
        v = probs[i:i + 4] * SCALE
        e = jnp.exp(v - jnp.max(v, axis=1, keepdims=True))
        probs[i:i + 4] = e / jnp.sum(e, axis=1, keepdims=True)
    for i, s, c in pairs(rows):
        v = qkv[s, 2 * inner + c:2 * inner + c + 256]
        mixed[s, c:c + 256] = pick_heads(dot_tn(probs[i].astype(bf), v)).astype(bf)


def ffn_kernel(embed, mixed, wm, gain, we, wc, wri, bri, middle, normed, hid, dhid, states, hidh, dh):
    mid = embed[...] + dot(mixed[...], wm[...])
    middle[...] = mid
    n = (mid * rms(mid) * gain[...][None, :]).astype(bf)
    normed[...] = n
    acc = mid
    for j in range(0, we.shape[1], TILE):
        t = slice(j, j + TILE)
        h, d = silu_parts(dot(n, we[:, t]))
        h = h.astype(bf)
        hid[:, t] = h
        dhid[:, t] = d.astype(bf)
        acc = acc + dot(h, wc[t, :])
    st = acc.astype(bf)
    states[...] = st
    for j in range(0, wri.shape[1], TILE):
        t = slice(j, j + TILE)
        h, d = silu_parts(dot(st, wri[:, t]) + bri[t][None, :])
        hidh[:, t] = h.astype(bf)
        dh[:, t] = d.astype(bf)


def put_slabs(scr, me, tile, value, offset, slabs):
    for i in range(8):
        for n, k in enumerate(slabs):
            scr[(8 * tile + i) ^ me, offset + 48 * n:offset + 48 * n + 48, :] = (
                value[48 * i:48 * i + 48, 128 * k:128 * k + 128])


def ship(parts, keep, send):
    at = 0
    for p in parts:
        n, rows = p.shape[0] // 2, p.shape[1]
        keep[:, at:at + rows] = p[:n]
        send[:, at:at + rows] = p[n:]
        at += rows


def first_rows(cols):
    return 16 * ((cols + 31) // 32)


def rows_of(tmp, row, v):
    for j in range(0, v.shape[1], 128):
        tmp[row:row + 1, :] = v[:, j:j + 128]
        row += 1
    return row


def columns_kernel(count, masks, *refs):
    states, hidh, sigma = refs[:3]
    cots, refs = refs[3:3 + count], refs[3 + count:]
    groups = max(count // 2, 1)
    outs, (tmp, *scrs) = refs[:2 * groups], refs[2 * groups:]
    me = me_of(masks, count)
    st = states[...]
    width = hidh.shape[1]
    cols = tmp.shape[0]
    cut = first_rows(cols)
    for r in range(count):
        turned = (cots[r][...].astype(f32) * sigma[...]).astype(bf)
        scr_a, scr_b = scrs[2 * (r // 2):2 * (r // 2) + 2]

        def put(c, v):
            rel = c ^ me
            core, y, z = rel // 8, (rel // 4) % 2, rel % 4
            scr_a[core * 16 + (r % 2) * 8 + y * 4 + z] = v[:cut]
            scr_b[core * 16 + y * 8 + (r % 2) * 4 + z] = v[cut:]

        for j in range(0, width, TILE):
            v = dot(turned, hidh[:, j:j + TILE]).astype(bf)
            for i in range(TILE // 128):
                put(j // 128 + i, v[:, 128 * i:128 * i + 128])
        v = dot(turned, st).astype(bf)
        for i in range(st.shape[1] // 128):
            put(width // 128 + i, v[:, 128 * i:128 * i + 128])
        tmp[...] = jnp.zeros_like(tmp)
        bias = dot_nt(jnp.ones((8, turned.shape[1]), bf), turned)
        for row, j in enumerate(range(0, cols, 128)):
            n = min(128, cols - j)
            tmp[row:row + 1, 0:n] = bias[0:1, j:j + n]
        put(15, tmp[...].astype(bf))
    for i in range(groups):
        ship(scrs[2 * i:2 * i + 2], *outs[2 * i:2 * i + 2])


def head_kernel(count, *refs):
    dh, sigma, wri = refs[:3]
    refs = refs[3:]
    cots, refs = refs[:count], refs[count:]
    whz, refs = refs[0], refs[1:]
    far, refs = refs[:2 * (count - 1)], refs[2 * (count - 1):]
    short, refs = refs[0], refs[1:]
    gstates, gpre, sums = refs[:3]
    mats, shorts = refs[3:2 + count], refs[2 + count:1 + 2 * count]
    width = wri.shape[1]
    dim = wri.shape[0]
    half, part = width // 2, (dim + 128) // 2
    core = lax.axis_index("wide") % 2
    for r in range(count - 1):
        for k, c in enumerate((core, 1 - core)):
            mats[r][:, pl.ds(pl.multiple_of(c * half, 128), half)] = far[2 * r + k][:, :half]
            shorts[r][:, pl.ds(pl.multiple_of(c * part, 128), part)] = far[2 * r + k][:, half:]
    mats = [whz] + list(mats)
    shorts = [short] + list(shorts)
    grads = [(c[...].astype(f32) * sigma[...]).astype(bf).T for c in cots]
    for j in range(0, width, TILE):
        t = slice(j, j + TILE)
        acc = dot(grads[0], mats[0][:, t])
        for r in range(1, count):
            acc = acc + dot(grads[r], mats[r][:, t])
        gp = (acc * dh[:, t].astype(f32)).astype(bf)
        gpre[:, t] = gp
        sums[:, t] = jnp.sum(gp.astype(f32), axis=0, keepdims=True)
    acc = dot_nt(gpre[...], wri[...])
    for r in range(count):
        acc = acc + dot(grads[r], shorts[r][:, :dim])
    gstates[...] = acc.astype(bf)


def ffn_back_kernel(count, masks, gstates, states, gpre, sums, hid, dhid, normed, middle, wc, we, gain,
                    gmiddle, keep, send, scr_a, scr_b, tmp):
    me_a, me_b = (me_of(m, count) for m in masks)
    g = gstates[...]
    nt = normed[...].T
    acc = None
    for j in range(4):
        t = slice(TILE * j, TILE * j + TILE)
        gp = (dot_nt(g, wc[t, :]) * dhid[:, t].astype(f32)).astype(bf)
        part = dot_nt(gp, we[:, t])
        acc = part if acc is None else acc + part
        up = dot(nt, gp).astype(bf)
        put_slabs(scr_a, me_a, j, up, 160, (0,))
        put_slabs(scr_b, me_b, j, up, 0, (1, 2))
        put_slabs(scr_b, me_b, j, dot_tn(hid[:, t], g).astype(bf), 96, (0, 1, 2))
    back, gg = norm_back(acc, middle[...], gain[...][None, :])
    gmiddle[...] = (g.astype(f32) + back).astype(bf)
    st = states[...].T
    for j in range(4):
        put_slabs(scr_a, me_a, j, dot(st, gpre[:, TILE * j:TILE * j + TILE]).astype(bf), 0, (0, 1, 2))
    scr_a[:, 144:160, :] = jnp.zeros((32, 16, 128), bf)
    tmp[...] = jnp.zeros_like(tmp)
    row = rows_of(tmp, 0, sums[...])
    rows_of(tmp, row, gg)
    scr_a[me_a, 144:160, :] = tmp[...].astype(bf)
    ship((scr_a, scr_b), keep, send)


def attend_back_kernel(gmiddle, wm, qkv, probs, gqkv, gmix, gprobs, low):
    keep = block_mask()
    inner = HEADS * HEAD_DIM
    rows = qkv.shape[0]
    gmix[...] = dot_nt(gmiddle[...], wm[...]).astype(bf)
    for i, s, c in pairs(rows):
        g = spread_heads(gmix[s, c:c + 256], keep)
        gprobs[i] = dot_nt(qkv[s, 2 * inner + c:2 * inner + c + 256], g)
        gqkv[s, 2 * inner + c:2 * inner + c + 256] = dot(probs[i].astype(bf), g).astype(bf)
    for i in range(0, rows // 16, 4):
        p, g = probs[i:i + 4], gprobs[i:i + 4]
        low[i:i + 4] = (p * (g - jnp.sum(g * p, axis=1, keepdims=True))).astype(bf)
    for i, s, c in pairs(rows):
        ds = low[i]
        q = spread_heads(qkv[s, c:c + 256], keep)
        k = qkv[s, inner + c:inner + c + 256]
        gqkv[s, c:c + 256] = (pick_heads(dot_tn(ds, k)) * SCALE).astype(bf)
        gqkv[s, inner + c:inner + c + 256] = (dot(ds, q) * SCALE).astype(bf)


def project_back_kernel(count, masks, gqkv, gmiddle, mixed, normed, embed, wq, wk, wv, gain, gembed, ggain, part_a, part_b):
    me_a, me_b = (me_of(m, count) for m in masks)
    inner = wq.shape[1]
    acc = dot_nt(gqkv[:, :inner], wq[...])
    acc = acc + dot_nt(gqkv[:, inner:2 * inner], wk[...])
    acc = acc + dot_nt(gqkv[:, 2 * inner:], wv[...])
    back, gg = norm_back(acc, embed[...], gain[...][None, :])
    ggain[...] = gg
    gm = gmiddle[...]
    gembed[...] = (gm.astype(f32) + back).astype(bf)
    nt = normed[...].T
    for j in range(4):
        put_slabs(part_a, me_a, j, dot(nt, gqkv[:, TILE * j:TILE * j + TILE]).astype(bf), 0, (0, 1, 2))
    v = dot_tn(mixed[...], gm).astype(bf)
    for i in range(32):
        for k in range(3):
            part_b[i ^ me_b, 16 * k:16 * k + 16, :] = v[16 * i:16 * i + 16, 128 * k:128 * k + 128]


def tokens_back_kernel(count, masks, patch, gembed, hid, dhid, patches, wfin, wskip, wi, gain_one, part_a, part_b,
                       gscaled, keep, send, scr_a, scr_b, tmp):
    me_a, me_b = (me_of(m, count) for m in masks)
    g = gembed[...]
    p = patches[...]
    pt = p.T
    tmp[...] = jnp.zeros_like(tmp)
    gpat = dot_nt(g, wskip[...])
    row = 480
    for j in range(4):
        t = slice(TILE * j, TILE * j + TILE)
        gp = (dot_nt(g, wfin[t, :]) * dhid[:, t].astype(f32)).astype(bf)
        gpat = gpat + dot_nt(gp, wi[:, t])
        v = dot(pt, gp)
        for i in range(3):
            c = 3 * j + i
            tmp[32 * c:32 * c + 32, :] = v[:, 128 * i:128 * i + 128]
        row = rows_of(tmp, row, jnp.sum(gp.astype(f32), axis=0, keepdims=True))
        put_slabs(scr_b, me_b, j, dot_tn(hid[:, t], g).astype(bf), 0, (0, 1, 2))
    v = dot(pt, g)
    for i in range(3):
        tmp[384 + 32 * i:416 + 32 * i, :] = v[:, 128 * i:128 * i + 128]
    row = rows_of(tmp, row, jnp.sum(g.astype(f32), axis=0, keepdims=True))
    rows_of(tmp, row, gain_one[...])
    for b in range(32):
        scr_a[b ^ me_a] = tmp[16 * b:16 * b + 16].astype(bf)
    ship((part_a, scr_a, scr_b, part_b), keep, send)
    series, points = gscaled.shape
    tokens = points // patch
    rows = series * tokens
    lane = iota((2 * patch, points), 1) % patch
    fold = (iota((2 * patch, points), 0) == lane).astype(f32).astype(bf)
    own = (iota((rows, points), 1) // patch == iota((rows, points), 0) % tokens).astype(f32)
    high = gpat.astype(bf)
    low = (gpat - high.astype(f32)).astype(bf)
    full = (dot(high, fold) + dot(low, fold)) * own
    gscaled[...] = jnp.sum(full.reshape(series, tokens, points), axis=1)


def forecast_kernel(count, patch, *refs):
    samples, mask, gscaled, hid, states, sigma_row, center_row = refs[:7]
    refs = refs[7:]
    mats, refs = refs[:count], refs[count:]
    short, refs = refs[:count], refs[count:]
    cots, refs = refs[:count], refs[count:]
    preds, series_grad = refs[:count], refs[count]
    sg = sigma_row[...]
    ct = center_row[...]
    st = states[...]
    dim = st.shape[1]
    row_c, row_s = 0.0, 0.0
    for r in range(count):
        raw = dot_nt(mats[r][...], hid[...]) + dot_nt(short[r][:, :dim], st) + short[r][:, dim:dim + 1].astype(f32)
        preds[r][...] = (raw * sg + ct).astype(preds[r].dtype)
        c = cots[r][...].astype(f32)
        row_c = row_c + jnp.sum(c, axis=0, keepdims=True)
        row_s = row_s + jnp.sum(c * raw, axis=0, keepdims=True)
    observed = mask[...].astype(f32)
    series = samples.shape[0]
    first, cnt, center, offset, spread, sigma = series_stats(samples[...], observed, patch)
    out_c = series_column(row_c, series)
    out_s = series_column(row_s, series)
    og = observed * gscaled[...]
    g_center = out_c - jnp.sum(og, axis=1, keepdims=True) / sigma
    g_sigma = out_s - jnp.sum(og * offset, axis=1, keepdims=True) / (sigma * sigma)
    g_spread = jnp.where(spread > 1.0, g_sigma * 0.5 / sigma, 0.0)
    g_center = g_center - g_spread * 2.0 * jnp.sum(first * offset, axis=1, keepdims=True) / cnt
    series_grad[...] = og / sigma + g_spread * 2.0 * first * offset / cnt + g_center * first / cnt


def place_kernel(count, *refs):
    preds, out = refs[:count], refs[count]
    rows = preds[0].shape[1]
    narrow = lax.axis_index("narrow")
    for r in range(count):
        out[:, pl.ds(pl.multiple_of((narrow ^ r) * rows, 128), rows)] = preds[r][...].astype(f32)


def added(a, b):
    return (a.astype(f32) + b.astype(f32)).astype(bf)


def add_core_kernel(keep, got, a0, a1, b0, b1):
    cut = a0.shape[1]
    n = keep.shape[0] // 2
    for k in range(2 * n):
        v = added(keep[k], got[k])
        (a0, a1)[k // n][k % n] = v[:cut]
        (b0, b1)[k // n][k % n] = v[cut:]


def add_pair_kernel(a, a_got, b, b_got, a0, a1, b0, b1):
    n = a.shape[0] // 2
    for k in range(2 * n):
        (a0, a1)[k // n][k % n] = added(a[k], a_got[k])
        (b0, b1)[k // n][k % n] = added(b[k], b_got[k])


def add_merge_kernel(a, a_got, b, b_got, *outs):
    n, cut = outs[0].shape[0], a.shape[1]
    for i, o in enumerate(outs):
        for k in range(n):
            o[k, :cut] = added(a[i * n + k], a_got[i * n + k])
            o[k, cut:] = added(b[i * n + k], b_got[i * n + k])


def add_split_kernel(v, got, *outs):
    n = outs[0].shape[0]
    for i, o in enumerate(outs):
        o[...] = added(v[i * n:i * n + n], got[i * n:i * n + n])


def join_split_kernel(cut, here, got, a, b):
    n = here.shape[0]
    for k, v in enumerate((here, got)):
        a[k * n:k * n + n] = v[:, :cut]
        b[k * n:k * n + n] = v[:, cut:]


def join_kernel(*refs):
    ins, out = refs[:-1], refs[-1]
    n = ins[0].shape[0]
    for k, v in enumerate(ins):
        out[k * n:k * n + n] = v[...]


def join_pair_kernel(a, a_got, b, b_got, a_out, b_out):
    n = a.shape[0]
    for k, (v, w) in enumerate(((a, b), (a_got, b_got))):
        a_out[k * n:k * n + n] = v[...]
        b_out[k * n:k * n + n] = w[...]


def join_merge_kernel(a, a_got, b, b_got, out):
    n, cut = a.shape[0], a.shape[1]
    for k, (v, w) in enumerate(((a, b), (a_got, b_got))):
        out[k * n:k * n + n, :cut] = v[...]
        out[k * n:k * n + n, cut:] = w[...]


def xor_send(v, mask, total):
    return lax.ppermute(v, AXES, [(i, i ^ mask) for i in range(total)])


class Flow:
    def __init__(self, chain, count, total, bits, rest, cut, keep, send, name, head=False):
        self.chain, self.count, self.total, self.rest, self.cut, self.head = chain, count, total, rest, cut, head
        self.core, self.x, self.y, self.z1, self.z0 = bits
        self.rows = keep.shape[1]
        self.name = name
        self.held = [keep, self.to(send, self.core)]

    def to(self, v, mask):
        with jax.named_scope(self.name + str(mask)):
            return xor_send(v, mask, self.total)

    def shapes(self, n):
        return [((n, self.cut, 128), bf), ((n, self.rows - self.cut, 128), bf)]

    def run(self, kernel, outs, args):
        return self.chain(kernel, outs, args, limit=4)

    def add_core(self):
        a, b = self.shapes(8)
        a0, a1, b0, b1 = self.run(add_core_kernel, [a, a, b, b], self.held)
        self.held = [a0, self.to(a1, self.x), b0, self.to(b1, self.y)]

    def add_first(self):
        a, b = self.shapes(4)
        a0, a1, b0, b1 = self.run(add_pair_kernel, [a, a, b, b], self.held)
        self.held = [a0, self.to(a1, self.y), b0, self.to(b1, self.x)]

    def add_second(self):
        parts = self.run(add_merge_kernel, [((2, self.rows, 128), bf)] * 2, self.held)
        self.held = [parts[0], self.to(parts[1], self.z0)]

    def add_z(self):
        parts = self.run(add_split_kernel, [((1, self.rows, 128), bf)] * 2, self.held)
        self.held = [parts[0], self.to(parts[1], self.z1)]

    def add_last(self):
        (own,) = self.run(add_split_kernel, [((1, self.rows, 128), bf)], self.held)
        for m in self.rest:
            own = own + self.to(own, m)
        self.held = [own, self.to(own, self.z1)]

    def join_last(self):
        (v,) = self.run(join_kernel, [((2, self.rows, 128), bf)], self.held)
        self.held = [v, self.to(v, self.z0)]

    def join_z(self):
        if self.head:
            (v,) = self.run(join_kernel, [((4, self.rows, 128), bf)], self.held)
            self.held = [v, self.to(v, self.y)]
        else:
            a, b = self.run(functools.partial(join_split_kernel, self.cut), self.shapes(4), self.held)
            self.held = [a, self.to(a, self.y), b, self.to(b, self.x)]

    def join_first(self):
        if self.head:
            (v,) = self.run(join_kernel, [((8, self.rows, 128), bf)], self.held)
            self.held = [v, self.to(v, self.core)]
        else:
            a, b = self.run(join_pair_kernel, self.shapes(8), self.held)
            self.held = [a, self.to(a, self.x), b, self.to(b, self.y)]

    def join_second(self):
        (v,) = self.run(join_merge_kernel, [((16, self.rows, 128), bf)], self.held)
        self.held = [v, self.to(v, self.core)]


def assemble(refs, scr):
    k = 0
    for a in refs:
        scr[k:k + a.shape[0]] = a[...]
        k += a.shape[0]


def slab(scr, index, at):
    return scr[index, at:at + 48, :].astype(f32)


def vectors(tmp, row, outs):
    for o in outs:
        n = o.shape[0]
        for j in range(0, n, 128):
            o[pl.ds(j, 128)] = tmp[row]
            row += 1


def unpack_columns(count, masks, here, there, w, skip, bias, scr, tmp):
    me = me_of(masks, count)
    assemble((here, there), scr)
    cols, width = w.shape
    for b in range(width // 128):
        w[:, 128 * b:128 * b + 128] = scr[b ^ me].astype(f32)
    for i in range(skip.shape[1] // 128):
        skip[:, 128 * i:128 * i + 128] = scr[(width // 128 + i) ^ me].astype(f32)
    tmp[...] = scr[15 ^ me].astype(f32)
    bias[...] = jnp.concatenate([tmp[i:i + 1, :] for i in range(-(-cols // 128))], axis=1)[0, :cols]


def unpack_ffn(count, masks, here, there, inner, up, down, bias, gain, scr, tmp):
    me_a, me_b = (me_of(m, count) for m in masks)
    assemble((here, there), scr)
    for b in range(32):
        a_at, b_at = b ^ me_a, b ^ me_b
        j, i = b // 8, b % 8
        rows = slice(48 * i, 48 * i + 48)
        for k in range(3):
            cols = slice(TILE * j + 128 * k, TILE * j + 128 * k + 128)
            inner[rows, cols] = slab(scr, a_at, 48 * k)
            up[rows, cols] = slab(scr, a_at, 160) if k == 0 else slab(scr, b_at, 208 + 48 * (k - 1))
            down[48 * b:48 * b + 48, 128 * k:128 * k + 128] = slab(scr, b_at, 304 + 48 * k)
    tmp[...] = scr[me_a, 144:160, :].astype(f32)
    vectors(tmp, 0, (bias, gain))


def unpack_tokens(count, masks, here, there, gq, gk, gv, wo, out, tin, skip, bin_, bout, gain, scr, tmp):
    me_a, me_b = (me_of(m, count) for m in masks)
    assemble((here, there), scr)
    for b in range(32):
        a_at, b_at = b ^ me_a, b ^ me_b
        j, i = b // 8, b % 8
        tmp[16 * b:16 * b + 16, :] = scr[a_at, 144:160, :].astype(f32)
        for k in range(3):
            c = TILE * j + 128 * k
            (gq, gk, gv)[c // 512][48 * i:48 * i + 48, c % 512:c % 512 + 128] = slab(scr, a_at, 48 * k)
            out[48 * b:48 * b + 48, 128 * k:128 * k + 128] = slab(scr, b_at, 160 + 48 * k)
            wo[16 * b:16 * b + 16, 128 * k:128 * k + 128] = scr[b_at, 304 + 16 * k:320 + 16 * k, :].astype(f32)
    for c in range(12):
        tin[:, 128 * c:128 * c + 128] = tmp[32 * c:32 * c + 32, :]
    for i in range(3):
        skip[:, 128 * i:128 * i + 128] = tmp[384 + 32 * i:416 + 32 * i, :]
    vectors(tmp, 480, (bin_, bout, gain))


def per_device(wide, count, signal_samples, present_mask, wi, bi, wfin, wskip, bfin, gain_one, wq, wk, wv, wm,
               gain_two, we, wc, wri, bri, whz, wrs, bro, cotangent):
    series, points = signal_samples.shape
    patch = wi.shape[0] // 2
    rows = series * (points // patch)
    dim, width = wri.shape
    cols = whz.shape[1]
    inner = wq.shape[1]
    total = wide * count
    X, CORE, Y, Z0, Z1 = 1, count, 2 * count, 4 * count, 8 * count
    bits = (CORE, X, Y, Z1, Z0)
    narrow_rest = [1 << i for i in range(1, count.bit_length() - 1)]
    wide_rest = [count << i for i in range(4, wide.bit_length() - 1)]
    masks = [[CORE, X, Y, Z0, Z1], [CORE, Y, X, Z0, Z1]]
    column_masks = [CORE, Y, Z0, Z1]
    chain = Chain()
    vmem = pltpu.VMEM

    whz_t, wrs_t, cot_t = whz.T, wrs.T, cotangent.T
    packed = (width + dim + 128) // 2
    prepared = chain(
        functools.partial(prepare_kernel, count, rows),
        [((cols, rows), bf)] * (count - 1) + [((cols, rows), f32), ((cols, packed), bf), ((cols, dim + 128), bf)],
        [bro], raw=[cot_t, whz_t, wrs_t],
        scratch=[vmem((max(count - 1, 1), cols, rows), f32), vmem((cols, width // 2), bf), vmem((cols, dim), bf),
                 pltpu.SemaphoreType.DMA((count + 2,))], limit=24)
    own_cot, mine, short = prepared[count - 1:]
    cots = [own_cot] + [xor_send(prepared[r - 1], r, total) for r in range(1, count)]
    far = [xor_send(mine, r, total) for r in range(1, count)]

    weights = [wi, wfin, wskip, wq, wk, wv, wm, we, wc, wri, whz_t]
    out = chain(
        functools.partial(tokens_kernel, patch),
        [((rows, 2 * patch), bf), ((rows, width), bf), ((rows, width), bf), ((rows, dim), f32), ((rows, dim), bf),
         ((rows, 3 * inner), bf), ((1, rows), f32), ((1, rows), f32)] + [(w.shape, bf) for w in weights],
        [signal_samples, present_mask, bi, bfin, gain_one], raw=weights,
        scratch=[pltpu.SemaphoreType.DMA((len(weights),))])
    patches, hid1, d1, embed, normed1, qkv, sigma, center = out[:8]
    wi, wfin, wskip, wq, wk, wv, wm, we, wc, wri, whz_t = out[8:]

    probs, mixed = chain(attend_kernel, [((2 * series, 32, 128), f32), ((rows, inner), bf)], [qkv])
    middle, normed2, hid2, d2, states, hidh, dh = chain(
        ffn_kernel,
        [((rows, dim), f32), ((rows, dim), bf), ((rows, width), bf), ((rows, width), bf), ((rows, dim), bf),
         ((rows, width), bf), ((rows, width), bf)],
        [embed, mixed, wm, gain_two, we, wc, wri, bri])

    cut = first_rows(cols)
    groups = max(count // 2, 1)

    def columns():
        out = chain(
            functools.partial(columns_kernel, count, column_masks), [((16, cols, 128), bf)] * (2 * groups),
            [states, hidh, sigma] + cots,
            scratch=[vmem((cols, 128), f32)] + [vmem((32, n, 128), bf) for n in (cut, cols - cut)] * groups, limit=24)
        first = list(out[:2])
        for i in range(1, groups):
            for k in range(2):
                first[k] = first[k] + xor_send(out[2 * i + k], 2 * i, total)
        return Flow(chain, count, total, bits, wide_rest, cut, *first, "columns", head=True)

    def gate():
        out = []
        for v in far:
            (v,) = chain(gate_kernel, [(v.shape, bf)], [v], limit=4)
            out += [v, xor_send(v, CORE, total)]
        return out

    def head():
        out = chain(
            functools.partial(head_kernel, count),
            [((rows, dim), bf), ((rows, width), bf), ((1, width), f32)] + [((cols, width), bf)] * (count - 1)
            + [((cols, dim + 128), bf)] * (count - 1),
            [dh, sigma, wri] + cots + [whz_t] + far_both + [short])
        return out[0], out[1], out[2], [whz_t] + out[3:2 + count], [short] + out[2 + count:]

    def ffn_back():
        gmiddle, keep, send = chain(
            functools.partial(ffn_back_kernel, count, masks), [((rows, dim), bf)] + [((16, 448, 128), bf)] * 2,
            [gstates, states, gpre, sums, hid2, d2, normed2, middle, wc, we, gain_two],
            scratch=[vmem((32, 208, 128), bf), vmem((32, 240, 128), bf), vmem((16, 128), f32)])
        return gmiddle, Flow(chain, count, total, bits, narrow_rest + wide_rest, 208, keep, send, "ffn")

    def attend_back():
        return chain(attend_back_kernel, [((rows, 3 * inner), bf)], [gmiddle, wm, qkv, probs],
                     scratch=[vmem((rows, inner), bf), vmem(probs.shape, f32), vmem(probs.shape, bf)])[0]

    def project_back():
        return chain(
            functools.partial(project_back_kernel, count, masks),
            [((rows, dim), bf), ((1, dim), f32), ((32, 144, 128), bf), ((32, 48, 128), bf)],
            [gqkv, gmiddle, mixed, normed1, embed, wq, wk, wv, gain_one])

    def tokens_back():
        gscaled, keep, send = chain(
            functools.partial(tokens_back_kernel, count, masks, patch),
            [((series, points), f32)] + [((16, 352, 128), bf)] * 2,
            [gembed, hid1, d1, patches, wfin, wskip, wi, gg1, part_a, part_b],
            scratch=[vmem((32, 16, 128), bf), vmem((32, 144, 128), bf), vmem((512, 128), f32)])
        return gscaled, Flow(chain, count, total, bits, narrow_rest + wide_rest, 160, keep, send, "tokens")

    def forecast():
        out = chain(
            functools.partial(forecast_kernel, count, patch),
            [((cols, rows), f32)] + [((cols, rows), bf)] * (count - 1) + [((series, points), f32)],
            [signal_samples, present_mask, gscaled, hidh, states, sigma, center] + mats + shorts + cots)
        return [out[0]] + [xor_send(out[r], r, total) for r in range(1, count)], out[count]

    def place():
        return chain(functools.partial(place_kernel, count), [((cols, count * rows), f32)], preds)[0]

    def finish_columns():
        return chain(functools.partial(unpack_columns, count, column_masks),
                     [((cols, width), f32), ((cols, dim), f32), ((cols,), f32)],
                     one.held, scratch=[vmem((16, cols, 128), bf), vmem((cols, 128), f32)], limit=24)

    def finish_ffn():
        return chain(functools.partial(unpack_ffn, count, masks),
                     [((dim, width), f32)] * 2 + [((width, dim), f32), ((width,), f32), ((dim,), f32)], two.held,
                     scratch=[vmem((32, 448, 128), bf), vmem((16, 128), f32)], limit=24)

    def finish_tokens():
        return chain(
            functools.partial(unpack_tokens, count, masks),
            [((dim, inner), f32)] * 3 + [((inner, dim), f32), ((width, dim), f32), ((2 * patch, width), f32),
                                         ((2 * patch, dim), f32), ((width,), f32), ((dim,), f32), ((dim,), f32)],
            three.held, scratch=[vmem((32, 352, 128), bf), vmem((512, 128), f32)], limit=24)

    one = columns()
    far_both = gate()
    gstates, gpre, sums, mats, shorts = head()
    one.add_core()
    gmiddle, two = ffn_back()
    gqkv = attend_back()
    one.add_first()
    two.add_core()
    gembed, gg1, part_a, part_b = project_back()
    gscaled, three = tokens_back()
    one.add_second()
    preds, g_series = forecast()
    three.add_core()
    two.add_first()
    one.add_z()
    three.add_first()
    two.add_second()
    one.add_last()
    three.add_second()
    one.join_last()
    two.add_z()
    one.join_z()
    three.add_z()
    two.add_last()
    three.add_last()
    one.join_first()
    prediction = place()
    two.join_last()
    three.join_last()
    columns_out = finish_columns()
    two.join_z()
    three.join_z()
    two.join_first()
    three.join_first()
    two.join_second()
    three.join_second()
    ffn_out = finish_ffn()
    tokens_out = finish_tokens()
    g_hw, g_hs, g_hb = columns_out
    g_hiw, g_up, g_down, g_hib, g_g2 = ffn_out
    g_q, g_k, g_v, g_wo, g_to, g_ti, g_ts, g_tib, g_tob, g_g1 = tokens_out
    return (prediction.T, g_series, g_ti, g_tib, g_to, g_ts, g_tob, g_g1, g_q, g_k, g_v, g_wo, g_g2, g_up, g_down,
            g_hiw, g_hib, g_hw.T, g_hs.T, g_hb)


def solution(mesh):
    wide, count = mesh.shape["wide"], mesh.shape["narrow"]
    both = P(("wide", "narrow"), None)
    return jax.shard_map(
        functools.partial(per_device, wide, count),
        mesh=mesh,
        in_specs=(both, both) + (P(),) * 15 + (P(None, "narrow"), P(None, "narrow"), P("narrow"), P("wide", "narrow")),
        out_specs=(P("wide", "narrow"), both) + (P(),) * 15
        + (P(None, "narrow"), P(None, "narrow"), P("narrow")),
        check_vma=False,
    )
```

profile of v0, /device:TPU:0, one launch (start us, length us, event | category | flops | bytes accessed | tf_op | source)
XLA Modules:
  0.0 187.7 jit_solution(12504772476292465286)
XLA Ops:
  3.0 3.0 %collective-permute-start = (bf16[288,512]{1,0:T(8,128)(2,1)S(1)}, bf16[288,512]{1,0:T(8,128)(2,1)S(1)}, u32[]{:S(2)}, u32[]{:S(2)}) collective-permute-start(bf16[288,512]{1,0:T(8,128)(2,1)S(1)} %get-tuple-element.134.refs_16_), channel_id=1, source_target_pairs={{0,1},{1,0},{2,3},{3,2},{4,5},{5,4},{6,7},{7,6},{8,9},{9,8},{10,11... | collective-permute-start | bytes 884744 | tf_op jit(solution)/shard_map/ppermute | solution.py:561
  6.1 5.4 %tokens_kernel.1 = (bf16[512,32]{1,0:T(8,128)(2,1)S(1)}, bf16[512,1536]{1,0:T(8,128)(2,1)S(1)}, bf16[512,1536]{1,0:T(8,128)(2,1)S(1)}, f32[512,384]{1,0:T(8,128)...) custom-call(f32[16,512]{1,0:T(8,128)S(1)} %copy-done.1, ...), custom_call_target="tpu_custom_call" | custom-call | flops 1000 | bytes 1000 | tf_op jit(solution)/shard_map/tokens_kernel/pallas_call | solution.py:48
  12.9 4.5 %ffn_kernel.1 = (f32[512,384]{1,0:T(8,128)S(1)}, bf16[512,384]{1,0:T(8,128)(2,1)S(1)}, bf16[512,1536]{1,0:T(8,128)(2,1)S(1)}, bf16[512,1536]{1,0:T(8,128)(2,1)S(...) custom-call(f32[512,384]{1,0:T(8,128)S(1)} %get-tuple-element.135.refs_0_.refs_4_, ...), custom_call_target="tpu_custom_call" | custom-call | flops 1000 | bytes 1000 | tf_op jit(solution)/shard_map/ffn_kernel/pallas_call | solution.py:48
  19.5 6.1 %collective-permute-done.1.refs_0_ = bf16[288,1024]{1,0:T(8,128)(2,1)S(1)} collective-permute-done((bf16[288,1024]{1,0:T(8,128)(2,1)S(1)}, bf16[288,1024]{1,0:T(8,128)(2,1)S(1)}, u32[]{:S(2)}, u32[]{:S(2)}) %collective-permute-start.1) | collective-permute-done | bytes 589856 | tf_op jit(solution)/shard_map/ppermute | solution.py:561
  27.7 3.8 %head_kernel.1 = (bf16[512,384]{1,0:T(8,128)(2,1)S(1)}, bf16[512,1536]{1,0:T(8,128)(2,1)S(1)}, f32[1,1536]{1,0:T(1,128)S(1)}, bf16[288,1536]{1,0:T(8,128)(2,1)S(1)}, bf16[288,512]{1,0:T(8,128)(2,1)S(1)}) custom-call(bf16[512,1536]{1,0:T(8,128)(2,1)S(1)} %get-tuple-element.144.refs_0_, f32[1,512]{1,0:T(1,128)S(1)} %get-tuple-element.137.refs_1_.refs_2_.refs_5_, ...), custom_call_target="tpu_custom_call" | custom-call | flops 1000 | bytes 1000 | tf_op jit(solution)/shard_map/head_kernel/pallas_call | solution.py:48
  31.8 5.2 %ffn_back_kernel.1 = (bf16[512,384]{1,0:T(8,128)(2,1)S(1)}, bf16[16,448,128]{2,1,0:T(8,128)(2,1)S(1)}, bf16[16,448,128]{2,1,0:T(8,128)(2,1)S(1)}) custom-call(bf16[512,384]{1,0:T(8,128)(2,1)S(1)} %get-tuple-element.153.refs_0_, bf16[512,384]{1,0:T(8,128)(2,1)S(1)} %get-tuple-element.148.refs_0_.refs_1_.refs_4_, ...), custom_call_target="tpu_custom_call" | custom-call | flops 1000 | bytes 1000 | tf_op jit(solution)/shard_map/ffn_back_kernel/pallas_call | solution.py:48
  42.6 3.9 %collective-permute-done.5.refs_1_ = bf16[8,144,128]{2,1,0:T(8,128)(2,1)S(1)} collective-permute-done((bf16[8,144,128]{2,1,0:T(8,128)(2,1)S(1)}, bf16[8,144,128]{2,1,0:T(8,128)(2,1)S(1)}, u32[]{:S(2)}, u32[]{:S(2)}) %collective-permute-start.5) | collective-permute-done | bytes 294944 | tf_op jit(solution)/shard_map/columns1/ppermute | solution.py:561
  50.7 3.8 %tokens_back_kernel.1 = (f32[16,512]{1,0:T(8,128)S(1)}, bf16[16,352,128]{2,1,0:T(8,128)(2,1)S(1)}, bf16[16,352,128]{2,1,0:T(8,128)(2,1)S(1)}) custom-call(bf16[512,384]{1,0:T(8,128)(2,1)S(1)} %get-tuple-element.173.refs_0_, bf16[512,1536]{1,0:T(8,128)(2,1)S(1)} %get-tuple-element.174.refs_1_, bf16[512,1536]{1,0:T(8,128)(2,1)S(1)} %get-tuple-element.175.refs_2_, ...), custom_call_target="tpu_custom_call" | custom-call | flops 1000 | bytes 1000 | tf_op jit(solution)/shard_map/tokens_back_kernel/pallas_call | solution.py:48
  58.7 12.7 %collective-permute-done.7.refs_1_ = bf16[4,144,128]{2,1,0:T(8,128)(2,1)S(1)} collective-permute-done((bf16[4,144,128]{2,1,0:T(8,128)(2,1)S(1)}, bf16[4,144,128]{2,1,0:T(8,128)(2,1)S(1)}, u32[]{:S(2)}, u32[]{:S(2)}) %collective-permute-start.7) | collective-permute-done | bytes 147488 | tf_op jit(solution)/shard_map/columns4/ppermute | solution.py:561
  82.1 4.9 %collective-permute-done.17.refs_1_ = bf16[8,160,128]{2,1,0:T(8,128)(2,1)S(1)} collective-permute-done((bf16[8,160,128]{2,1,0:T(8,128)(2,1)S(1)}, bf16[8,160,128]{2,1,0:T(8,128)(2,1)S(1)}, u32[]{:S(2)}, u32[]{:S(2)}) %collective-permute-start.17) | collective-permute-done | bytes 327712 | tf_op jit(solution)/shard_map/tokens1/ppermute | solution.py:561
  95.0 3.0 %collective-permute-start.19 = (bf16[1,288,128]{2,1,0:T(8,128)(2,1)S(1)}, bf16[1,288,128]{2,1,0:T(8,128)(2,1)S(1)}, u32[]{:S(2)}, u32[]{:S(2)}) collective-permute-start(bf16[1,288,128]{2,1,0:T(8,128)(2,1)S(1)} %add_split_kernel.7.refs_4_.refs_0_), channel_id=1, source_target_pairs={{0,16},{1,17},{2,18},{3,19},{4,20},{5,21},{6,22},{7,23},{8,24},{9,... | collective-permute-start | bytes 221192 | tf_op jit(solution)/shard_map/columns16/ppermute | solution.py:561
  100.7 3.2 %collective-permute-start.22 = (bf16[2,288,128]{2,1,0:T(8,128)(2,1)S(1)}, bf16[2,288,128]{2,1,0:T(8,128)(2,1)S(1)}, u32[]{:S(2)}, u32[]{:S(2)}) collective-permute-start(bf16[2,288,128]{2,1,0:T(8,128)(2,1)S(1)} %join_kernel.5.refs_2_.refs_0_), channel_id=1, source_target_pairs={{0,8},{1,9},{2,10},{3,11},{4,12},{5,13},{6,14},{7,15},{8,0},{9,1},... | collective-permute-start | bytes 442376 | tf_op jit(solution)/shard_map/columns8/ppermute | solution.py:561
  103.9 5.8 %collective-permute-done.22.refs_1_ = bf16[2,288,128]{2,1,0:T(8,128)(2,1)S(1)} collective-permute-done((bf16[2,288,128]{2,1,0:T(8,128)(2,1)S(1)}, bf16[2,288,128]{2,1,0:T(8,128)(2,1)S(1)}, u32[]{:S(2)}, u32[]{:S(2)}) %collective-permute-start.22) | collective-permute-done | bytes 147488 | tf_op jit(solution)/shard_map/columns8/ppermute | solution.py:561
  111.0 3.1 %collective-permute-start.27 = (bf16[1,448,128]{2,1,0:T(8,128)(2,1)S(1)}, bf16[1,448,128]{2,1,0:T(8,128)(2,1)S(1)}, u32[]{:S(2)}, u32[]{:S(2)}) collective-permute-start(bf16[1,448,128]{2,1,0:T(8,128)(2,1)S(1)} %get-tuple-element.221), channel_id=1, source_target_pairs={{0,16},{1,17},{2,18},{3,19},{4,20},{5,21},{6,22},{7,23},{8,24},{9,... | collective-permute-start | bytes 344072 | tf_op jit(solution)/shard_map/ffn16/ppermute | solution.py:561
  114.2 3.5 %collective-permute-done.25.refs_1_ = bf16[2,352,128]{2,1,0:T(8,128)(2,1)S(1)} collective-permute-done((bf16[2,352,128]{2,1,0:T(8,128)(2,1)S(1)}, bf16[2,352,128]{2,1,0:T(8,128)(2,1)S(1)}, u32[]{:S(2)}, u32[]{:S(2)}) %collective-permute-start.25) | collective-permute-done | bytes 180256 | tf_op jit(solution)/shard_map/tokens8/ppermute | solution.py:561
  118.5 5.4 %collective-permute-done.26.refs_1_ = bf16[1,352,128]{2,1,0:T(8,128)(2,1)S(1)} collective-permute-done((bf16[1,352,128]{2,1,0:T(8,128)(2,1)S(1)}, bf16[1,352,128]{2,1,0:T(8,128)(2,1)S(1)}, u32[]{:S(2)}, u32[]{:S(2)}) %collective-permute-start.26) | collective-permute-done | bytes 90144 | tf_op jit(solution)/shard_map/tokens16/ppermute | solution.py:561
  125.8 7.7 %collective-permute-done.9.refs_1_ = bf16[288,512]{1,0:T(8,128)(2,1)S(1)} collective-permute-done((bf16[288,512]{1,0:T(8,128)(2,1)S(1)}, bf16[288,512]{1,0:T(8,128)(2,1)S(1)}, u32[]{:S(2)}, u32[]{:S(2)}) %collective-permute-start.9) | collective-permute-done | bytes 294944 | tf_op jit(solution)/shard_map/ppermute | solution.py:561
  138.5 4.4 %collective-permute-done.28.refs_1_ = bf16[1,352,128]{2,1,0:T(8,128)(2,1)S(1)} collective-permute-done((bf16[1,352,128]{2,1,0:T(8,128)(2,1)S(1)}, bf16[1,352,128]{2,1,0:T(8,128)(2,1)S(1)}, u32[]{:S(2)}, u32[]{:S(2)}) %collective-permute-start.28) | collective-permute-done | bytes 90144 | tf_op jit(solution)/shard_map/tokens16/ppermute | solution.py:561
  147.4 3.3 %collective-permute-start.30 = (bf16[2,352,128]{2,1,0:T(8,128)(2,1)S(1)}, bf16[2,352,128]{2,1,0:T(8,128)(2,1)S(1)}, u32[]{:S(2)}, u32[]{:S(2)}) collective-permute-start(bf16[2,352,128]{2,1,0:T(8,128)(2,1)S(1)} %join_kernel.9.refs_2_.refs_0_), channel_id=1, source_target_pairs={{0,8},{1,9},{2,10},{3,11},{4,12},{5,13},{6,14},{7,15},{8,0},{9,1},... | collective-permute-start | bytes 540680 | tf_op jit(solution)/shard_map/tokens8/ppermute | solution.py:561
  150.7 3.5 %collective-permute-done.30.refs_1_ = bf16[2,352,128]{2,1,0:T(8,128)(2,1)S(1)} collective-permute-done((bf16[2,352,128]{2,1,0:T(8,128)(2,1)S(1)}, bf16[2,352,128]{2,1,0:T(8,128)(2,1)S(1)}, u32[]{:S(2)}, u32[]{:S(2)}) %collective-permute-start.30) | collective-permute-done | bytes 180256 | tf_op jit(solution)/shard_map/tokens8/ppermute | solution.py:561
  158.5 10.7 %collective-permute-done.33.refs_1_ = bf16[4,160,128]{2,1,0:T(8,128)(2,1)S(1)} collective-permute-done((bf16[4,160,128]{2,1,0:T(8,128)(2,1)S(1)}, bf16[4,160,128]{2,1,0:T(8,128)(2,1)S(1)}, u32[]{:S(2)}, u32[]{:S(2)}) %collective-permute-start.33) | collective-permute-done | bytes 163872 | tf_op jit(solution)/shard_map/tokens4/ppermute | solution.py:561
  171.1 9.6 %collective-permute-done.37.refs_1_ = bf16[8,160,128]{2,1,0:T(8,128)(2,1)S(1)} collective-permute-done((bf16[8,160,128]{2,1,0:T(8,128)(2,1)S(1)}, bf16[8,160,128]{2,1,0:T(8,128)(2,1)S(1)}, u32[]{:S(2)}, u32[]{:S(2)}) %collective-permute-start.37) | collective-permute-done | bytes 327712 | tf_op jit(solution)/shard_map/tokens1/ppermute | solution.py:561
  180.9 3.4 %unpack_ffn.1 = (f32[384,1536]{1,0:T(8,128)}, f32[384,1536]{1,0:T(8,128)}, f32[1536,384]{1,0:T(8,128)}, f32[1536]{0:T(1024)}, f32[384]{0:T(512)}) custom-call(bf16[16,448,128]{2,1,0:T(8,128)(2,1)S(1)} %join_merge_kernel.2.refs_4_.refs_0_, bf16[16,448,128]{2,1,0:T(8,128)(2,1)S(1)} %collective-permute-done.42.refs_1_, ...), custom_call_target="tpu_custom_call" | custom-call | flops 1000 | bytes 1000 | tf_op jit(solution)/shard_map/unpack_ffn/pallas_call | solution.py:48
  184.9 2.8 %unpack_tokens.1 = (f32[384,512]{1,0:T(8,128)}, f32[384,512]{1,0:T(8,128)}, f32[384,512]{1,0:T(8,128)}, f32[512,384]{1,0:T(8,128)}, f32[1536,384]{1,0:T(8,128)},...) custom-call(bf16[16,352,128]{2,1,0:T(8,128)(2,1)S(1)} %join_merge_kernel.3.refs_2_.refs_, ...), custom_call_target="tpu_custom_call" | custom-call | flops 1000 | bytes 1000 | tf_op jit(solution)/shard_map/unpack_tokens/pallas_call | solution.py:48
  (128 shorter events, 64.0 us)
Async XLA Ops:
  3.0 14.5 %collective-permute-start = (bf16[288,512]{1,0:T(8,128)(2,1)S(1)}, bf16[288,512]{1,0:T(8,128)(2,1)S(1)}, u32[]{:S(2)}, u32[]{:S(2)}) collective-permute-start(bf16[288,512]{1,0:T(8,128)(2,1)S(1)} %get-tuple-element.134.refs_16_), channel_id=1, source_target_pairs={{0,1},{1,0},{2,3},{3,2},{4,5},{5,4},{6,7},{7,6},{8,9},{9,8},{10,11... | collective-permute-start | bytes 884744 | tf_op jit(solution)/shard_map/ppermute | solution.py:561
  6.0 19.6 %collective-permute-start.1 = (bf16[288,1024]{1,0:T(8,128)(2,1)S(1)}, bf16[288,1024]{1,0:T(8,128)(2,1)S(1)}, u32[]{:S(2)}, u32[]{:S(2)}) collective-permute-start(bf16[288,1024]{1,0:T(8,128)(2,1)S(1)} %get-tuple-element.147), channel_id=1, source_target_pairs={{0,1},{1,0},{2,3},{3,2},{4,5},{5,4},{6,7},{7,6},{8,9},{9,8},{10,11... | collective-permute-start | bytes 1769480 | tf_op jit(solution)/shard_map/ppermute | solution.py:561
  19.4 12.1 %collective-permute-start.3 = (bf16[16,288,128]{2,1,0:T(8,128)(2,1)S(1)}, bf16[16,288,128]{2,1,0:T(8,128)(2,1)S(1)}, u32[]{:S(2)}, u32[]{:S(2)}) collective-permute-start(bf16[16,288,128]{2,1,0:T(8,128)(2,1)S(1)} %get-tuple-element.159), channel_id=1, source_target_pairs={{0,2},{1,3},{2,0},{3,1},{4,6},{5,7},{6,4},{7,5},{8,10},{9,11},{10,... | collective-permute-start | bytes 3538952 | tf_op jit(solution)/shard_map/columns2/ppermute | solution.py:561
  37.0 11.1 %collective-permute-start.4 = (bf16[16,448,128]{2,1,0:T(8,128)(2,1)S(1)}, bf16[16,448,128]{2,1,0:T(8,128)(2,1)S(1)}, u32[]{:S(2)}, u32[]{:S(2)}) collective-permute-start(bf16[16,448,128]{2,1,0:T(8,128)(2,1)S(1)} %get-tuple-element.167), channel_id=1, source_target_pairs={{0,2},{1,3},{2,0},{3,1},{4,6},{5,7},{6,4},{7,5},{8,10},{9,11},{10,... | collective-permute-start | bytes 5505032 | tf_op jit(solution)/shard_map/ffn2/ppermute | solution.py:561
  54.5 19.2 %collective-permute-start.13 = (bf16[16,352,128]{2,1,0:T(8,128)(2,1)S(1)}, bf16[16,352,128]{2,1,0:T(8,128)(2,1)S(1)}, u32[]{:S(2)}, u32[]{:S(2)}) collective-permute-start(bf16[16,352,128]{2,1,0:T(8,128)(2,1)S(1)} %get-tuple-element.198), channel_id=1, source_target_pairs={{0,2},{1,3},{2,0},{3,1},{4,6},{5,7},{6,4},{7,5},{8,10},{9,11},{10,... | collective-permute-start | bytes 4325384 | tf_op jit(solution)/shard_map/tokens2/ppermute | solution.py:561
  54.6 23.9 %collective-permute-start.12 = (bf16[8,240,128]{2,1,0:T(8,128)(2,1)S(1)}, bf16[8,240,128]{2,1,0:T(8,128)(2,1)S(1)}, u32[]{:S(2)}, u32[]{:S(2)}) collective-permute-start(bf16[8,240,128]{2,1,0:T(8,128)(2,1)S(1)} %get-tuple-element.196), channel_id=1, source_target_pairs={{0,4},{1,5},{2,6},{3,7},{4,0},{5,1},{6,2},{7,3},{8,12},{9,13},{10,... | collective-permute-start | bytes 1474568 | tf_op jit(solution)/shard_map/ffn4/ppermute | solution.py:561
  56.2 22.3 %collective-permute-start.11 = (bf16[8,208,128]{2,1,0:T(8,128)(2,1)S(1)}, bf16[8,208,128]{2,1,0:T(8,128)(2,1)S(1)}, u32[]{:S(2)}, u32[]{:S(2)}) collective-permute-start(bf16[8,208,128]{2,1,0:T(8,128)(2,1)S(1)} %get-tuple-element.194), channel_id=1, source_target_pairs={{0,1},{1,0},{2,3},{3,2},{4,5},{5,4},{6,7},{7,6},{8,9},{9,8},{10,11... | collective-permute-start | bytes 1277960 | tf_op jit(solution)/shard_map/ffn1/ppermute | solution.py:561
  56.7 14.7 %collective-permute-start.7 = (bf16[4,144,128]{2,1,0:T(8,128)(2,1)S(1)}, bf16[4,144,128]{2,1,0:T(8,128)(2,1)S(1)}, u32[]{:S(2)}, u32[]{:S(2)}) collective-permute-start(bf16[4,144,128]{2,1,0:T(8,128)(2,1)S(1)} %get-tuple-element.187), channel_id=1, source_target_pairs={{0,4},{1,5},{2,6},{3,7},{4,0},{5,1},{6,2},{7,3},{8,12},{9,13},{10,... | collective-permute-start | bytes 442376 | tf_op jit(solution)/shard_map/columns4/ppermute | solution.py:561
  57.0 14.4 %collective-permute-start.8 = (bf16[4,144,128]{2,1,0:T(8,128)(2,1)S(1)}, bf16[4,144,128]{2,1,0:T(8,128)(2,1)S(1)}, u32[]{:S(2)}, u32[]{:S(2)}) collective-permute-start(bf16[4,144,128]{2,1,0:T(8,128)(2,1)S(1)} %get-tuple-element.189), channel_id=1, source_target_pairs={{0,1},{1,0},{2,3},{3,2},{4,5},{5,4},{6,7},{7,6},{8,9},{9,8},{10,11... | collective-permute-start | bytes 442376 | tf_op jit(solution)/shard_map/columns1/ppermute | solution.py:561
  74.8 12.2 %collective-permute-start.18 = (bf16[8,192,128]{2,1,0:T(8,128)(2,1)S(1)}, bf16[8,192,128]{2,1,0:T(8,128)(2,1)S(1)}, u32[]{:S(2)}, u32[]{:S(2)}) collective-permute-start(bf16[8,192,128]{2,1,0:T(8,128)(2,1)S(1)} %get-tuple-element.209), channel_id=1, source_target_pairs={{0,4},{1,5},{2,6},{3,7},{4,0},{5,1},{6,2},{7,3},{8,12},{9,13},{10,... | collective-permute-start | bytes 1179656 | tf_op jit(solution)/shard_map/tokens4/ppermute | solution.py:561
  76.4 10.6 %collective-permute-start.17 = (bf16[8,160,128]{2,1,0:T(8,128)(2,1)S(1)}, bf16[8,160,128]{2,1,0:T(8,128)(2,1)S(1)}, u32[]{:S(2)}, u32[]{:S(2)}) collective-permute-start(bf16[8,160,128]{2,1,0:T(8,128)(2,1)S(1)} %get-tuple-element.207), channel_id=1, source_target_pairs={{0,1},{1,0},{2,3},{3,2},{4,5},{5,4},{6,7},{7,6},{8,9},{9,8},{10,11... | collective-permute-start | bytes 983048 | tf_op jit(solution)/shard_map/tokens1/ppermute | solution.py:561
  78.7 13.6 %collective-permute-start.16 = (bf16[4,240,128]{2,1,0:T(8,128)(2,1)S(1)}, bf16[4,240,128]{2,1,0:T(8,128)(2,1)S(1)}, u32[]{:S(2)}, u32[]{:S(2)}) collective-permute-start(bf16[4,240,128]{2,1,0:T(8,128)(2,1)S(1)} %get-tuple-element.206), channel_id=1, source_target_pairs={{0,1},{1,0},{2,3},{3,2},{4,5},{5,4},{6,7},{7,6},{8,9},{9,8},{10,11... | collective-permute-start | bytes 737288 | tf_op jit(solution)/shard_map/ffn1/ppermute | solution.py:561
  80.3 11.5 %collective-permute-start.15 = (bf16[4,208,128]{2,1,0:T(8,128)(2,1)S(1)}, bf16[4,208,128]{2,1,0:T(8,128)(2,1)S(1)}, u32[]{:S(2)}, u32[]{:S(2)}) collective-permute-start(bf16[4,208,128]{2,1,0:T(8,128)(2,1)S(1)} %get-tuple-element.204), channel_id=1, source_target_pairs={{0,4},{1,5},{2,6},{3,7},{4,0},{5,1},{6,2},{7,3},{8,12},{9,13},{10,... | collective-permute-start | bytes 638984 | tf_op jit(solution)/shard_map/ffn4/ppermute | solution.py:561
  87.2 10.9 %collective-permute-start.21 = (bf16[4,192,128]{2,1,0:T(8,128)(2,1)S(1)}, bf16[4,192,128]{2,1,0:T(8,128)(2,1)S(1)}, u32[]{:S(2)}, u32[]{:S(2)}) collective-permute-start(bf16[4,192,128]{2,1,0:T(8,128)(2,1)S(1)} %get-tuple-element.214), channel_id=1, source_target_pairs={{0,1},{1,0},{2,3},{3,2},{4,5},{5,4},{6,7},{7,6},{8,9},{9,8},{10,11... | collective-permute-start | bytes 589832 | tf_op jit(solution)/shard_map/tokens1/ppermute | solution.py:561
  87.8 10.3 %collective-permute-start.20 = (bf16[4,160,128]{2,1,0:T(8,128)(2,1)S(1)}, bf16[4,160,128]{2,1,0:T(8,128)(2,1)S(1)}, u32[]{:S(2)}, u32[]{:S(2)}) collective-permute-start(bf16[4,160,128]{2,1,0:T(8,128)(2,1)S(1)} %get-tuple-element.212), channel_id=1, source_target_pairs={{0,4},{1,5},{2,6},{3,7},{4,0},{5,1},{6,2},{7,3},{8,12},{9,13},{10,... | collective-permute-start | bytes 491528 | tf_op jit(solution)/shard_map/tokens4/ppermute | solution.py:561
  92.4 11.5 %collective-permute-start.23 = (bf16[2,448,128]{2,1,0:T(8,128)(2,1)S(1)}, bf16[2,448,128]{2,1,0:T(8,128)(2,1)S(1)}, u32[]{:S(2)}, u32[]{:S(2)}) collective-permute-start(bf16[2,448,128]{2,1,0:T(8,128)(2,1)S(1)} %get-tuple-element.216), channel_id=1, source_target_pairs={{0,8},{1,9},{2,10},{3,11},{4,12},{5,13},{6,14},{7,15},{8,0},{9,1},... | collective-permute-start | bytes 688136 | tf_op jit(solution)/shard_map/ffn8/ppermute | solution.py:561
  109.7 14.2 %collective-permute-start.24 = (bf16[4,288,128]{2,1,0:T(8,128)(2,1)S(1)}, bf16[4,288,128]{2,1,0:T(8,128)(2,1)S(1)}, u32[]{:S(2)}, u32[]{:S(2)}) collective-permute-start(bf16[4,288,128]{2,1,0:T(8,128)(2,1)S(1)} %join_kernel.6.refs_2_.refs_0_), channel_id=1, source_target_pairs={{0,4},{1,5},{2,6},{3,7},{4,0},{5,1},{6,2},{7,3},{8,12},{9,13},{10,... | collective-permute-start | bytes 884744 | tf_op jit(solution)/shard_map/columns4/ppermute | solution.py:561
  124.0 18.9 %collective-permute-start.32 = (bf16[8,288,128]{2,1,0:T(8,128)(2,1)S(1)}, bf16[8,288,128]{2,1,0:T(8,128)(2,1)S(1)}, u32[]{:S(2)}, u32[]{:S(2)}) collective-permute-start(bf16[8,288,128]{2,1,0:T(8,128)(2,1)S(1)} %join_kernel.7.refs_2_.refs_0_), channel_id=1, source_target_pairs={{0,2},{1,3},{2,0},{3,1},{4,6},{5,7},{6,4},{7,5},{8,10},{9,11},{10,... | collective-permute-start | bytes 1769480 | tf_op jit(solution)/shard_map/columns2/ppermute | solution.py:561
  154.3 16.0 %collective-permute-start.40 = (bf16[8,240,128]{2,1,0:T(8,128)(2,1)S(1)}, bf16[8,240,128]{2,1,0:T(8,128)(2,1)S(1)}, u32[]{:S(2)}, u32[]{:S(2)}) collective-permute-start(bf16[8,240,128]{2,1,0:T(8,128)(2,1)S(1)} %get-tuple-element.230.refs_2_), channel_id=1, source_target_pairs={{0,4},{1,5},{2,6},{3,7},{4,0},{5,1},{6,2},{7,3},{8,12},{9,13},{10,... | collective-permute-start | bytes 1474568 | tf_op jit(solution)/shard_map/ffn4/ppermute | solution.py:561
  155.5 14.9 %collective-permute-start.39 = (bf16[8,208,128]{2,1,0:T(8,128)(2,1)S(1)}, bf16[8,208,128]{2,1,0:T(8,128)(2,1)S(1)}, u32[]{:S(2)}, u32[]{:S(2)}) collective-permute-start(bf16[8,208,128]{2,1,0:T(8,128)(2,1)S(1)} %get-tuple-element.227.refs_4_.refs_0_), channel_id=1, source_target_pairs={{0,1},{1,0},{2,3},{3,2},{4,5},{5,4},{6,7},{7,6},{8,9},{9,8},{10,11... | collective-permute-start | bytes 1277960 | tf_op jit(solution)/shard_map/ffn1/ppermute | solution.py:561
  155.9 13.3 %collective-permute-start.34 = (bf16[4,192,128]{2,1,0:T(8,128)(2,1)S(1)}, bf16[4,192,128]{2,1,0:T(8,128)(2,1)S(1)}, u32[]{:S(2)}, u32[]{:S(2)}) collective-permute-start(bf16[4,192,128]{2,1,0:T(8,128)(2,1)S(1)} %get-tuple-element.225.refs_2_), channel_id=1, source_target_pairs={{0,1},{1,0},{2,3},{3,2},{4,5},{5,4},{6,7},{7,6},{8,9},{9,8},{10,11... | collective-permute-start | bytes 589832 | tf_op jit(solution)/shard_map/tokens1/ppermute | solution.py:561
  157.5 11.7 %collective-permute-start.33 = (bf16[4,160,128]{2,1,0:T(8,128)(2,1)S(1)}, bf16[4,160,128]{2,1,0:T(8,128)(2,1)S(1)}, u32[]{:S(2)}, u32[]{:S(2)}) collective-permute-start(bf16[4,160,128]{2,1,0:T(8,128)(2,1)S(1)} %get-tuple-element.224.refs_4_.refs_0_), channel_id=1, source_target_pairs={{0,4},{1,5},{2,6},{3,7},{4,0},{5,1},{6,2},{7,3},{8,12},{9,13},{10,... | collective-permute-start | bytes 491528 | tf_op jit(solution)/shard_map/tokens4/ppermute | solution.py:561
  169.2 11.5 %collective-permute-start.38 = (bf16[8,192,128]{2,1,0:T(8,128)(2,1)S(1)}, bf16[8,192,128]{2,1,0:T(8,128)(2,1)S(1)}, u32[]{:S(2)}, u32[]{:S(2)}) collective-permute-start(bf16[8,192,128]{2,1,0:T(8,128)(2,1)S(1)} %get-tuple-element.229.refs_2_), channel_id=1, source_target_pairs={{0,4},{1,5},{2,6},{3,7},{4,0},{5,1},{6,2},{7,3},{8,12},{9,13},{10,... | collective-permute-start | bytes 1179656 | tf_op jit(solution)/shard_map/tokens4/ppermute | solution.py:561
  170.5 10.4 %collective-permute-start.42 = (bf16[16,448,128]{2,1,0:T(8,128)(2,1)S(1)}, bf16[16,448,128]{2,1,0:T(8,128)(2,1)S(1)}, u32[]{:S(2)}, u32[]{:S(2)}) collective-permute-start(bf16[16,448,128]{2,1,0:T(8,128)(2,1)S(1)} %join_merge_kernel.2.refs_4_.refs_0_), channel_id=1, source_target_pairs={{0,2},{1,3},{2,0},{3,1},{4,6},{5,7},{6,4},{7,5},{8,10},{9,11},{10,... | collective-permute-start | bytes 5505032 | tf_op jit(solution)/shard_map/ffn2/ppermute | solution.py:561
  (31 other events, 171.2 us)
where the time goes:
time: 188 us
  waiting for transfers between devices  87.7 us (47%)
  starting transfers between devices  49.5 us (26%)
  Pallas kernels  45.4 us (24%)
  local copies, waits for them, and re-layouts  4.13 us (2%)
    ppermute x43, waiting for transfers between devices, xor_send(): return lax.ppermute(v, AXES, [(i, i ^ mask) for i in range(total)])  87.7 us
    ppermute x43, starting transfers between devices, xor_send(): return lax.ppermute(v, AXES, [(i, i ^ mask) for i in range(total)])  49.5 us
    pallas_call x42, Pallas kernels, __call__(): pl.pallas_call(body, name=name, out_shape=[jax.ShapeDtypeStruct(s, d) for...  45.4 us
    unnamed x24, local copies, waits for them, and re-layouts  4.13 us
  transfers between devices with their start and end apart: 43, of which 19 were waited for; matrix products, arithmetic and copies ran while one was open for 0% of the time, Pallas kernels for 15%

commit v1 on v0

--- a/solution.py
+++ b/solution.py
@@ -16,6 +16,7 @@
 TILE = 384
 AXES = ("wide", "narrow")
 MIB = 1 << 20
+COSTS = {25: 10000000000, 31: 20000000000, 20: 6000000000, 12: 30000000000, 19: 30000000000, 35: 30000000000, 27: 30000000000, 5: 10000000000, 16: 3000000000, 21: 6000000000, 28: 3000000000, 23: 30000000000, 29: 15000000000}
 
 
 def dot(a, b):
@@ -33,6 +34,7 @@
 class Chain:
     def __init__(self):
         self.last = None
+        self.calls = 0
 
     def __call__(self, kernel, outs, args, scratch=(), limit=16, raw=()):
         vmem = pl.BlockSpec(memory_space=pltpu.VMEM)
@@ -40,6 +42,8 @@
         args, raw = list(args), [pltpu.with_memory_space_constraint(v, pltpu.HBM) for v in raw]
         deps = [] if self.last is None or any(a is self.last for a in args) else [self.last]
         n, d = len(args) + len(raw), len(deps)
+        cost = COSTS.get(self.calls, 1000)
+        self.calls += 1
 
         def body(*refs):
             kernel(*refs[:n], *refs[n + d:])
@@ -52,7 +56,7 @@
             in_specs=[vmem] * len(args) + [pl.BlockSpec(memory_space=pltpu.HBM)] * len(raw) + [hbm] * d,
             out_specs=[vmem] * len(outs),
             scratch_shapes=list(scratch),
-            cost_estimate=pl.CostEstimate(flops=1000, bytes_accessed=1000, transcendentals=0),
+            cost_estimate=pl.CostEstimate(flops=cost, bytes_accessed=1000, transcendentals=0),
             compiler_params=pltpu.CompilerParams(vmem_limit_bytes=limit * MIB),
         )(*args, *raw, *deps))
         self.last = min(res, key=lambda r: r.size)
@@ -252,24 +256,55 @@
         dh[:, t] = d.astype(bf)
 
 
-def put_slabs(scr, me, tile, value, offset, slabs):
-    for i in range(8):
-        for n, k in enumerate(slabs):
-            scr[(8 * tile + i) ^ me, offset + 48 * n:offset + 48 * n + 48, :] = (
-                value[48 * i:48 * i + 48, 128 * k:128 * k + 128])
-
-
-def ship(parts, keep, send):
+HEAD_ORDER = "pqxy"
+FFN_PARTS = [
+    ("xypq", [("down", 0), ("down", 1), ("down", 2), ("up", 0), ("up", 1)]),
+    ("yqxp", [("inner", 0), ("inner", 1), ("inner", 2), ("up", 2), ("vector", 0)]),
+]
+TOKEN_PARTS = [
+    ("xypq", [("final", 0), ("final", 1), ("final", 2), ("small", 0)]),
+    ("yxpq", [("attention", 0), ("attention", 1), ("attention", 2), ("merge", 0), ("merge", 1), ("merge", 2)]),
+]
+SLAB_ROWS = {"merge": 16, "vector": 16, "small": 16}
+
+
+def part_rows(items):
+    return sum(SLAB_ROWS.get(name, 48) for name, _ in items)
+
+
+def layout(parts):
+    out = {}
+    for p, (_, items) in enumerate(parts):
+        at = 0
+        for item in items:
+            out[item] = p, at
+            at += SLAB_ROWS.get(item[0], 48)
+    return out
+
+
+def sizes(parts):
+    return [(part_rows(items), order) for order, items in parts]
+
+
+def put_matrix(scrs, mes, where, name, tile, value):
+    value = value.astype(bf)
+    for k in range(3):
+        p, at = where[name, k]
+        for i in range(8):
+            scrs[p][(8 * tile + i) ^ mes[p], at:at + 48, :] = value[48 * i:48 * i + 48, 128 * k:128 * k + 128]
+
+
+def ship(sources, keep, send):
     at = 0
-    for p in parts:
-        n, rows = p.shape[0] // 2, p.shape[1]
-        keep[:, at:at + rows] = p[:n]
-        send[:, at:at + rows] = p[n:]
+    for v, first, rows in sources:
+        n = v.shape[0] // 2
+        keep[:, at:at + rows] = v[:n, first:first + rows]
+        send[:, at:at + rows] = v[n:, first:first + rows]
         at += rows
 
 
-def first_rows(cols):
-    return 16 * ((cols + 31) // 32)
+def index_bits(index, count):
+    return [(index // (1 << (count - 1 - k))) % 2 for k in range(count)]
 
 
 def rows_of(tmp, row, v):
@@ -288,16 +323,16 @@
     st = states[...]
     width = hidh.shape[1]
     cols = tmp.shape[0]
-    cut = first_rows(cols)
     for r in range(count):
         turned = (cots[r][...].astype(f32) * sigma[...]).astype(bf)
-        scr_a, scr_b = scrs[2 * (r // 2):2 * (r // 2) + 2]
+        scr = scrs[r // 2]
 
         def put(c, v):
-            rel = c ^ me
-            core, y, z = rel // 8, (rel // 4) % 2, rel % 4
-            scr_a[core * 16 + (r % 2) * 8 + y * 4 + z] = v[:cut]
-            scr_b[core * 16 + y * 8 + (r % 2) * 4 + z] = v[cut:]
+            core, *others = index_bits(c ^ me, 4)
+            at = core
+            for axis in HEAD_ORDER:
+                at = at * 2 + (r % 2 if axis == "x" else others.pop(0))
+            scr[at] = v
 
         for j in range(0, width, TILE):
             v = dot(turned, hidh[:, j:j + TILE]).astype(bf)
@@ -313,7 +348,7 @@
             tmp[row:row + 1, 0:n] = bias[0:1, j:j + n]
         put(15, tmp[...].astype(bf))
     for i in range(groups):
-        ship(scrs[2 * i:2 * i + 2], *outs[2 * i:2 * i + 2])
+        ship([(scrs[i], 0, cols)], *outs[2 * i:2 * i + 2])
 
 
 def head_kernel(count, *refs):
@@ -351,8 +386,10 @@
 
 
 def ffn_back_kernel(count, masks, gstates, states, gpre, sums, hid, dhid, normed, middle, wc, we, gain,
-                    gmiddle, keep, send, scr_a, scr_b, tmp):
-    me_a, me_b = (me_of(m, count) for m in masks)
+                    gmiddle, keep, send, *scrs):
+    *scrs, tmp = scrs
+    mes = [me_of(m, count) for m in masks]
+    where = layout(FFN_PARTS)
     g = gstates[...]
     nt = normed[...].T
     acc = None
@@ -361,21 +398,20 @@
         gp = (dot_nt(g, wc[t, :]) * dhid[:, t].astype(f32)).astype(bf)
         part = dot_nt(gp, we[:, t])
         acc = part if acc is None else acc + part
-        up = dot(nt, gp).astype(bf)
-        put_slabs(scr_a, me_a, j, up, 160, (0,))
-        put_slabs(scr_b, me_b, j, up, 0, (1, 2))
-        put_slabs(scr_b, me_b, j, dot_tn(hid[:, t], g).astype(bf), 96, (0, 1, 2))
+        put_matrix(scrs, mes, where, "up", j, dot(nt, gp))
+        put_matrix(scrs, mes, where, "down", j, dot_tn(hid[:, t], g))
     back, gg = norm_back(acc, middle[...], gain[...][None, :])
     gmiddle[...] = (g.astype(f32) + back).astype(bf)
     st = states[...].T
     for j in range(4):
-        put_slabs(scr_a, me_a, j, dot(st, gpre[:, TILE * j:TILE * j + TILE]).astype(bf), 0, (0, 1, 2))
-    scr_a[:, 144:160, :] = jnp.zeros((32, 16, 128), bf)
+        put_matrix(scrs, mes, where, "inner", j, dot(st, gpre[:, TILE * j:TILE * j + TILE]))
+    p, at = where["vector", 0]
+    scrs[p][:, at:at + 16, :] = jnp.zeros((32, 16, 128), bf)
     tmp[...] = jnp.zeros_like(tmp)
     row = rows_of(tmp, 0, sums[...])
     rows_of(tmp, row, gg)
-    scr_a[me_a, 144:160, :] = tmp[...].astype(bf)
-    ship((scr_a, scr_b), keep, send)
+    scrs[p][mes[p], at:at + 16, :] = tmp[...].astype(bf)
+    ship([(v, 0, v.shape[1]) for v in scrs], keep, send)
 
 
 def attend_back_kernel(gmiddle, wm, qkv, probs, gqkv, gmix, gprobs, low):
@@ -398,8 +434,10 @@
         gqkv[s, inner + c:inner + c + 256] = (dot(ds, q) * SCALE).astype(bf)
 
 
-def project_back_kernel(count, masks, gqkv, gmiddle, mixed, normed, embed, wq, wk, wv, gain, gembed, ggain, part_a, part_b):
-    me_a, me_b = (me_of(m, count) for m in masks)
+def project_back_kernel(count, masks, gqkv, gmiddle, mixed, normed, embed, wq, wk, wv, gain, gembed, ggain,
+                        *scrs):
+    mes = [me_of(m, count) for m in masks]
+    where = layout(TOKEN_PARTS)
     inner = wq.shape[1]
     acc = dot_nt(gqkv[:, :inner], wq[...])
     acc = acc + dot_nt(gqkv[:, inner:2 * inner], wk[...])
@@ -410,16 +448,19 @@
     gembed[...] = (gm.astype(f32) + back).astype(bf)
     nt = normed[...].T
     for j in range(4):
-        put_slabs(part_a, me_a, j, dot(nt, gqkv[:, TILE * j:TILE * j + TILE]).astype(bf), 0, (0, 1, 2))
+        put_matrix(scrs, mes, where, "attention", j, dot(nt, gqkv[:, TILE * j:TILE * j + TILE]))
     v = dot_tn(mixed[...], gm).astype(bf)
-    for i in range(32):
-        for k in range(3):
-            part_b[i ^ me_b, 16 * k:16 * k + 16, :] = v[16 * i:16 * i + 16, 128 * k:128 * k + 128]
-
-
-def tokens_back_kernel(count, masks, patch, gembed, hid, dhid, patches, wfin, wskip, wi, gain_one, part_a, part_b,
-                       gscaled, keep, send, scr_a, scr_b, tmp):
-    me_a, me_b = (me_of(m, count) for m in masks)
+    for k in range(3):
+        p, at = where["merge", k]
+        for i in range(32):
+            scrs[p][i ^ mes[p], at:at + 16, :] = v[16 * i:16 * i + 16, 128 * k:128 * k + 128]
+
+
+def tokens_back_kernel(count, masks, patch, gembed, hid, dhid, patches, wfin, wskip, wi, gain_one, *refs):
+    n = len(masks)
+    earlier, (gscaled, keep, send), scrs, tmp = refs[:n], refs[n:n + 3], refs[n + 3:2 * n + 3], refs[-1]
+    mes = [me_of(m, count) for m in masks]
+    where = layout(TOKEN_PARTS)
     g = gembed[...]
     p = patches[...]
     pt = p.T
@@ -435,15 +476,17 @@
             c = 3 * j + i
             tmp[32 * c:32 * c + 32, :] = v[:, 128 * i:128 * i + 128]
         row = rows_of(tmp, row, jnp.sum(gp.astype(f32), axis=0, keepdims=True))
-        put_slabs(scr_b, me_b, j, dot_tn(hid[:, t], g).astype(bf), 0, (0, 1, 2))
+        put_matrix(scrs, mes, where, "final", j, dot_tn(hid[:, t], g))
     v = dot(pt, g)
     for i in range(3):
         tmp[384 + 32 * i:416 + 32 * i, :] = v[:, 128 * i:128 * i + 128]
     row = rows_of(tmp, row, jnp.sum(g.astype(f32), axis=0, keepdims=True))
     rows_of(tmp, row, gain_one[...])
+    p, at = where["small", 0]
     for b in range(32):
-        scr_a[b ^ me_a] = tmp[16 * b:16 * b + 16].astype(bf)
-    ship((part_a, scr_a, scr_b, part_b), keep, send)
+        scrs[p][b ^ mes[p], at:at + 16, :] = tmp[16 * b:16 * b + 16].astype(bf)
+    ship([((earlier if item[0] in ("attention", "merge") else scrs)[where[item][0]], where[item][1],
+           SLAB_ROWS.get(item[0], 48)) for _, items in TOKEN_PARTS for item in items], keep, send)
     series, points = gscaled.shape
     tokens = points // patch
     rows = series * tokens
@@ -495,137 +538,107 @@
         out[:, pl.ds(pl.multiple_of((narrow ^ r) * rows, 128), rows)] = preds[r][...].astype(f32)
 
 
-def added(a, b):
-    return (a.astype(f32) + b.astype(f32)).astype(bf)
-
-
-def add_core_kernel(keep, got, a0, a1, b0, b1):
-    cut = a0.shape[1]
-    n = keep.shape[0] // 2
-    for k in range(2 * n):
-        v = added(keep[k], got[k])
-        (a0, a1)[k // n][k % n] = v[:cut]
-        (b0, b1)[k // n][k % n] = v[cut:]
-
-
-def add_pair_kernel(a, a_got, b, b_got, a0, a1, b0, b1):
-    n = a.shape[0] // 2
-    for k in range(2 * n):
-        (a0, a1)[k // n][k % n] = added(a[k], a_got[k])
-        (b0, b1)[k // n][k % n] = added(b[k], b_got[k])
-
-
-def add_merge_kernel(a, a_got, b, b_got, *outs):
-    n, cut = outs[0].shape[0], a.shape[1]
-    for i, o in enumerate(outs):
-        for k in range(n):
-            o[k, :cut] = added(a[i * n + k], a_got[i * n + k])
-            o[k, cut:] = added(b[i * n + k], b_got[i * n + k])
-
-
-def add_split_kernel(v, got, *outs):
-    n = outs[0].shape[0]
-    for i, o in enumerate(outs):
-        o[...] = added(v[i * n:i * n + n], got[i * n:i * n + n])
-
-
-def join_split_kernel(cut, here, got, a, b):
-    n = here.shape[0]
-    for k, v in enumerate((here, got)):
-        a[k * n:k * n + n] = v[:, :cut]
-        b[k * n:k * n + n] = v[:, cut:]
-
-
-def join_kernel(*refs):
-    ins, out = refs[:-1], refs[-1]
-    n = ins[0].shape[0]
-    for k, v in enumerate(ins):
-        out[k * n:k * n + n] = v[...]
-
-
-def join_pair_kernel(a, a_got, b, b_got, a_out, b_out):
-    n = a.shape[0]
-    for k, (v, w) in enumerate(((a, b), (a_got, b_got))):
-        a_out[k * n:k * n + n] = v[...]
-        b_out[k * n:k * n + n] = w[...]
-
-
-def join_merge_kernel(a, a_got, b, b_got, out):
-    n, cut = a.shape[0], a.shape[1]
-    for k, (v, w) in enumerate(((a, b), (a_got, b_got))):
-        out[k * n:k * n + n, :cut] = v[...]
-        out[k * n:k * n + n, cut:] = w[...]
-
-
 def xor_send(v, mask, total):
     return lax.ppermute(v, AXES, [(i, i ^ mask) for i in range(total)])
 
 
+def grouped(parts, level):
+    groups = {}
+    for p, (_, order) in enumerate(parts):
+        groups.setdefault(order[level:], []).append(p)
+    return list(groups.values())
+
+
+def places(parts, groups):
+    out = {}
+    for g, members in enumerate(groups):
+        at = 0
+        for p in members:
+            out[p] = g, at
+            at += parts[p][0]
+    return out
+
+
+def add_kernel(parts, before, after, split, *refs):
+    n_in = 2 * (max(g for g, _ in before.values()) + 1)
+    ins, outs = refs[:n_in], refs[n_in:]
+    n = ins[0].shape[0]
+    half = n // split
+    for p, (rows, _) in enumerate(parts):
+        (g, a), (o, b) = before[p], after[p]
+        for k in range(n):
+            v = ins[2 * g][k, a:a + rows].astype(f32) + ins[2 * g + 1][k, a:a + rows].astype(f32)
+            outs[split * o + k // half][k % half, b:b + rows] = v.astype(bf)
+
+
+def join_kernel(parts, before, after, *refs):
+    n_in = 2 * (max(g for g, _ in before.values()) + 1)
+    ins, outs = refs[:n_in], refs[n_in:]
+    n = ins[0].shape[0]
+    for p, (rows, _) in enumerate(parts):
+        (g, a), (o, b) = before[p], after[p]
+        for k in range(2):
+            outs[o][n * k:n * k + n, b:b + rows] = ins[2 * g + k][:, a:a + rows]
+
+
 class Flow:
-    def __init__(self, chain, count, total, bits, rest, cut, keep, send, name, head=False):
-        self.chain, self.count, self.total, self.rest, self.cut, self.head = chain, count, total, rest, cut, head
-        self.core, self.x, self.y, self.z1, self.z0 = bits
-        self.rows = keep.shape[1]
-        self.name = name
-        self.held = [keep, self.to(send, self.core)]
+    def __init__(self, chain, total, bits, rest, parts, keep, send, name, head=False):
+        self.chain, self.total, self.bits, self.rest, self.parts = chain, total, bits, rest, parts
+        self.name, self.head = name, head
+        self.whole = {p: (0, sum(r for r, _ in parts[:p])) for p in range(len(parts))}
+        self.level, self.down, self.at = 0, True, self.whole
+        self.held = [keep, self.to(send, bits["c"])]
 
     def to(self, v, mask):
         with jax.named_scope(self.name + str(mask)):
             return xor_send(v, mask, self.total)
 
-    def shapes(self, n):
-        return [((n, self.cut, 128), bf), ((n, self.rows - self.cut, 128), bf)]
-
-    def run(self, kernel, outs, args):
-        return self.chain(kernel, outs, args, limit=4)
-
-    def add_core(self):
-        a, b = self.shapes(8)
-        a0, a1, b0, b1 = self.run(add_core_kernel, [a, a, b, b], self.held)
-        self.held = [a0, self.to(a1, self.x), b0, self.to(b1, self.y)]
-
-    def add_first(self):
-        a, b = self.shapes(4)
-        a0, a1, b0, b1 = self.run(add_pair_kernel, [a, a, b, b], self.held)
-        self.held = [a0, self.to(a1, self.y), b0, self.to(b1, self.x)]
-
-    def add_second(self):
-        parts = self.run(add_merge_kernel, [((2, self.rows, 128), bf)] * 2, self.held)
-        self.held = [parts[0], self.to(parts[1], self.z0)]
-
-    def add_z(self):
-        parts = self.run(add_split_kernel, [((1, self.rows, 128), bf)] * 2, self.held)
-        self.held = [parts[0], self.to(parts[1], self.z1)]
-
-    def add_last(self):
-        (own,) = self.run(add_split_kernel, [((1, self.rows, 128), bf)], self.held)
+    def shapes(self, groups, n):
+        return [((n, sum(self.parts[p][0] for p in g), 128), bf) for g in groups]
+
+    def axis(self, group, level):
+        return self.parts[group[0]][1][level]
+
+    def step(self):
+        (self.add if self.down else self.join)()
+
+    def add(self):
+        n = self.held[0].shape[0]
+        last = self.level == 4
+        groups = grouped(self.parts, 3 if last else self.level)
+        at = places(self.parts, groups)
+        shapes = self.shapes(groups, n if last else n // 2)
+        outs = self.chain(functools.partial(add_kernel, self.parts, self.at, at, 1 if last else 2),
+                          shapes if last else [s for s in shapes for _ in range(2)], self.held, limit=4)
+        self.at = at
+        if not last:
+            self.held = [v for g, (a, b) in zip(groups, zip(outs[::2], outs[1::2]))
+                         for v in (a, self.to(b, self.bits[self.axis(g, self.level)]))]
+            self.level += 1
+            return
         for m in self.rest:
-            own = own + self.to(own, m)
-        self.held = [own, self.to(own, self.z1)]
-
-    def join_last(self):
-        (v,) = self.run(join_kernel, [((2, self.rows, 128), bf)], self.held)
-        self.held = [v, self.to(v, self.z0)]
-
-    def join_z(self):
-        if self.head:
-            (v,) = self.run(join_kernel, [((4, self.rows, 128), bf)], self.held)
-            self.held = [v, self.to(v, self.y)]
-        else:
-            a, b = self.run(functools.partial(join_split_kernel, self.cut), self.shapes(4), self.held)
-            self.held = [a, self.to(a, self.y), b, self.to(b, self.x)]
-
-    def join_first(self):
-        if self.head:
-            (v,) = self.run(join_kernel, [((8, self.rows, 128), bf)], self.held)
-            self.held = [v, self.to(v, self.core)]
-        else:
-            a, b = self.run(join_pair_kernel, self.shapes(8), self.held)
-            self.held = [a, self.to(a, self.x), b, self.to(b, self.y)]
-
-    def join_second(self):
-        (v,) = self.run(join_merge_kernel, [((16, self.rows, 128), bf)], self.held)
-        self.held = [v, self.to(v, self.core)]
+            outs = [v + self.to(v, m) for v in outs]
+        self.down = False
+        self.level = 3
+        self.spread(groups, outs)
+
+    def spread(self, groups, arrays):
+        if self.head and self.axis(groups[0], self.level) == "x":
+            self.level -= 1
+        if self.level < 0:
+            self.held = [v for a in arrays for v in (a, self.to(a, self.bits["c"]))]
+            return
+        self.held = [v for g, a in zip(groups, arrays) for v in (a, self.to(a, self.bits[self.axis(g, self.level)]))]
+
+    def join(self):
+        n = self.held[0].shape[0]
+        self.level -= 1
+        groups = grouped(self.parts, self.level) if self.level >= 0 else [list(range(len(self.parts)))]
+        at = places(self.parts, groups)
+        outs = self.chain(functools.partial(join_kernel, self.parts, self.at, at), self.shapes(groups, 2 * n),
+                          self.held, limit=4)
+        self.at = at
+        self.spread(groups, outs)
 
 
 def assemble(refs, scr):
@@ -635,8 +648,16 @@
         k += a.shape[0]
 
 
-def slab(scr, index, at):
-    return scr[index, at:at + 48, :].astype(f32)
+def finder(scr, parts, masks, count):
+    where, mes = layout(parts), [me_of(m, count) for m in masks]
+    base = [sum(part_rows(items) for _, items in parts[:p]) for p in range(len(parts))]
+
+    def find(name, k, b):
+        p, at = where[name, k]
+        at += base[p]
+        return scr[b ^ mes[p], at:at + SLAB_ROWS.get(name, 48), :].astype(f32)
+
+    return find
 
 
 def vectors(tmp, row, outs):
@@ -660,33 +681,31 @@
 
 
 def unpack_ffn(count, masks, here, there, inner, up, down, bias, gain, scr, tmp):
-    me_a, me_b = (me_of(m, count) for m in masks)
     assemble((here, there), scr)
+    find = finder(scr, FFN_PARTS, masks, count)
     for b in range(32):
-        a_at, b_at = b ^ me_a, b ^ me_b
         j, i = b // 8, b % 8
         rows = slice(48 * i, 48 * i + 48)
         for k in range(3):
             cols = slice(TILE * j + 128 * k, TILE * j + 128 * k + 128)
-            inner[rows, cols] = slab(scr, a_at, 48 * k)
-            up[rows, cols] = slab(scr, a_at, 160) if k == 0 else slab(scr, b_at, 208 + 48 * (k - 1))
-            down[48 * b:48 * b + 48, 128 * k:128 * k + 128] = slab(scr, b_at, 304 + 48 * k)
-    tmp[...] = scr[me_a, 144:160, :].astype(f32)
+            inner[rows, cols] = find("inner", k, b)
+            up[rows, cols] = find("up", k, b)
+            down[48 * b:48 * b + 48, 128 * k:128 * k + 128] = find("down", k, b)
+    tmp[...] = find("vector", 0, 0)
     vectors(tmp, 0, (bias, gain))
 
 
 def unpack_tokens(count, masks, here, there, gq, gk, gv, wo, out, tin, skip, bin_, bout, gain, scr, tmp):
-    me_a, me_b = (me_of(m, count) for m in masks)
     assemble((here, there), scr)
+    find = finder(scr, TOKEN_PARTS, masks, count)
     for b in range(32):
-        a_at, b_at = b ^ me_a, b ^ me_b
         j, i = b // 8, b % 8
-        tmp[16 * b:16 * b + 16, :] = scr[a_at, 144:160, :].astype(f32)
+        tmp[16 * b:16 * b + 16, :] = find("small", 0, b)
         for k in range(3):
             c = TILE * j + 128 * k
-            (gq, gk, gv)[c // 512][48 * i:48 * i + 48, c % 512:c % 512 + 128] = slab(scr, a_at, 48 * k)
-            out[48 * b:48 * b + 48, 128 * k:128 * k + 128] = slab(scr, b_at, 160 + 48 * k)
-            wo[16 * b:16 * b + 16, 128 * k:128 * k + 128] = scr[b_at, 304 + 16 * k:320 + 16 * k, :].astype(f32)
+            (gq, gk, gv)[c // 512][48 * i:48 * i + 48, c % 512:c % 512 + 128] = find("attention", k, b)
+            out[48 * b:48 * b + 48, 128 * k:128 * k + 128] = find("final", k, b)
+            wo[16 * b:16 * b + 16, 128 * k:128 * k + 128] = find("merge", k, b)
     for c in range(12):
         tin[:, 128 * c:128 * c + 128] = tmp[32 * c:32 * c + 32, :]
     for i in range(3):
@@ -704,11 +723,13 @@
     inner = wq.shape[1]
     total = wide * count
     X, CORE, Y, Z0, Z1 = 1, count, 2 * count, 4 * count, 8 * count
-    bits = (CORE, X, Y, Z1, Z0)
+    bits = {"c": CORE, "x": X, "y": Y, "p": Z0, "q": Z1}
     narrow_rest = [1 << i for i in range(1, count.bit_length() - 1)]
     wide_rest = [count << i for i in range(4, wide.bit_length() - 1)]
-    masks = [[CORE, X, Y, Z0, Z1], [CORE, Y, X, Z0, Z1]]
-    column_masks = [CORE, Y, Z0, Z1]
+    ffn_masks, token_masks = ([[CORE] + [bits[a] for a in order] for order, _ in parts]
+                              for parts in (FFN_PARTS, TOKEN_PARTS))
+    column_masks = [CORE] + [bits[a] for a in HEAD_ORDER if a != "x"]
+    ffn_rows, token_rows = ([r for r, _ in sizes(parts)] for parts in (FFN_PARTS, TOKEN_PARTS))
     chain = Chain()
     vmem = pltpu.VMEM
 
@@ -741,19 +762,18 @@
          ((rows, width), bf), ((rows, width), bf)],
         [embed, mixed, wm, gain_two, we, wc, wri, bri])
 
-    cut = first_rows(cols)
     groups = max(count // 2, 1)
 
     def columns():
         out = chain(
             functools.partial(columns_kernel, count, column_masks), [((16, cols, 128), bf)] * (2 * groups),
             [states, hidh, sigma] + cots,
-            scratch=[vmem((cols, 128), f32)] + [vmem((32, n, 128), bf) for n in (cut, cols - cut)] * groups, limit=24)
+            scratch=[vmem((cols, 128), f32)] + [vmem((32, cols, 128), bf)] * groups, limit=24)
         first = list(out[:2])
         for i in range(1, groups):
             for k in range(2):
                 first[k] = first[k] + xor_send(out[2 * i + k], 2 * i, total)
-        return Flow(chain, count, total, bits, wide_rest, cut, *first, "columns", head=True)
+        return Flow(chain, total, bits, wide_rest, [(cols, HEAD_ORDER)], *first, "columns", head=True)
 
     def gate():
         out = []
@@ -772,10 +792,11 @@
 
     def ffn_back():
         gmiddle, keep, send = chain(
-            functools.partial(ffn_back_kernel, count, masks), [((rows, dim), bf)] + [((16, 448, 128), bf)] * 2,
+            functools.partial(ffn_back_kernel, count, ffn_masks),
+            [((rows, dim), bf)] + [((16, sum(ffn_rows), 128), bf)] * 2,
             [gstates, states, gpre, sums, hid2, d2, normed2, middle, wc, we, gain_two],
-            scratch=[vmem((32, 208, 128), bf), vmem((32, 240, 128), bf), vmem((16, 128), f32)])
-        return gmiddle, Flow(chain, count, total, bits, narrow_rest + wide_rest, 208, keep, send, "ffn")
+            scratch=[vmem((32, n, 128), bf) for n in ffn_rows] + [vmem((16, 128), f32)])
+        return gmiddle, Flow(chain, total, bits, narrow_rest + wide_rest, sizes(FFN_PARTS), keep, send, "ffn")
 
     def attend_back():
         return chain(attend_back_kernel, [((rows, 3 * inner), bf)], [gmiddle, wm, qkv, probs],
@@ -783,17 +804,17 @@
 
     def project_back():
         return chain(
-            functools.partial(project_back_kernel, count, masks),
-            [((rows, dim), bf), ((1, dim), f32), ((32, 144, 128), bf), ((32, 48, 128), bf)],
+            functools.partial(project_back_kernel, count, token_masks),
+            [((rows, dim), bf), ((1, dim), f32)] + [((32, n, 128), bf) for n in token_rows],
             [gqkv, gmiddle, mixed, normed1, embed, wq, wk, wv, gain_one])
 
     def tokens_back():
         gscaled, keep, send = chain(
-            functools.partial(tokens_back_kernel, count, masks, patch),
-            [((series, points), f32)] + [((16, 352, 128), bf)] * 2,
-            [gembed, hid1, d1, patches, wfin, wskip, wi, gg1, part_a, part_b],
-            scratch=[vmem((32, 16, 128), bf), vmem((32, 144, 128), bf), vmem((512, 128), f32)])
-        return gscaled, Flow(chain, count, total, bits, narrow_rest + wide_rest, 160, keep, send, "tokens")
+            functools.partial(tokens_back_kernel, count, token_masks, patch),
+            [((series, points), f32)] + [((16, sum(token_rows), 128), bf)] * 2,
+            [gembed, hid1, d1, patches, wfin, wskip, wi, gg1] + earlier,
+            scratch=[vmem((32, n, 128), bf) for n in token_rows] + [vmem((512, 128), f32)])
+        return gscaled, Flow(chain, total, bits, narrow_rest + wide_rest, sizes(TOKEN_PARTS), keep, send, "tokens")
 
     def forecast():
         out = chain(
@@ -811,55 +832,55 @@
                      one.held, scratch=[vmem((16, cols, 128), bf), vmem((cols, 128), f32)], limit=24)
 
     def finish_ffn():
-        return chain(functools.partial(unpack_ffn, count, masks),
+        return chain(functools.partial(unpack_ffn, count, ffn_masks),
                      [((dim, width), f32)] * 2 + [((width, dim), f32), ((width,), f32), ((dim,), f32)], two.held,
-                     scratch=[vmem((32, 448, 128), bf), vmem((16, 128), f32)], limit=24)
+                     scratch=[vmem((32, sum(ffn_rows), 128), bf), vmem((16, 128), f32)], limit=24)
 
     def finish_tokens():
         return chain(
-            functools.partial(unpack_tokens, count, masks),
+            functools.partial(unpack_tokens, count, token_masks),
             [((dim, inner), f32)] * 3 + [((inner, dim), f32), ((width, dim), f32), ((2 * patch, width), f32),
                                          ((2 * patch, dim), f32), ((width,), f32), ((dim,), f32), ((dim,), f32)],
-            three.held, scratch=[vmem((32, 352, 128), bf), vmem((512, 128), f32)], limit=24)
-
+            three.held, scratch=[vmem((32, sum(token_rows), 128), bf), vmem((512, 128), f32)], limit=24)
+
+    far_both = gate()
     one = columns()
-    far_both = gate()
     gstates, gpre, sums, mats, shorts = head()
-    one.add_core()
     gmiddle, two = ffn_back()
     gqkv = attend_back()
-    one.add_first()
-    two.add_core()
-    gembed, gg1, part_a, part_b = project_back()
+    gembed, gg1, *earlier = project_back()
+    two.step()
     gscaled, three = tokens_back()
-    one.add_second()
+    one.step()
     preds, g_series = forecast()
-    three.add_core()
-    two.add_first()
-    one.add_z()
-    three.add_first()
-    two.add_second()
-    one.add_last()
-    three.add_second()
-    one.join_last()
-    two.add_z()
-    one.join_z()
-    three.add_z()
-    two.add_last()
-    three.add_last()
-    one.join_first()
+    three.step()
+    two.step()
     prediction = place()
-    two.join_last()
-    three.join_last()
+    one.step()
+    three.step()
+    two.step()
+    three.step()
+    two.step()
+    one.step()
+    three.step()
+    one.step()
+    two.step()
+    three.step()
+    two.step()
+    one.step()
+    three.step()
+    one.step()
+    two.step()
+    three.step()
+    three.step()
+    two.step()
+    one.step()
+    two.step()
+    ffn_out = finish_ffn()
+    one.step()
+    three.step()
+    tokens_out = finish_tokens()
     columns_out = finish_columns()
-    two.join_z()
-    three.join_z()
-    two.join_first()
-    three.join_first()
-    two.join_second()
-    three.join_second()
-    ffn_out = finish_ffn()
-    tokens_out = finish_tokens()
     g_hw, g_hs, g_hb = columns_out
     g_hiw, g_up, g_down, g_hib, g_g2 = ffn_out
     g_q, g_k, g_v, g_wo, g_to, g_ti, g_ts, g_tib, g_tob, g_g1 = tokens_out

time: 188 us -> 156 us (0.83)
  waiting for transfers between devices: 87.7 us -> 54 us
    ppermute x43 -> x45, waiting for transfers between devices: 87.7 us -> 54 us  [xor_send(): return lax.ppermute(v, AXES, [(i, i ^ mask) for i in range(total)])]
    ppermute x43 -> x45, starting transfers between devices: 49.5 us -> 50.7 us  [xor_send(): return lax.ppermute(v, AXES, [(i, i ^ mask) for i in range(total)])]
  transfers between devices with their start and end apart: 43 -> 45, of which waited for: 19 -> 24; matrix products, arithmetic and copies ran while one was open for 0% -> 0% of each run, Pallas kernels for 15% -> 21%
where the time goes in v1:
time: 156 us; the launch traced here: 155 us
  waiting for transfers between devices  54 us (35%)
  starting transfers between devices  50.7 us (32%)
  Pallas kernels  45.4 us (29%)
  local copies, waits for them, and re-layouts  4.12 us (3%)
    ppermute x45, waiting for transfers between devices, xor_send(): return lax.ppermute(v, AXES, [(i, i ^ mask) for i in range(total)])  54 us
    ppermute x45, starting transfers between devices, xor_send(): return lax.ppermute(v, AXES, [(i, i ^ mask) for i in range(total)])  50.7 us
    pallas_call x42, Pallas kernels, __call__(): pl.pallas_call(body, name=name, out_shape=[jax.ShapeDtypeStruct(s, d) for...  45.4 us
    unnamed x24, local copies, waits for them, and re-layouts  4.12 us
  transfers between devices with their start and end apart: 45, of which 24 were waited for; matrix products, arithmetic and copies ran while one was open for 0% of the time, Pallas kernels for 21%

profile of v1, /device:TPU:0, one launch (start us, length us, event | category | flops | bytes accessed | tf_op | source)
XLA Modules:
  0.0 155.3 jit_solution(3935940666553625706)
XLA Ops:
  3.0 3.0 %collective-permute-start.1 = (bf16[288,1024]{1,0:T(8,128)(2,1)S(1)}, bf16[288,1024]{1,0:T(8,128)(2,1)S(1)}, u32[]{:S(2)}, u32[]{:S(2)}) collective-permute-start(bf16[288,1024]{1,0:T(8,128)(2,1)S(1)} %get-tuple-element.151), channel_id=1, source_target_pairs={{0,1},{1,0},{2,3},{3,2},{4,5},{5,4},{6,7},{7,6},{8,9},{9,8},{10,11... | collective-permute-start | bytes 1769480 | tf_op jit(solution)/shard_map/ppermute | solution.py:542
  6.1 5.4 %tokens_kernel.1 = (bf16[512,32]{1,0:T(8,128)(2,1)S(1)}, bf16[512,1536]{1,0:T(8,128)(2,1)S(1)}, bf16[512,1536]{1,0:T(8,128)(2,1)S(1)}, f32[512,384]{1,0:T(8,128)...) custom-call(f32[16,512]{1,0:T(8,128)S(1)} %copy-done.1, ...), custom_call_target="tpu_custom_call" | custom-call | flops 1000 | bytes 1000 | tf_op jit(solution)/shard_map/tokens_kernel/pallas_call | solution.py:52
  12.9 4.5 %ffn_kernel.1 = (f32[512,384]{1,0:T(8,128)S(1)}, bf16[512,384]{1,0:T(8,128)(2,1)S(1)}, bf16[512,1536]{1,0:T(8,128)(2,1)S(1)}, bf16[512,1536]{1,0:T(8,128)(2,1)S(...) custom-call(f32[512,384]{1,0:T(8,128)S(1)} %get-tuple-element.139.refs_0_.refs_4_, ...), custom_call_target="tpu_custom_call" | custom-call | flops 1000 | bytes 1000 | tf_op jit(solution)/shard_map/ffn_kernel/pallas_call | solution.py:52
  17.4 2.7 %collective-permute-done.1.refs_0_ = bf16[288,1024]{1,0:T(8,128)(2,1)S(1)} collective-permute-done((bf16[288,1024]{1,0:T(8,128)(2,1)S(1)}, bf16[288,1024]{1,0:T(8,128)(2,1)S(1)}, u32[]{:S(2)}, u32[]{:S(2)}) %collective-permute-start.1) | collective-permute-done | bytes 589856 | tf_op jit(solution)/shard_map/ppermute | solution.py:542
  20.3 5.4 %collective-permute-done.refs_4_.refs_12_ = bf16[288,512]{1,0:T(8,128)(2,1)S(1)} collective-permute-done((bf16[288,512]{1,0:T(8,128)(2,1)S(1)}, bf16[288,512]{1,0:T(8,128)(2,1)S(1)}, u32[]{:S(2)}, u32[]{:S(2)}) %collective-permute-start) | collective-permute-done | bytes 294944 | tf_op jit(solution)/shard_map/ppermute | solution.py:542
  27.7 3.8 %head_kernel.1 = (bf16[512,384]{1,0:T(8,128)(2,1)S(1)}, bf16[512,1536]{1,0:T(8,128)(2,1)S(1)}, f32[1,1536]{1,0:T(1,128)S(1)}, bf16[288,1536]{1,0:T(8,128)(2,1)S(1)}, bf16[288,512]{1,0:T(8,128)(2,1)S(1)}) custom-call(bf16[512,1536]{1,0:T(8,128)(2,1)S(1)} %get-tuple-element.148.refs_0_, f32[1,512]{1,0:T(1,128)S(1)} %get-tuple-element.141.refs_1_.refs_2_.refs_5_, ...), custom_call_target="tpu_custom_call" | custom-call | flops 1000 | bytes 1000 | tf_op jit(solution)/shard_map/head_kernel/pallas_call | solution.py:52
  31.5 5.2 %ffn_back_kernel.1 = (bf16[512,384]{1,0:T(8,128)(2,1)S(1)}, bf16[16,448,128]{2,1,0:T(8,128)(2,1)S(1)}, bf16[16,448,128]{2,1,0:T(8,128)(2,1)S(1)}) custom-call(bf16[512,384]{1,0:T(8,128)(2,1)S(1)} %get-tuple-element.157.refs_0_, bf16[512,384]{1,0:T(8,128)(2,1)S(1)} %get-tuple-element.154.refs_0_.refs_1_.refs_4_, ...), custom_call_target="tpu_custom_call" | custom-call | flops 1000 | bytes 1000 | tf_op jit(solution)/shard_map/ffn_back_kernel/pallas_call | solution.py:52
  45.3 3.8 %tokens_back_kernel.1 = (f32[16,512]{1,0:T(8,128)S(1)}, bf16[16,352,128]{2,1,0:T(8,128)(2,1)S(1)}, bf16[16,352,128]{2,1,0:T(8,128)(2,1)S(1)}) custom-call(bf16[512,384]{1,0:T(8,128)(2,1)S(1)} %get-tuple-element.168.refs_0_, bf16[512,1536]{1,0:T(8,128)(2,1)S(1)} %get-tuple-element.169.refs_1_, bf16[512,1536]{1,0:T(8,128)(2,1)S(1)} %get-tuple-element.170.refs_2_, ...), custom_call_target="tpu_custom_call" | custom-call | flops 1000 | bytes 1000 | tf_op jit(solution)/shard_map/tokens_back_kernel/pallas_call | solution.py:52
  57.5 2.6 %collective-permute-start.15 = (bf16[4,208,128]{2,1,0:T(8,128)(2,1)S(1)}, bf16[4,208,128]{2,1,0:T(8,128)(2,1)S(1)}, u32[]{:S(2)}, u32[]{:S(2)}) collective-permute-start(bf16[4,208,128]{2,1,0:T(8,128)(2,1)S(1)} %get-tuple-element.208), channel_id=1, source_target_pairs={{0,16},{1,17},{2,18},{3,19},{4,20},{5,21},{6,22},{7,23},{8,24},{9,... | collective-permute-start | bytes 638984 | tf_op jit(solution)/shard_map/ffn16/ppermute | solution.py:542
  60.2 3.5 %collective-permute-done.5.refs_1_ = bf16[288,512]{1,0:T(8,128)(2,1)S(1)} collective-permute-done((bf16[288,512]{1,0:T(8,128)(2,1)S(1)}, bf16[288,512]{1,0:T(8,128)(2,1)S(1)}, u32[]{:S(2)}, u32[]{:S(2)}) %collective-permute-start.5) | collective-permute-done | bytes 294944 | tf_op jit(solution)/shard_map/ppermute | solution.py:542
  65.0 4.8 %collective-permute-done.11.refs_1_ = bf16[8,288,128]{2,1,0:T(8,128)(2,1)S(1)} collective-permute-done((bf16[8,288,128]{2,1,0:T(8,128)(2,1)S(1)}, bf16[8,288,128]{2,1,0:T(8,128)(2,1)S(1)}, u32[]{:S(2)}, u32[]{:S(2)}) %collective-permute-start.11) | collective-permute-done | bytes 589856 | tf_op jit(solution)/shard_map/columns8/ppermute | solution.py:542
  80.9 2.5 %collective-permute-start.16 = (bf16[2,352,128]{2,1,0:T(8,128)(2,1)S(1)}, bf16[2,352,128]{2,1,0:T(8,128)(2,1)S(1)}, u32[]{:S(2)}, u32[]{:S(2)}) collective-permute-start(bf16[2,352,128]{2,1,0:T(8,128)(2,1)S(1)} %get-tuple-element.211), channel_id=1, source_target_pairs={{0,8},{1,9},{2,10},{3,11},{4,12},{5,13},{6,14},{7,15},{8,0},{9,1},... | collective-permute-start | bytes 540680 | tf_op jit(solution)/shard_map/tokens8/ppermute | solution.py:542
  89.4 2.8 %collective-permute-done.16.refs_1_ = bf16[2,352,128]{2,1,0:T(8,128)(2,1)S(1)} collective-permute-done((bf16[2,352,128]{2,1,0:T(8,128)(2,1)S(1)}, bf16[2,352,128]{2,1,0:T(8,128)(2,1)S(1)}, u32[]{:S(2)}, u32[]{:S(2)}) %collective-permute-start.16) | collective-permute-done | bytes 180256 | tf_op jit(solution)/shard_map/tokens8/ppermute | solution.py:542
  97.0 2.7 %collective-permute-start.25 = (bf16[1,288,128]{2,1,0:T(8,128)(2,1)S(1)}, bf16[1,288,128]{2,1,0:T(8,128)(2,1)S(1)}, u32[]{:S(2)}, u32[]{:S(2)}) collective-permute-start(bf16[1,288,128]{2,1,0:T(8,128)(2,1)S(1)} %get-tuple-element.226), channel_id=1, source_target_pairs={{0,4},{1,5},{2,6},{3,7},{4,0},{5,1},{6,2},{7,3},{8,12},{9,13},{10,... | collective-permute-start | bytes 221192 | tf_op jit(solution)/shard_map/columns4/ppermute | solution.py:542
  102.1 3.2 %collective-permute-start.31 = (bf16[1,288,128]{2,1,0:T(8,128)(2,1)S(1)}, bf16[1,288,128]{2,1,0:T(8,128)(2,1)S(1)}, u32[]{:S(2)}, u32[]{:S(2)}) collective-permute-start(bf16[1,288,128]{2,1,0:T(8,128)(2,1)S(1)} %add_kernel.29.refs_2_.refs_0_), channel_id=1, source_target_pairs={{0,4},{1,5},{2,6},{3,7},{4,0},{5,1},{6,2},{7,3},{8,12},{9,13},{10,... | collective-permute-start | bytes 221192 | tf_op jit(solution)/shard_map/columns4/ppermute | solution.py:542
  107.7 2.5 %collective-permute-done.29.refs_1_ = bf16[2,240,128]{2,1,0:T(8,128)(2,1)S(1)} collective-permute-done((bf16[2,240,128]{2,1,0:T(8,128)(2,1)S(1)}, bf16[2,240,128]{2,1,0:T(8,128)(2,1)S(1)}, u32[]{:S(2)}, u32[]{:S(2)}) %collective-permute-start.29) | collective-permute-done | bytes 122912 | tf_op jit(solution)/shard_map/ffn8/ppermute | solution.py:542
  113.0 3.3 %collective-permute-start.33 = (bf16[4,192,128]{2,1,0:T(8,128)(2,1)S(1)}, bf16[4,192,128]{2,1,0:T(8,128)(2,1)S(1)}, u32[]{:S(2)}, u32[]{:S(2)}) collective-permute-start(bf16[4,192,128]{2,1,0:T(8,128)(2,1)S(1)} %get-tuple-element.232.refs_2_), channel_id=1, source_target_pairs={{0,1},{1,0},{2,3},{3,2},{4,5},{5,4},{6,7},{7,6},{8,9},{9,8},{10,11... | collective-permute-start | bytes 589832 | tf_op jit(solution)/shard_map/tokens1/ppermute | solution.py:542
  116.4 5.2 %collective-permute-done.32.refs_1_ = bf16[4,160,128]{2,1,0:T(8,128)(2,1)S(1)} collective-permute-done((bf16[4,160,128]{2,1,0:T(8,128)(2,1)S(1)}, bf16[4,160,128]{2,1,0:T(8,128)(2,1)S(1)}, u32[]{:S(2)}, u32[]{:S(2)}) %collective-permute-start.32) | collective-permute-done | bytes 163872 | tf_op jit(solution)/shard_map/tokens4/ppermute | solution.py:542
  121.7 3.5 %collective-permute-done.38.refs_3_ = bf16[4,208,128]{2,1,0:T(8,128)(2,1)S(1)} collective-permute-done((bf16[4,208,128]{2,1,0:T(8,128)(2,1)S(1)}, bf16[4,208,128]{2,1,0:T(8,128)(2,1)S(1)}, u32[]{:S(2)}, u32[]{:S(2)}) %collective-permute-start.38) | collective-permute-done | bytes 213024 | tf_op jit(solution)/shard_map/ffn16/ppermute | solution.py:542
  127.0 6.4 %collective-permute-done.41.refs_3_ = bf16[8,208,128]{2,1,0:T(8,128)(2,1)S(1)} collective-permute-done((bf16[8,208,128]{2,1,0:T(8,128)(2,1)S(1)}, bf16[8,208,128]{2,1,0:T(8,128)(2,1)S(1)}, u32[]{:S(2)}, u32[]{:S(2)}) %collective-permute-start.41) | collective-permute-done | bytes 426016 | tf_op jit(solution)/shard_map/ffn4/ppermute | solution.py:542
  138.5 3.4 %unpack_ffn.1 = (f32[384,1536]{1,0:T(8,128)}, f32[384,1536]{1,0:T(8,128)}, f32[1536,384]{1,0:T(8,128)}, f32[1536]{0:T(1024)}, f32[384]{0:T(512)}) custom-call(bf16[16,448,128]{2,1,0:T(8,128)(2,1)S(1)} %join_kernel.19.refs_0_, bf16[16,448,128]{2,1,0:T(8,128)(2,1)S(1)} %collective-permute-done.42.refs_1_), custom_call_target="tpu_custom_call" | custom-call | flops 1000 | bytes 1000 | tf_op jit(solution)/shard_map/unpack_ffn/pallas_call | solution.py:52
  141.9 4.3 %collective-permute-done.39.refs_1_ = bf16[4,288,128]{2,1,0:T(8,128)(2,1)S(1)} collective-permute-done((bf16[4,288,128]{2,1,0:T(8,128)(2,1)S(1)}, bf16[4,288,128]{2,1,0:T(8,128)(2,1)S(1)}, u32[]{:S(2)}, u32[]{:S(2)}) %collective-permute-start.39) | collective-permute-done | bytes 294944 | tf_op jit(solution)/shard_map/columns8/ppermute | solution.py:542
  147.6 2.7 %collective-permute-done.43.refs_1_ = bf16[16,352,128]{2,1,0:T(8,128)(2,1)S(1)} collective-permute-done((bf16[16,352,128]{2,1,0:T(8,128)(2,1)S(1)}, bf16[16,352,128]{2,1,0:T(8,128)(2,1)S(1)}, u32[]{:S(2)}, u32[]{:S(2)}) %collective-permute-start.43) | collective-permute-done | bytes 1441824 | tf_op jit(solution)/shard_map/tokens2/ppermute | solution.py:542
  150.3 2.8 %unpack_tokens.1 = (f32[384,512]{1,0:T(8,128)}, f32[384,512]{1,0:T(8,128)}, f32[384,512]{1,0:T(8,128)}, f32[512,384]{1,0:T(8,128)}, f32[1536,384]{1,0:T(8,128)},...) custom-call(bf16[16,352,128]{2,1,0:T(8,128)(2,1)S(1)} %join_kernel.21.refs_0_, ...), custom_call_target="tpu_custom_call" | custom-call | flops 1000 | bytes 1000 | tf_op jit(solution)/shard_map/unpack_tokens/pallas_call | solution.py:52
  (132 shorter events, 64.2 us)
Async XLA Ops:
  3.0 17.2 %collective-permute-start.1 = (bf16[288,1024]{1,0:T(8,128)(2,1)S(1)}, bf16[288,1024]{1,0:T(8,128)(2,1)S(1)}, u32[]{:S(2)}, u32[]{:S(2)}) collective-permute-start(bf16[288,1024]{1,0:T(8,128)(2,1)S(1)} %get-tuple-element.151), channel_id=1, source_target_pairs={{0,1},{1,0},{2,3},{3,2},{4,5},{5,4},{6,7},{7,6},{8,9},{9,8},{10,11... | collective-permute-start | bytes 1769480 | tf_op jit(solution)/shard_map/ppermute | solution.py:542
  6.0 19.6 %collective-permute-start = (bf16[288,512]{1,0:T(8,128)(2,1)S(1)}, bf16[288,512]{1,0:T(8,128)(2,1)S(1)}, u32[]{:S(2)}, u32[]{:S(2)}) collective-permute-start(bf16[288,512]{1,0:T(8,128)(2,1)S(1)} %get-tuple-element.138.refs_16_), channel_id=1, source_target_pairs={{0,1},{1,0},{2,3},{3,2},{4,5},{5,4},{6,7},{7,6},{8,9},{9,8},{10,11... | collective-permute-start | bytes 884744 | tf_op jit(solution)/shard_map/ppermute | solution.py:542
  36.7 12.5 %collective-permute-start.4 = (bf16[16,288,128]{2,1,0:T(8,128)(2,1)S(1)}, bf16[16,288,128]{2,1,0:T(8,128)(2,1)S(1)}, u32[]{:S(2)}, u32[]{:S(2)}) collective-permute-start(bf16[16,288,128]{2,1,0:T(8,128)(2,1)S(1)} %get-tuple-element.185), channel_id=1, source_target_pairs={{0,2},{1,3},{2,0},{3,1},{4,6},{5,7},{6,4},{7,5},{8,10},{9,11},{10,... | collective-permute-start | bytes 3538952 | tf_op jit(solution)/shard_map/columns2/ppermute | solution.py:542
  42.0 13.5 %collective-permute-start.7 = (bf16[8,208,128]{2,1,0:T(8,128)(2,1)S(1)}, bf16[8,208,128]{2,1,0:T(8,128)(2,1)S(1)}, u32[]{:S(2)}, u32[]{:S(2)}) collective-permute-start(bf16[8,208,128]{2,1,0:T(8,128)(2,1)S(1)} %get-tuple-element.191), channel_id=1, source_target_pairs={{0,4},{1,5},{2,6},{3,7},{4,0},{5,1},{6,2},{7,3},{8,12},{9,13},{10,... | collective-permute-start | bytes 1277960 | tf_op jit(solution)/shard_map/ffn4/ppermute | solution.py:542
  43.8 13.5 %collective-permute-start.6 = (bf16[8,240,128]{2,1,0:T(8,128)(2,1)S(1)}, bf16[8,240,128]{2,1,0:T(8,128)(2,1)S(1)}, u32[]{:S(2)}, u32[]{:S(2)}) collective-permute-start(bf16[8,240,128]{2,1,0:T(8,128)(2,1)S(1)} %get-tuple-element.190), channel_id=1, source_target_pairs={{0,1},{1,0},{2,3},{3,2},{4,5},{5,4},{6,7},{7,6},{8,9},{9,8},{10,11... | collective-permute-start | bytes 1474568 | tf_op jit(solution)/shard_map/ffn1/ppermute | solution.py:542
  49.5 20.3 %collective-permute-start.11 = (bf16[8,288,128]{2,1,0:T(8,128)(2,1)S(1)}, bf16[8,288,128]{2,1,0:T(8,128)(2,1)S(1)}, u32[]{:S(2)}, u32[]{:S(2)}) collective-permute-start(bf16[8,288,128]{2,1,0:T(8,128)(2,1)S(1)} %get-tuple-element.200), channel_id=1, source_target_pairs={{0,8},{1,9},{2,10},{3,11},{4,12},{5,13},{6,14},{7,15},{8,0},{9,1},... | collective-permute-start | bytes 1769480 | tf_op jit(solution)/shard_map/columns8/ppermute | solution.py:542
  53.3 10.4 %collective-permute-start.5 = (bf16[288,512]{1,0:T(8,128)(2,1)S(1)}, bf16[288,512]{1,0:T(8,128)(2,1)S(1)}, u32[]{:S(2)}, u32[]{:S(2)}) collective-permute-start(bf16[288,512]{1,0:T(8,128)(2,1)S(1)} %get-tuple-element.188), channel_id=1, source_target_pairs={{0,1},{1,0},{2,3},{3,2},{4,5},{5,4},{6,7},{7,6},{8,9},{9,8},{10,11... | collective-permute-start | bytes 884744 | tf_op jit(solution)/shard_map/ppermute | solution.py:542
  54.9 18.1 %collective-permute-start.10 = (bf16[8,192,128]{2,1,0:T(8,128)(2,1)S(1)}, bf16[8,192,128]{2,1,0:T(8,128)(2,1)S(1)}, u32[]{:S(2)}, u32[]{:S(2)}) collective-permute-start(bf16[8,192,128]{2,1,0:T(8,128)(2,1)S(1)} %get-tuple-element.199), channel_id=1, source_target_pairs={{0,4},{1,5},{2,6},{3,7},{4,0},{5,1},{6,2},{7,3},{8,12},{9,13},{10,... | collective-permute-start | bytes 1179656 | tf_op jit(solution)/shard_map/tokens4/ppermute | solution.py:542
  55.5 17.5 %collective-permute-start.9 = (bf16[8,160,128]{2,1,0:T(8,128)(2,1)S(1)}, bf16[8,160,128]{2,1,0:T(8,128)(2,1)S(1)}, u32[]{:S(2)}, u32[]{:S(2)}) collective-permute-start(bf16[8,160,128]{2,1,0:T(8,128)(2,1)S(1)} %get-tuple-element.197), channel_id=1, source_target_pairs={{0,1},{1,0},{2,3},{3,2},{4,5},{5,4},{6,7},{7,6},{8,9},{9,8},{10,11... | collective-permute-start | bytes 983048 | tf_op jit(solution)/shard_map/tokens1/ppermute | solution.py:542
  57.5 16.2 %collective-permute-start.15 = (bf16[4,208,128]{2,1,0:T(8,128)(2,1)S(1)}, bf16[4,208,128]{2,1,0:T(8,128)(2,1)S(1)}, u32[]{:S(2)}, u32[]{:S(2)}) collective-permute-start(bf16[4,208,128]{2,1,0:T(8,128)(2,1)S(1)} %get-tuple-element.208), channel_id=1, source_target_pairs={{0,16},{1,17},{2,18},{3,19},{4,20},{5,21},{6,22},{7,23},{8,24},{9,... | collective-permute-start | bytes 638984 | tf_op jit(solution)/shard_map/ffn16/ppermute | solution.py:542
  63.7 10.1 %collective-permute-start.14 = (bf16[4,240,128]{2,1,0:T(8,128)(2,1)S(1)}, bf16[4,240,128]{2,1,0:T(8,128)(2,1)S(1)}, u32[]{:S(2)}, u32[]{:S(2)}) collective-permute-start(bf16[4,240,128]{2,1,0:T(8,128)(2,1)S(1)} %get-tuple-element.207), channel_id=1, source_target_pairs={{0,4},{1,5},{2,6},{3,7},{4,0},{5,1},{6,2},{7,3},{8,12},{9,13},{10,... | collective-permute-start | bytes 737288 | tf_op jit(solution)/shard_map/ffn4/ppermute | solution.py:542
  71.2 16.7 %collective-permute-start.17 = (bf16[4,288,128]{2,1,0:T(8,128)(2,1)S(1)}, bf16[4,288,128]{2,1,0:T(8,128)(2,1)S(1)}, u32[]{:S(2)}, u32[]{:S(2)}) collective-permute-start(bf16[4,288,128]{2,1,0:T(8,128)(2,1)S(1)} %get-tuple-element.212), channel_id=1, source_target_pairs={{0,16},{1,17},{2,18},{3,19},{4,20},{5,21},{6,22},{7,23},{8,24},{9,... | collective-permute-start | bytes 884744 | tf_op jit(solution)/shard_map/columns16/ppermute | solution.py:542
  73.8 9.6 %collective-permute-start.19 = (bf16[2,208,128]{2,1,0:T(8,128)(2,1)S(1)}, bf16[2,208,128]{2,1,0:T(8,128)(2,1)S(1)}, u32[]{:S(2)}, u32[]{:S(2)}) collective-permute-start(bf16[2,208,128]{2,1,0:T(8,128)(2,1)S(1)} %get-tuple-element.215), channel_id=1, source_target_pairs={{0,1},{1,0},{2,3},{3,2},{4,5},{5,4},{6,7},{7,6},{8,9},{9,8},{10,11... | collective-permute-start | bytes 319496 | tf_op jit(solution)/shard_map/ffn1/ppermute | solution.py:542
  80.9 11.4 %collective-permute-start.16 = (bf16[2,352,128]{2,1,0:T(8,128)(2,1)S(1)}, bf16[2,352,128]{2,1,0:T(8,128)(2,1)S(1)}, u32[]{:S(2)}, u32[]{:S(2)}) collective-permute-start(bf16[2,352,128]{2,1,0:T(8,128)(2,1)S(1)} %get-tuple-element.211), channel_id=1, source_target_pairs={{0,8},{1,9},{2,10},{3,11},{4,12},{5,13},{6,14},{7,15},{8,0},{9,1},... | collective-permute-start | bytes 540680 | tf_op jit(solution)/shard_map/tokens8/ppermute | solution.py:542
  83.5 9.7 %collective-permute-start.22 = (bf16[1,208,128]{2,1,0:T(8,128)(2,1)S(1)}, bf16[1,208,128]{2,1,0:T(8,128)(2,1)S(1)}, u32[]{:S(2)}, u32[]{:S(2)}) collective-permute-start(bf16[1,208,128]{2,1,0:T(8,128)(2,1)S(1)} %get-tuple-element.222), channel_id=1, source_target_pairs={{0,8},{1,9},{2,10},{3,11},{4,12},{5,13},{6,14},{7,15},{8,0},{9,1},... | collective-permute-start | bytes 159752 | tf_op jit(solution)/shard_map/ffn8/ppermute | solution.py:542
  110.2 15.0 %collective-permute-start.37 = (bf16[4,240,128]{2,1,0:T(8,128)(2,1)S(1)}, bf16[4,240,128]{2,1,0:T(8,128)(2,1)S(1)}, u32[]{:S(2)}, u32[]{:S(2)}) collective-permute-start(bf16[4,240,128]{2,1,0:T(8,128)(2,1)S(1)} %get-tuple-element.235.refs_0_), channel_id=1, source_target_pairs={{0,4},{1,5},{2,6},{3,7},{4,0},{5,1},{6,2},{7,3},{8,12},{9,13},{10,... | collective-permute-start | bytes 737288 | tf_op jit(solution)/shard_map/ffn4/ppermute | solution.py:542
  111.4 13.8 %collective-permute-start.38 = (bf16[4,208,128]{2,1,0:T(8,128)(2,1)S(1)}, bf16[4,208,128]{2,1,0:T(8,128)(2,1)S(1)}, u32[]{:S(2)}, u32[]{:S(2)}) collective-permute-start(bf16[4,208,128]{2,1,0:T(8,128)(2,1)S(1)} %get-tuple-element.230.refs_2_), channel_id=1, source_target_pairs={{0,16},{1,17},{2,18},{3,19},{4,20},{5,21},{6,22},{7,23},{8,24},{9,... | collective-permute-start | bytes 638984 | tf_op jit(solution)/shard_map/ffn16/ppermute | solution.py:542
  113.0 8.6 %collective-permute-start.33 = (bf16[4,192,128]{2,1,0:T(8,128)(2,1)S(1)}, bf16[4,192,128]{2,1,0:T(8,128)(2,1)S(1)}, u32[]{:S(2)}, u32[]{:S(2)}) collective-permute-start(bf16[4,192,128]{2,1,0:T(8,128)(2,1)S(1)} %get-tuple-element.232.refs_2_), channel_id=1, source_target_pairs={{0,1},{1,0},{2,3},{3,2},{4,5},{5,4},{6,7},{7,6},{8,9},{9,8},{10,11... | collective-permute-start | bytes 589832 | tf_op jit(solution)/shard_map/tokens1/ppermute | solution.py:542
  116.4 10.6 %collective-permute-start.36 = (bf16[2,288,128]{2,1,0:T(8,128)(2,1)S(1)}, bf16[2,288,128]{2,1,0:T(8,128)(2,1)S(1)}, u32[]{:S(2)}, u32[]{:S(2)}) collective-permute-start(bf16[2,288,128]{2,1,0:T(8,128)(2,1)S(1)} %join_kernel.13.refs_4_.refs_0_), channel_id=1, source_target_pairs={{0,16},{1,17},{2,18},{3,19},{4,20},{5,21},{6,22},{7,23},{8,24},{9,... | collective-permute-start | bytes 442376 | tf_op jit(solution)/shard_map/columns16/ppermute | solution.py:542
  125.3 8.2 %collective-permute-start.41 = (bf16[8,208,128]{2,1,0:T(8,128)(2,1)S(1)}, bf16[8,208,128]{2,1,0:T(8,128)(2,1)S(1)}, u32[]{:S(2)}, u32[]{:S(2)}) collective-permute-start(bf16[8,208,128]{2,1,0:T(8,128)(2,1)S(1)} %get-tuple-element.236.refs_2_), channel_id=1, source_target_pairs={{0,4},{1,5},{2,6},{3,7},{4,0},{5,1},{6,2},{7,3},{8,12},{9,13},{10,... | collective-permute-start | bytes 1277960 | tf_op jit(solution)/shard_map/ffn4/ppermute | solution.py:542
  125.7 8.8 %collective-permute-start.40 = (bf16[8,240,128]{2,1,0:T(8,128)(2,1)S(1)}, bf16[8,240,128]{2,1,0:T(8,128)(2,1)S(1)}, u32[]{:S(2)}, u32[]{:S(2)}) collective-permute-start(bf16[8,240,128]{2,1,0:T(8,128)(2,1)S(1)} %get-tuple-element.237.refs_0_), channel_id=1, source_target_pairs={{0,1},{1,0},{2,3},{3,2},{4,5},{5,4},{6,7},{7,6},{8,9},{9,8},{10,11... | collective-permute-start | bytes 1474568 | tf_op jit(solution)/shard_map/ffn1/ppermute | solution.py:542
  134.7 12.2 %collective-permute-start.35 = (bf16[8,192,128]{2,1,0:T(8,128)(2,1)S(1)}, bf16[8,192,128]{2,1,0:T(8,128)(2,1)S(1)}, u32[]{:S(2)}, u32[]{:S(2)}) collective-permute-start(bf16[8,192,128]{2,1,0:T(8,128)(2,1)S(1)} %get-tuple-element.234.refs_2_), channel_id=1, source_target_pairs={{0,4},{1,5},{2,6},{3,7},{4,0},{5,1},{6,2},{7,3},{8,12},{9,13},{10,... | collective-permute-start | bytes 1179656 | tf_op jit(solution)/shard_map/tokens4/ppermute | solution.py:542
  136.4 10.5 %collective-permute-start.34 = (bf16[8,160,128]{2,1,0:T(8,128)(2,1)S(1)}, bf16[8,160,128]{2,1,0:T(8,128)(2,1)S(1)}, u32[]{:S(2)}, u32[]{:S(2)}) collective-permute-start(bf16[8,160,128]{2,1,0:T(8,128)(2,1)S(1)} %get-tuple-element.233.refs_4_.refs_0_), channel_id=1, source_target_pairs={{0,1},{1,0},{2,3},{3,2},{4,5},{5,4},{6,7},{7,6},{8,9},{9,8},{10,11... | collective-permute-start | bytes 983048 | tf_op jit(solution)/shard_map/tokens1/ppermute | solution.py:542
  137.4 8.8 %collective-permute-start.39 = (bf16[4,288,128]{2,1,0:T(8,128)(2,1)S(1)}, bf16[4,288,128]{2,1,0:T(8,128)(2,1)S(1)}, u32[]{:S(2)}, u32[]{:S(2)}) collective-permute-start(bf16[4,288,128]{2,1,0:T(8,128)(2,1)S(1)} %join_kernel.18.refs_4_.refs_0_), channel_id=1, source_target_pairs={{0,8},{1,9},{2,10},{3,11},{4,12},{5,13},{6,14},{7,15},{8,0},{9,1},... | collective-permute-start | bytes 884744 | tf_op jit(solution)/shard_map/columns8/ppermute | solution.py:542
  (33 other events, 157.8 us)

commit v2 on v1

--- a/solution.py
+++ b/solution.py
@@ -14,9 +14,10 @@
 bf = jnp.bfloat16
 f32 = jnp.float32
 TILE = 384
+WIDE = 256
 AXES = ("wide", "narrow")
 MIB = 1 << 20
-COSTS = {25: 10000000000, 31: 20000000000, 20: 6000000000, 12: 30000000000, 19: 30000000000, 35: 30000000000, 27: 30000000000, 5: 10000000000, 16: 3000000000, 21: 6000000000, 28: 3000000000, 23: 30000000000, 29: 15000000000}
+COSTS = {31: 20000000000, 20: 6000000000, 12: 30000000000, 19: 30000000000, 35: 20000000000, 27: 30000000000, 5: 10000000000, 16: 3000000000, 21: 10000000000, 28: 6000000000, 23: 30000000000, 29: 6000000000, 32: 30000000000, 26: 10000000000, 10: 3000000000, 8: 20000000000, 38: 10000000000}
 
 
 def dot(a, b):
@@ -111,34 +112,32 @@
     index = lax.axis_index("wide") * count + lax.axis_index("narrow")
     out = jnp.int32(0)
     for m in masks:
-        out = out * 2 + (index // m) % 2
+        out = out * 2 + ((index // m) % 2 if m else 0)
     return out
 
 
 def prepare_kernel(count, rows, bias, cot, whz, wrs, *refs):
     cots, (own, mine, short) = refs[:count - 1], refs[count - 1:count + 2]
-    wide_cots, half, shortcut, sems = refs[count + 2:]
+    wide_cots, shortcut, offsets, sems = refs[count + 2:]
     narrow = lax.axis_index("narrow")
     core = lax.axis_index("wide") % 2
-    width, dim = half.shape[1], shortcut.shape[1]
+    width, dim = mine.shape[1], shortcut.shape[1]
 
     def tokens(r):
         return cot.at[:, pl.ds(pl.multiple_of((narrow ^ r) * rows, 128), rows)]
 
     copies = [
-        pltpu.make_async_copy(whz.at[:, pl.ds(pl.multiple_of(core * width, 128), width)], half, sems.at[0]),
+        pltpu.make_async_copy(bias, offsets, sems.at[0]),
         pltpu.make_async_copy(wrs, shortcut, sems.at[1]),
-        pltpu.make_async_copy(tokens(0), own, sems.at[2]),
-    ] + [pltpu.make_async_copy(tokens(r), wide_cots.at[r - 1], sems.at[2 + r]) for r in range(1, count)]
+        pltpu.make_async_copy(whz.at[:, pl.ds(pl.multiple_of(core * width, 128), width)], mine, sems.at[2]),
+        pltpu.make_async_copy(tokens(0), own, sems.at[3]),
+    ] + [pltpu.make_async_copy(tokens(r), wide_cots.at[r - 1], sems.at[3 + r]) for r in range(1, count)]
     for c in copies:
         c.start()
     for c in copies[:2]:
         c.wait()
     short[:, :dim] = shortcut[...]
-    short[:, dim:] = dot_tn(bias[...].astype(f32)[None, :].astype(bf), jnp.ones((1, 128), bf)).astype(bf)
-    mine[:, :width] = half[...]
-    part = (dim + 128) // 2
-    mine[:, width:] = short[:, pl.ds(pl.multiple_of(core * part, 128), part)]
+    short[:, dim:] = dot_tn(offsets[...].astype(f32)[None, :].astype(bf), jnp.ones((1, 128), bf)).astype(bf)
     for c in copies[2:]:
         c.wait()
     for r in range(1, count):
@@ -179,8 +178,8 @@
     for c in copies[:3]:
         c.wait()
     acc = dot(p, wskip[...]) + bfin[...][None, :]
-    for j in range(0, wi.shape[1], TILE):
-        t = slice(j, j + TILE)
+    for j in range(0, wi.shape[1], WIDE):
+        t = slice(j, j + WIDE)
         h, d = silu_parts(dot(p, wi[:, t]) + bi[t][None, :])
         h = h.astype(bf)
         hid[:, t] = h
@@ -240,8 +239,8 @@
     n = (mid * rms(mid) * gain[...][None, :]).astype(bf)
     normed[...] = n
     acc = mid
-    for j in range(0, we.shape[1], TILE):
-        t = slice(j, j + TILE)
+    for j in range(0, we.shape[1], WIDE):
+        t = slice(j, j + WIDE)
         h, d = silu_parts(dot(n, we[:, t]))
         h = h.astype(bf)
         hid[:, t] = h
@@ -249,8 +248,8 @@
         acc = acc + dot(h, wc[t, :])
     st = acc.astype(bf)
     states[...] = st
-    for j in range(0, wri.shape[1], TILE):
-        t = slice(j, j + TILE)
+    for j in range(0, wri.shape[1], WIDE):
+        t = slice(j, j + WIDE)
         h, d = silu_parts(dot(st, wri[:, t]) + bri[t][None, :])
         hidh[:, t] = h.astype(bf)
         dh[:, t] = d.astype(bf)
@@ -262,7 +261,7 @@
     ("yqxp", [("inner", 0), ("inner", 1), ("inner", 2), ("up", 2), ("vector", 0)]),
 ]
 TOKEN_PARTS = [
-    ("xypq", [("final", 0), ("final", 1), ("final", 2), ("small", 0)]),
+    ("xpyq", [("final", 0), ("final", 1), ("final", 2), ("small", 0)]),
     ("yxpq", [("attention", 0), ("attention", 1), ("attention", 2), ("merge", 0), ("merge", 1), ("merge", 2)]),
 ]
 SLAB_ROWS = {"merge": 16, "vector": 16, "small": 16}
@@ -330,7 +329,7 @@
         def put(c, v):
             core, *others = index_bits(c ^ me, 4)
             at = core
-            for axis in HEAD_ORDER:
+            for axis in HEAD_ORDER.replace("d", "yx").replace("z", "qp"):
                 at = at * 2 + (r % 2 if axis == "x" else others.pop(0))
             scr[at] = v
 
@@ -352,45 +351,42 @@
 
 
 def head_kernel(count, *refs):
-    dh, sigma, wri = refs[:3]
-    refs = refs[3:]
+    dh, sigma = refs[:2]
+    refs = refs[2:]
     cots, refs = refs[:count], refs[count:]
     whz, refs = refs[0], refs[1:]
     far, refs = refs[:2 * (count - 1)], refs[2 * (count - 1):]
-    short, refs = refs[0], refs[1:]
-    gstates, gpre, sums = refs[:3]
-    mats, shorts = refs[3:2 + count], refs[2 + count:1 + 2 * count]
-    width = wri.shape[1]
-    dim = wri.shape[0]
-    half, part = width // 2, (dim + 128) // 2
+    gpre, sums = refs[:2]
+    gs, mats = refs[2:2 + count], refs[2 + count:]
+    width = dh.shape[1]
+    half = width // 2
     core = lax.axis_index("wide") % 2
     for r in range(count - 1):
         for k, c in enumerate((core, 1 - core)):
-            mats[r][:, pl.ds(pl.multiple_of(c * half, 128), half)] = far[2 * r + k][:, :half]
-            shorts[r][:, pl.ds(pl.multiple_of(c * part, 128), part)] = far[2 * r + k][:, half:]
+            mats[r][:, pl.ds(pl.multiple_of(c * half, 128), half)] = far[2 * r + k][...]
     mats = [whz] + list(mats)
-    shorts = [short] + list(shorts)
     grads = [(c[...].astype(f32) * sigma[...]).astype(bf).T for c in cots]
-    for j in range(0, width, TILE):
-        t = slice(j, j + TILE)
+    for o, g in zip(gs, grads):
+        o[...] = g
+    for j in range(0, width, WIDE):
+        t = slice(j, j + WIDE)
         acc = dot(grads[0], mats[0][:, t])
         for r in range(1, count):
             acc = acc + dot(grads[r], mats[r][:, t])
         gp = (acc * dh[:, t].astype(f32)).astype(bf)
         gpre[:, t] = gp
         sums[:, t] = jnp.sum(gp.astype(f32), axis=0, keepdims=True)
+
+
+def ffn_back_kernel(count, masks, states, gpre, sums, wri, hid, dhid, normed, middle, wc, we, gain, *refs):
+    gs, shorts, refs = refs[:count], refs[count:2 * count], refs[2 * count:]
+    gmiddle, keep, send, *scrs, tmp = refs
+    mes = [me_of(m, count) for m in masks]
+    where = layout(FFN_PARTS)
     acc = dot_nt(gpre[...], wri[...])
     for r in range(count):
-        acc = acc + dot(grads[r], shorts[r][:, :dim])
-    gstates[...] = acc.astype(bf)
-
-
-def ffn_back_kernel(count, masks, gstates, states, gpre, sums, hid, dhid, normed, middle, wc, we, gain,
-                    gmiddle, keep, send, *scrs):
-    *scrs, tmp = scrs
-    mes = [me_of(m, count) for m in masks]
-    where = layout(FFN_PARTS)
-    g = gstates[...]
+        acc = acc + dot(gs[r][...], shorts[r][:, :wri.shape[0]])
+    g = acc.astype(bf)
     nt = normed[...].T
     acc = None
     for j in range(4):
@@ -458,7 +454,7 @@
 
 def tokens_back_kernel(count, masks, patch, gembed, hid, dhid, patches, wfin, wskip, wi, gain_one, *refs):
     n = len(masks)
-    earlier, (gscaled, keep, send), scrs, tmp = refs[:n], refs[n:n + 3], refs[n + 3:2 * n + 3], refs[-1]
+    earlier, (gpatches, keep, send), scrs, tmp = refs[:n], refs[n:n + 3], refs[n + 3:2 * n + 3], refs[-1]
     mes = [me_of(m, count) for m in masks]
     where = layout(TOKEN_PARTS)
     g = gembed[...]
@@ -487,20 +483,11 @@
         scrs[p][b ^ mes[p], at:at + 16, :] = tmp[16 * b:16 * b + 16].astype(bf)
     ship([((earlier if item[0] in ("attention", "merge") else scrs)[where[item][0]], where[item][1],
            SLAB_ROWS.get(item[0], 48)) for _, items in TOKEN_PARTS for item in items], keep, send)
-    series, points = gscaled.shape
-    tokens = points // patch
-    rows = series * tokens
-    lane = iota((2 * patch, points), 1) % patch
-    fold = (iota((2 * patch, points), 0) == lane).astype(f32).astype(bf)
-    own = (iota((rows, points), 1) // patch == iota((rows, points), 0) % tokens).astype(f32)
-    high = gpat.astype(bf)
-    low = (gpat - high.astype(f32)).astype(bf)
-    full = (dot(high, fold) + dot(low, fold)) * own
-    gscaled[...] = jnp.sum(full.reshape(series, tokens, points), axis=1)
+    gpatches[...] = gpat
 
 
 def forecast_kernel(count, patch, *refs):
-    samples, mask, gscaled, hid, states, sigma_row, center_row = refs[:7]
+    samples, mask, gpatches, hid, states, sigma_row, center_row = refs[:7]
     refs = refs[7:]
     mats, refs = refs[:count], refs[count:]
     short, refs = refs[:count], refs[count:]
@@ -522,7 +509,17 @@
     first, cnt, center, offset, spread, sigma = series_stats(samples[...], observed, patch)
     out_c = series_column(row_c, series)
     out_s = series_column(row_s, series)
-    og = observed * gscaled[...]
+    points = samples.shape[1]
+    per_series = points // patch
+    rows = series * per_series
+    lane = iota((2 * patch, points), 1) % patch
+    fold = (iota((2 * patch, points), 0) == lane).astype(f32).astype(bf)
+    own = (iota((rows, points), 1) // patch == iota((rows, points), 0) % per_series).astype(f32)
+    gpat = gpatches[...]
+    high = gpat.astype(bf)
+    low = (gpat - high.astype(f32)).astype(bf)
+    full = (dot(high, fold) + dot(low, fold)) * own
+    og = observed * jnp.sum(full.reshape(series, per_series, points), axis=1)
     g_center = out_c - jnp.sum(og, axis=1, keepdims=True) / sigma
     g_sigma = out_s - jnp.sum(og * offset, axis=1, keepdims=True) / (sigma * sigma)
     g_spread = jnp.where(spread > 1.0, g_sigma * 0.5 / sigma, 0.0)
@@ -559,86 +556,118 @@
     return out
 
 
-def add_kernel(parts, before, after, split, *refs):
-    n_in = 2 * (max(g for g, _ in before.values()) + 1)
-    ins, outs = refs[:n_in], refs[n_in:]
-    n = ins[0].shape[0]
-    half = n // split
-    for p, (rows, _) in enumerate(parts):
-        (g, a), (o, b) = before[p], after[p]
-        for k in range(n):
-            v = ins[2 * g][k, a:a + rows].astype(f32) + ins[2 * g + 1][k, a:a + rows].astype(f32)
-            outs[split * o + k // half][k % half, b:b + rows] = v.astype(bf)
-
-
-def join_kernel(parts, before, after, *refs):
-    n_in = 2 * (max(g for g, _ in before.values()) + 1)
-    ins, outs = refs[:n_in], refs[n_in:]
+def combos(bits):
+    out = [0]
+    for b in bits:
+        out = [o + s for o in out for s in (0, b)]
+    return out
+
+
+def starts(counts):
+    return [sum(counts[:k]) for k in range(len(counts))]
+
+
+def swaps(parts, head=False):
+    return all(order[-1] in "xypq" for _, order in parts) and not (head and parts[0][1][-1] == "x")
+
+
+def add_kernel(parts, before, came, after, split, *refs):
+    ins, outs = refs[:sum(came)], refs[sum(came):]
+    first, to = starts(came), starts(split)
     n = ins[0].shape[0]
     for p, (rows, _) in enumerate(parts):
         (g, a), (o, b) = before[p], after[p]
-        for k in range(2):
-            outs[o][n * k:n * k + n, b:b + rows] = ins[2 * g + k][:, a:a + rows]
+        step = n // split[o]
+        for k in range(n):
+            v = ins[first[g]][k, a:a + rows].astype(f32)
+            for c in range(1, came[g]):
+                v = v + ins[first[g] + c][k, a:a + rows].astype(f32)
+            outs[to[o] + k // step][k % step, b:b + rows] = v.astype(bf)
+
+
+def join_kernel(parts, before, came, after, *refs):
+    ins, outs = refs[:sum(came)], refs[sum(came):]
+    first = starts(came)
+    for p, (rows, _) in enumerate(parts):
+        (g, a), (o, b) = before[p], after[p]
+        n = ins[first[g]].shape[0]
+        for k in range(came[g]):
+            outs[o][n * k:n * k + n, b:b + rows] = ins[first[g] + k][:, a:a + rows]
 
 
 class Flow:
     def __init__(self, chain, total, bits, rest, parts, keep, send, name, head=False):
         self.chain, self.total, self.bits, self.rest, self.parts = chain, total, bits, rest, parts
         self.name, self.head = name, head
-        self.whole = {p: (0, sum(r for r, _ in parts[:p])) for p in range(len(parts))}
-        self.level, self.down, self.at = 0, True, self.whole
-        self.held = [keep, self.to(send, bits["c"])]
+        self.swap = swaps(parts, head)
+        self.level, self.down = 0, True
+        self.groups = [list(range(len(parts)))]
+        self.held = [[keep, self.to(send, bits["c"][0])]]
 
     def to(self, v, mask):
         with jax.named_scope(self.name + str(mask)):
             return xor_send(v, mask, self.total)
 
-    def shapes(self, groups, n):
-        return [((n, sum(self.parts[p][0] for p in g), 128), bf) for g in groups]
-
-    def axis(self, group, level):
-        return self.parts[group[0]][1][level]
+    def rows(self, group):
+        return sum(self.parts[p][0] for p in group)
+
+    def levels(self, group):
+        return len(self.parts[group[0]][1])
+
+    def masks(self, group, gather=False):
+        bits = self.bits[self.parts[group[0]][1][self.level]]
+        return combos([b for b in bits if not (gather and self.head and b == self.bits["x"][0])])[1:]
 
     def step(self):
         (self.add if self.down else self.join)()
 
     def add(self):
-        n = self.held[0].shape[0]
-        last = self.level == 4
-        groups = grouped(self.parts, 3 if last else self.level)
-        at = places(self.parts, groups)
-        shapes = self.shapes(groups, n if last else n // 2)
-        outs = self.chain(functools.partial(add_kernel, self.parts, self.at, at, 1 if last else 2),
-                          shapes if last else [s for s in shapes for _ in range(2)], self.held, limit=4)
-        self.at = at
+        before, came = places(self.parts, self.groups), [len(h) for h in self.held]
+        n = self.held[0][0].shape[0]
+        last = self.level == self.levels([0])
         if not last:
-            self.held = [v for g, (a, b) in zip(groups, zip(outs[::2], outs[1::2]))
-                         for v in (a, self.to(b, self.bits[self.axis(g, self.level)]))]
+            self.groups = grouped(self.parts, self.level)
+            whole = self.swap and self.level + 1 == self.levels([0])
+            split = [1 if whole else 1 + len(self.masks(g)) for g in self.groups]
+        else:
+            if self.swap:
+                self.groups = grouped(self.parts, self.level - 2)
+            split = [1] * len(self.groups)
+        shapes = [((n // c, self.rows(g), 128), bf) for g, c in zip(self.groups, split) for _ in range(c)]
+        outs = self.chain(
+            functools.partial(add_kernel, self.parts, before, came, places(self.parts, self.groups), split),
+            shapes, [v for h in self.held for v in h], limit=4)
+        at = starts(split)
+        if not last:
+            self.held = [[outs[k]] + [self.to(outs[k if whole else k + 1 + i], m) for i, m in enumerate(self.masks(g))]
+                         for g, k in zip(self.groups, at)]
             self.level += 1
             return
         for m in self.rest:
             outs = [v + self.to(v, m) for v in outs]
         self.down = False
-        self.level = 3
-        self.spread(groups, outs)
-
-    def spread(self, groups, arrays):
-        if self.head and self.axis(groups[0], self.level) == "x":
+        if self.swap:
+            self.level -= 1
+        self.spread(outs)
+
+    def spread(self, arrays):
+        self.level -= 1
+        if self.level >= 0 and not self.masks(self.groups[0], True):
             self.level -= 1
         if self.level < 0:
-            self.held = [v for a in arrays for v in (a, self.to(a, self.bits["c"]))]
+            self.held = [[a, self.to(a, self.bits["c"][0])] for a in arrays]
             return
-        self.held = [v for g, a in zip(groups, arrays) for v in (a, self.to(a, self.bits[self.axis(g, self.level)]))]
+        self.held = [[a] + [self.to(a, m) for m in self.masks(g, True)] for g, a in zip(self.groups, arrays)]
 
     def join(self):
-        n = self.held[0].shape[0]
-        self.level -= 1
-        groups = grouped(self.parts, self.level) if self.level >= 0 else [list(range(len(self.parts)))]
-        at = places(self.parts, groups)
-        outs = self.chain(functools.partial(join_kernel, self.parts, self.at, at), self.shapes(groups, 2 * n),
-                          self.held, limit=4)
-        self.at = at
-        self.spread(groups, outs)
+        before, came = places(self.parts, self.groups), [len(h) for h in self.held]
+        ns = {p: self.held[g][0].shape[0] * came[g] for p, (g, _) in before.items()}
+        up = self.level - 1
+        self.groups = grouped(self.parts, up) if up >= 0 else [list(range(len(self.parts)))]
+        outs = self.chain(
+            functools.partial(join_kernel, self.parts, before, came, places(self.parts, self.groups)),
+            [((ns[g[0]], self.rows(g), 128), bf) for g in self.groups], [v for h in self.held for v in h], limit=4)
+        self.spread(outs)
 
 
 def assemble(refs, scr):
@@ -723,27 +752,34 @@
     inner = wq.shape[1]
     total = wide * count
     X, CORE, Y, Z0, Z1 = 1, count, 2 * count, 4 * count, 8 * count
-    bits = {"c": CORE, "x": X, "y": Y, "p": Z0, "q": Z1}
+    bits = {"c": [CORE], "x": [X], "y": [Y], "p": [Z0], "q": [Z1], "d": [Y, X], "z": [Z1, Z0]}
     narrow_rest = [1 << i for i in range(1, count.bit_length() - 1)]
     wide_rest = [count << i for i in range(4, wide.bit_length() - 1)]
-    ffn_masks, token_masks = ([[CORE] + [bits[a] for a in order] for order, _ in parts]
-                              for parts in (FFN_PARTS, TOKEN_PARTS))
-    column_masks = [CORE] + [bits[a] for a in HEAD_ORDER if a != "x"]
+    def block_bits(parts, head=False):
+        out = []
+        for _, order in parts:
+            own = [CORE] + [b for a in order for b in bits[a] if not (head and b == X)]
+            out.append(own[:-1] + [0] if swaps(parts, head) else own)
+        return out
+
+    ffn_masks, token_masks = block_bits(sizes(FFN_PARTS)), block_bits(sizes(TOKEN_PARTS))
+    (column_masks,) = block_bits([(cols, HEAD_ORDER)], True)
     ffn_rows, token_rows = ([r for r, _ in sizes(parts)] for parts in (FFN_PARTS, TOKEN_PARTS))
     chain = Chain()
     vmem = pltpu.VMEM
 
     whz_t, wrs_t, cot_t = whz.T, wrs.T, cotangent.T
-    packed = (width + dim + 128) // 2
     prepared = chain(
         functools.partial(prepare_kernel, count, rows),
-        [((cols, rows), bf)] * (count - 1) + [((cols, rows), f32), ((cols, packed), bf), ((cols, dim + 128), bf)],
-        [bro], raw=[cot_t, whz_t, wrs_t],
-        scratch=[vmem((max(count - 1, 1), cols, rows), f32), vmem((cols, width // 2), bf), vmem((cols, dim), bf),
-                 pltpu.SemaphoreType.DMA((count + 2,))], limit=24)
+        [((cols, rows), bf)] * (count - 1)
+        + [((cols, rows), f32), ((cols, width // 2), bf), ((cols, dim + 128), bf)],
+        [], raw=[bro, cot_t, whz_t, wrs_t],
+        scratch=[vmem((max(count - 1, 1), cols, rows), f32), vmem((cols, dim), bf), vmem((cols,), bf),
+                 pltpu.SemaphoreType.DMA((count + 3,))], limit=24)
     own_cot, mine, short = prepared[count - 1:]
     cots = [own_cot] + [xor_send(prepared[r - 1], r, total) for r in range(1, count)]
     far = [xor_send(mine, r, total) for r in range(1, count)]
+    shorts = [short] + [xor_send(short, r, total) for r in range(1, count)]
 
     weights = [wi, wfin, wskip, wq, wk, wv, wm, we, wc, wri, whz_t]
     out = chain(
@@ -785,16 +821,16 @@
     def head():
         out = chain(
             functools.partial(head_kernel, count),
-            [((rows, dim), bf), ((rows, width), bf), ((1, width), f32)] + [((cols, width), bf)] * (count - 1)
-            + [((cols, dim + 128), bf)] * (count - 1),
-            [dh, sigma, wri] + cots + [whz_t] + far_both + [short])
-        return out[0], out[1], out[2], [whz_t] + out[3:2 + count], [short] + out[2 + count:]
+            [((rows, width), bf), ((1, width), f32)] + [((rows, cols), bf)] * count
+            + [((cols, width), bf)] * (count - 1),
+            [dh, sigma] + cots + [whz_t] + far_both)
+        return out[0], out[1], out[2:2 + count], [whz_t] + out[2 + count:]
 
     def ffn_back():
         gmiddle, keep, send = chain(
             functools.partial(ffn_back_kernel, count, ffn_masks),
             [((rows, dim), bf)] + [((16, sum(ffn_rows), 128), bf)] * 2,
-            [gstates, states, gpre, sums, hid2, d2, normed2, middle, wc, we, gain_two],
+            [states, gpre, sums, wri, hid2, d2, normed2, middle, wc, we, gain_two] + gs + shorts,
             scratch=[vmem((32, n, 128), bf) for n in ffn_rows] + [vmem((16, 128), f32)])
         return gmiddle, Flow(chain, total, bits, narrow_rest + wide_rest, sizes(FFN_PARTS), keep, send, "ffn")
 
@@ -809,18 +845,18 @@
             [gqkv, gmiddle, mixed, normed1, embed, wq, wk, wv, gain_one])
 
     def tokens_back():
-        gscaled, keep, send = chain(
+        gpatches, keep, send = chain(
             functools.partial(tokens_back_kernel, count, token_masks, patch),
-            [((series, points), f32)] + [((16, sum(token_rows), 128), bf)] * 2,
+            [((rows, 2 * patch), f32)] + [((16, sum(token_rows), 128), bf)] * 2,
             [gembed, hid1, d1, patches, wfin, wskip, wi, gg1] + earlier,
             scratch=[vmem((32, n, 128), bf) for n in token_rows] + [vmem((512, 128), f32)])
-        return gscaled, Flow(chain, total, bits, narrow_rest + wide_rest, sizes(TOKEN_PARTS), keep, send, "tokens")
+        return gpatches, Flow(chain, total, bits, narrow_rest + wide_rest, sizes(TOKEN_PARTS), keep, send, "tokens")
 
     def forecast():
         out = chain(
             functools.partial(forecast_kernel, count, patch),
             [((cols, rows), f32)] + [((cols, rows), bf)] * (count - 1) + [((series, points), f32)],
-            [signal_samples, present_mask, gscaled, hidh, states, sigma, center] + mats + shorts + cots)
+            [signal_samples, present_mask, gpatches, hidh, states, sigma, center] + mats + shorts + cots)
         return [out[0]] + [xor_send(out[r], r, total) for r in range(1, count)], out[count]
 
     def place():
@@ -829,11 +865,11 @@
     def finish_columns():
         return chain(functools.partial(unpack_columns, count, column_masks),
                      [((cols, width), f32), ((cols, dim), f32), ((cols,), f32)],
-                     one.held, scratch=[vmem((16, cols, 128), bf), vmem((cols, 128), f32)], limit=24)
+                     one.held[0], scratch=[vmem((16, cols, 128), bf), vmem((cols, 128), f32)], limit=24)
 
     def finish_ffn():
         return chain(functools.partial(unpack_ffn, count, ffn_masks),
-                     [((dim, width), f32)] * 2 + [((width, dim), f32), ((width,), f32), ((dim,), f32)], two.held,
+                     [((dim, width), f32)] * 2 + [((width, dim), f32), ((width,), f32), ((dim,), f32)], two.held[0],
                      scratch=[vmem((32, sum(ffn_rows), 128), bf), vmem((16, 128), f32)], limit=24)
 
     def finish_tokens():
@@ -841,45 +877,42 @@
             functools.partial(unpack_tokens, count, token_masks),
             [((dim, inner), f32)] * 3 + [((inner, dim), f32), ((width, dim), f32), ((2 * patch, width), f32),
                                          ((2 * patch, dim), f32), ((width,), f32), ((dim,), f32), ((dim,), f32)],
-            three.held, scratch=[vmem((32, sum(token_rows), 128), bf), vmem((512, 128), f32)], limit=24)
+            three.held[0], scratch=[vmem((32, sum(token_rows), 128), bf), vmem((512, 128), f32)], limit=24)
 
     far_both = gate()
     one = columns()
-    gstates, gpre, sums, mats, shorts = head()
+    gpre, sums, gs, mats = head()
     gmiddle, two = ffn_back()
     gqkv = attend_back()
     gembed, gg1, *earlier = project_back()
     two.step()
-    gscaled, three = tokens_back()
+    gpatches, three = tokens_back()
     one.step()
+    three.step()
+    two.step()
     preds, g_series = forecast()
     three.step()
-    two.step()
-    prediction = place()
     one.step()
     three.step()
     two.step()
     three.step()
-    two.step()
-    one.step()
-    three.step()
+    prediction = place()
     one.step()
     two.step()
     three.step()
     two.step()
-    one.step()
     three.step()
     one.step()
     two.step()
-    three.step()
+    one.step()
     three.step()
     two.step()
     one.step()
+    three.step()
     two.step()
+    one.step()
+    tokens_out = finish_tokens()
     ffn_out = finish_ffn()
-    one.step()
-    three.step()
-    tokens_out = finish_tokens()
     columns_out = finish_columns()
     g_hw, g_hs, g_hb = columns_out
     g_hiw, g_up, g_down, g_hib, g_g2 = ffn_out

time: 156 us -> 149 us (0.955)
  waiting for transfers between devices: 54 us -> 42 us
  starting transfers between devices: 50.7 us -> 57.4 us
    ppermute x45 -> x44, waiting for transfers between devices: 54 us -> 42 us  [xor_send(): return lax.ppermute(v, AXES, [(i, i ^ mask) for i in range(total)])]
    ppermute x45 -> x44, starting transfers between devices: 50.7 us -> 57.4 us  [xor_send(): return lax.ppermute(v, AXES, [(i, i ^ mask) for i in range(total)])]
    pallas_call x42 -> x39, Pallas kernels: 45.4 us -> 44.3 us  [__call__(): pl.pallas_call(body, name=name, out_shape=[jax.ShapeDtypeStruct(s, d) for...]
    unnamed x24 -> x22, local copies, waits for them, and re-layouts: 4.12 us -> 3.43 us
  transfers between devices with their start and end apart: 45 -> 44, of which waited for: 24 -> 16; matrix products, arithmetic and copies ran while one was open for 0% -> 0% of each run, Pallas kernels for 21% -> 28%
where the time goes in v2:
time: 149 us; the launch traced here: 148 us
  starting transfers between devices  57.4 us (39%)
  Pallas kernels  44.3 us (30%)
  waiting for transfers between devices  42 us (28%)
  local copies, waits for them, and re-layouts  3.43 us (2%)
    ppermute x44, starting transfers between devices, xor_send(): return lax.ppermute(v, AXES, [(i, i ^ mask) for i in range(total)])  57.4 us
    pallas_call x39, Pallas kernels, __call__(): pl.pallas_call(body, name=name, out_shape=[jax.ShapeDtypeStruct(s, d) for...  44.3 us
    ppermute x44, waiting for transfers between devices, xor_send(): return lax.ppermute(v, AXES, [(i, i ^ mask) for i in range(total)])  42 us
    unnamed x22, local copies, waits for them, and re-layouts  3.43 us
  transfers between devices with their start and end apart: 44, of which 16 were waited for; matrix products, arithmetic and copies ran while one was open for 0% of the time, Pallas kernels for 28%

profile of v2, /device:TPU:0, one launch (start us, length us, event | category | flops | bytes accessed | tf_op | source)
XLA Modules:
  0.0 148.3 jit_solution(14731884642657941547)
XLA Ops:
  2.3 3.0 %collective-permute-start.1 = (bf16[288,768]{1,0:T(8,128)(2,1)S(1)}, bf16[288,768]{1,0:T(8,128)(2,1)S(1)}, u32[]{:S(2)}, u32[]{:S(2)}) collective-permute-start(bf16[288,768]{1,0:T(8,128)(2,1)S(1)} %get-tuple-element.148), channel_id=1, source_target_pairs={{0,1},{1,0},{2,3},{3,2},{4,5},{5,4},{6,7},{7,6},{8,9},{9,8},{10,11... | collective-permute-start | bytes 1327112 | tf_op jit(solution)/shard_map/ppermute | solution.py:539
  7.4 5.3 %tokens_kernel.1 = (bf16[512,32]{1,0:T(8,128)(2,1)S(1)}, bf16[512,1536]{1,0:T(8,128)(2,1)S(1)}, bf16[512,1536]{1,0:T(8,128)(2,1)S(1)}, f32[512,384]{1,0:T(8,128)...) custom-call(f32[16,512]{1,0:T(8,128)S(1)} %copy-done.1, ...), custom_call_target="tpu_custom_call" | custom-call | flops 1000 | bytes 1000 | tf_op jit(solution)/shard_map/tokens_kernel/pallas_call | solution.py:53
  14.1 3.6 %ffn_kernel.1 = (f32[512,384]{1,0:T(8,128)S(1)}, bf16[512,384]{1,0:T(8,128)(2,1)S(1)}, bf16[512,1536]{1,0:T(8,128)(2,1)S(1)}, bf16[512,1536]{1,0:T(8,128)(2,1)S(...) custom-call(f32[512,384]{1,0:T(8,128)S(1)} %get-tuple-element.135.refs_0_.refs_4_, ...), custom_call_target="tpu_custom_call" | custom-call | flops 1000 | bytes 1000 | tf_op jit(solution)/shard_map/ffn_kernel/pallas_call | solution.py:53
  17.9 4.8 %collective-permute-done.refs_4_.refs_3_.refs_12_ = bf16[288,512]{1,0:T(8,128)(2,1)S(1)} collective-permute-done((bf16[288,512]{1,0:T(8,128)(2,1)S(1)}, bf16[288,512]{1,0:T(8,128)(2,1)S(1)}, u32[]{:S(2)}, u32[]{:S(2)}) %collective-permute-start) | collective-permute-done | bytes 294944 | tf_op jit(solution)/shard_map/ppermute | solution.py:539
  22.6 2.0 %columns_kernel.1 = (bf16[16,288,128]{2,1,0:T(8,128)(2,1)S(1)}, bf16[16,288,128]{2,1,0:T(8,128)(2,1)S(1)}) custom-call(bf16[512,384]{1,0:T(8,128)(2,1)S(1)} %get-tuple-element.144.refs_0_.refs_4_, bf16[512,1536]{1,0:T(8,128)(2,1)S(1)} %get-tuple-element.150.refs_1_.refs_3_, f32[1,512]{1,0:T(1,128)S(1)} %get-tuple-element.137.refs_1_.refs_2_.refs_5_, ...), custom_call_target="tpu_custom_call" | custom-call | flops 10000000000 | bytes 1000 | tf_op jit(solution)/shard_map/columns_kernel/pallas_call | solution.py:53
  28.1 6.7 %ffn_back_kernel.1 = (bf16[512,384]{1,0:T(8,128)(2,1)S(1)}, bf16[16,448,128]{2,1,0:T(8,128)(2,1)S(1)}, bf16[16,448,128]{2,1,0:T(8,128)(2,1)S(1)}) custom-call(bf16[512,384]{1,0:T(8,128)(2,1)S(1)} %get-tuple-element.144.refs_0_.refs_4_, bf16[512,1536]{1,0:T(8,128)(2,1)S(1)} %get-tuple-element.152.refs_1_, f32[1,1536]{1,0:T(1,128)S(1)} %get-tuple-element.153.refs_2_, ...), custom_call_target="tpu_custom_call" | custom-call | flops 1000 | bytes 1000 | tf_op jit(solution)/shard_map/ffn_back_kernel/pallas_call | solution.py:53
  34.9 2.1 %attend_back_kernel.1.refs_0_ = bf16[512,1536]{1,0:T(8,128)(2,1)S(1)} custom-call(bf16[512,384]{1,0:T(8,128)(2,1)S(1)} %get-tuple-element.160.refs_0_.refs_1_, bf16[512,384]{1,0:T(8,128)(2,1)S(1)} %get-tuple-element.139.refs_2_.refs_1_, bf16[512,1536]{1,0:T(8,128)(2,1)S(1)} %get-tuple-element.136.refs_0_.refs_2_, ...), custom_call_target="tpu_custom_call" | custom-call | flops 20000000000 | bytes 1000 | tf_op jit(solution)/shard_map/attend_back_kernel/pallas_call | solution.py:53
  37.0 2.3 %project_back_kernel.1 = (bf16[512,384]{1,0:T(8,128)(2,1)S(1)}, f32[1,384]{1,0:T(1,128)S(1)}, bf16[32,160,128]{2,1,0:T(8,128)(2,1)S(1)}, bf16[32,192,128]{2,1,0:T(8,128)(2,1)S(1)}) custom-call(bf16[512,1536]{1,0:T(8,128)(2,1)S(1)} %attend_back_kernel.1.refs_0_, bf16[512,384]{1,0:T(8,128)(2,1)S(1)} %get-tuple-element.160.refs_0_.refs_1_, ...), custom_call_target="tpu_custom_call" | custom-call | flops 1000 | bytes 1000 | tf_op jit(solution)/shard_map/project_back_kernel/pallas_call | solution.py:53
  43.1 3.4 %tokens_back_kernel.1 = (f32[512,32]{1,0:T(8,128)S(1)}, bf16[16,352,128]{2,1,0:T(8,128)(2,1)S(1)}, bf16[16,352,128]{2,1,0:T(8,128)(2,1)S(1)}) custom-call(bf16[512,384]{1,0:T(8,128)(2,1)S(1)} %get-tuple-element.165.refs_0_, bf16[512,1536]{1,0:T(8,128)(2,1)S(1)} %get-tuple-element.166.refs_1_, bf16[512,1536]{1,0:T(8,128)(2,1)S(1)} %get-tuple-element.167.refs_2_, ...), custom_call_target="tpu_custom_call" | custom-call | flops 1000 | bytes 1000 | tf_op jit(solution)/shard_map/tokens_back_kernel/pallas_call | solution.py:53
  46.9 2.9 %collective-permute-done.7.refs_1_ = bf16[16,352,128]{2,1,0:T(8,128)(2,1)S(1)} collective-permute-done((bf16[16,352,128]{2,1,0:T(8,128)(2,1)S(1)}, bf16[16,352,128]{2,1,0:T(8,128)(2,1)S(1)}, u32[]{:S(2)}, u32[]{:S(2)}) %collective-permute-start.7) | collective-permute-done | bytes 1441824 | tf_op jit(solution)/shard_map/tokens2/ppermute | solution.py:539
  52.8 2.8 %collective-permute-done.5.refs_1_ = bf16[8,240,128]{2,1,0:T(8,128)(2,1)S(1)} collective-permute-done((bf16[8,240,128]{2,1,0:T(8,128)(2,1)S(1)}, bf16[8,240,128]{2,1,0:T(8,128)(2,1)S(1)}, u32[]{:S(2)}, u32[]{:S(2)}) %collective-permute-start.5) | collective-permute-done | bytes 491552 | tf_op jit(solution)/shard_map/ffn1/ppermute | solution.py:539
  55.9 2.7 %collective-permute-start.18 = (bf16[4,208,128]{2,1,0:T(8,128)(2,1)S(1)}, bf16[4,208,128]{2,1,0:T(8,128)(2,1)S(1)}, u32[]{:S(2)}, u32[]{:S(2)}) collective-permute-start(bf16[4,208,128]{2,1,0:T(8,128)(2,1)S(1)} %get-tuple-element.208), channel_id=1, source_target_pairs={{0,16},{1,17},{2,18},{3,19},{4,20},{5,21},{6,22},{7,23},{8,24},{9,... | collective-permute-start | bytes 638984 | tf_op jit(solution)/shard_map/ffn16/ppermute | solution.py:539
  59.0 2.5 %forecast_kernel.1 = (f32[288,512]{1,0:T(8,128)S(1)}, bf16[288,512]{1,0:T(8,128)(2,1)S(1)}, f32[16,512]{1,0:T(8,128)}) custom-call(f32[16,512]{1,0:T(8,128)S(1)} %copy-done.1, s32[16,512]{1,0:T(8,128)S(1)} %copy-done.2, f32[512,32]{1,0:T(8,128)S(1)} %get-tuple-element.178.refs_2_, bf16[512,1536]{1,0:T(8,128)(2,1)S(1)} %get-tuple-element.150.refs_1_.refs_3_, ...), custom_call_target="tpu_custom_call" | custom-call | flops 1000 | bytes 1000 | tf_op jit(solution)/shard_map/forecast_kernel/pallas_call | solution.py:53
  66.0 5.8 %collective-permute-done.14.refs_1_ = bf16[8,288,128]{2,1,0:T(8,128)(2,1)S(1)} collective-permute-done((bf16[8,288,128]{2,1,0:T(8,128)(2,1)S(1)}, bf16[8,288,128]{2,1,0:T(8,128)(2,1)S(1)}, u32[]{:S(2)}, u32[]{:S(2)}) %collective-permute-start.14) | collective-permute-done | bytes 589856 | tf_op jit(solution)/shard_map/columns8/ppermute | solution.py:539
  74.0 2.7 %collective-permute-start.22 = (bf16[4,288,128]{2,1,0:T(8,128)(2,1)S(1)}, bf16[4,288,128]{2,1,0:T(8,128)(2,1)S(1)}, u32[]{:S(2)}, u32[]{:S(2)}) collective-permute-start(bf16[4,288,128]{2,1,0:T(8,128)(2,1)S(1)} %get-tuple-element.213), channel_id=1, source_target_pairs={{0,16},{1,17},{2,18},{3,19},{4,20},{5,21},{6,22},{7,23},{8,24},{9,... | collective-permute-start | bytes 884744 | tf_op jit(solution)/shard_map/columns16/ppermute | solution.py:539
  82.9 3.2 %collective-permute-done.16.refs_3_ = bf16[2,192,128]{2,1,0:T(8,128)(2,1)S(1)} collective-permute-done((bf16[2,192,128]{2,1,0:T(8,128)(2,1)S(1)}, bf16[2,192,128]{2,1,0:T(8,128)(2,1)S(1)}, u32[]{:S(2)}, u32[]{:S(2)}) %collective-permute-start.16) | collective-permute-done | bytes 98336 | tf_op jit(solution)/shard_map/tokens8/ppermute | solution.py:539
  88.9 3.2 %collective-permute-done.22.refs_1_ = bf16[4,288,128]{2,1,0:T(8,128)(2,1)S(1)} collective-permute-done((bf16[4,288,128]{2,1,0:T(8,128)(2,1)S(1)}, bf16[4,288,128]{2,1,0:T(8,128)(2,1)S(1)}, u32[]{:S(2)}, u32[]{:S(2)}) %collective-permute-start.22) | collective-permute-done | bytes 294944 | tf_op jit(solution)/shard_map/columns16/ppermute | solution.py:539
  93.6 6.1 %collective-permute-start.26 = (bf16[2,208,128]{2,1,0:T(8,128)(2,1)S(1)}, bf16[2,208,128]{2,1,0:T(8,128)(2,1)S(1)}, u32[]{:S(2)}, u32[]{:S(2)}) collective-permute-start(bf16[2,208,128]{2,1,0:T(8,128)(2,1)S(1)} %get-tuple-element.215.refs_2_), channel_id=1, source_target_pairs={{0,8},{1,9},{2,10},{3,11},{4,12},{5,13},{6,14},{7,15},{8,0},{9,1},... | collective-permute-start | bytes 319496 | tf_op jit(solution)/shard_map/ffn8/ppermute | solution.py:539
  104.9 2.0 %collective-permute-start.31 = (bf16[2,240,128]{2,1,0:T(8,128)(2,1)S(1)}, bf16[2,240,128]{2,1,0:T(8,128)(2,1)S(1)}, u32[]{:S(2)}, u32[]{:S(2)}) collective-permute-start(bf16[2,240,128]{2,1,0:T(8,128)(2,1)S(1)} %get-tuple-element.223.refs_0_), channel_id=1, source_target_pairs={{0,8},{1,9},{2,10},{3,11},{4,12},{5,13},{6,14},{7,15},{8,0},{9,1},... | collective-permute-start | bytes 368648 | tf_op jit(solution)/shard_map/ffn8/ppermute | solution.py:539
  110.1 4.1 %collective-permute-start.37 = (bf16[4,208,128]{2,1,0:T(8,128)(2,1)S(1)}, bf16[4,208,128]{2,1,0:T(8,128)(2,1)S(1)}, u32[]{:S(2)}, u32[]{:S(2)}) collective-permute-start(bf16[4,208,128]{2,1,0:T(8,128)(2,1)S(1)} %get-tuple-element.224.refs_2_), channel_id=1, source_target_pairs={{0,16},{1,17},{2,18},{3,19},{4,20},{5,21},{6,22},{7,23},{8,24},{9,... | collective-permute-start | bytes 638984 | tf_op jit(solution)/shard_map/ffn16/ppermute | solution.py:539
  120.6 7.0 %collective-permute-done.37.refs_3_ = bf16[4,208,128]{2,1,0:T(8,128)(2,1)S(1)} collective-permute-done((bf16[4,208,128]{2,1,0:T(8,128)(2,1)S(1)}, bf16[4,208,128]{2,1,0:T(8,128)(2,1)S(1)}, u32[]{:S(2)}, u32[]{:S(2)}) %collective-permute-start.37) | collective-permute-done | bytes 213024 | tf_op jit(solution)/shard_map/ffn16/ppermute | solution.py:539
  130.8 7.2 %collective-permute-done.41.refs_3_ = bf16[8,208,128]{2,1,0:T(8,128)(2,1)S(1)} collective-permute-done((bf16[8,208,128]{2,1,0:T(8,128)(2,1)S(1)}, bf16[8,208,128]{2,1,0:T(8,128)(2,1)S(1)}, u32[]{:S(2)}, u32[]{:S(2)}) %collective-permute-start.41) | collective-permute-done | bytes 426016 | tf_op jit(solution)/shard_map/ffn4/ppermute | solution.py:539
  138.8 2.8 %unpack_tokens.1 = (f32[384,512]{1,0:T(8,128)}, f32[384,512]{1,0:T(8,128)}, f32[384,512]{1,0:T(8,128)}, f32[512,384]{1,0:T(8,128)}, f32[1536,384]{1,0:T(8,128)},...) custom-call(bf16[16,352,128]{2,1,0:T(8,128)(2,1)S(1)} %join_kernel.13.refs_4_.refs_0_, ...), custom_call_target="tpu_custom_call" | custom-call | flops 1000 | bytes 1000 | tf_op jit(solution)/shard_map/unpack_tokens/pallas_call | solution.py:53
  142.7 3.4 %unpack_ffn.1 = (f32[384,1536]{1,0:T(8,128)}, f32[384,1536]{1,0:T(8,128)}, f32[1536,384]{1,0:T(8,128)}, f32[1536]{0:T(1024)}, f32[384]{0:T(512)}) custom-call(bf16[16,448,128]{2,1,0:T(8,128)(2,1)S(1)} %join_kernel.14.refs_2_.refs_0_, bf16[16,448,128]{2,1,0:T(8,128)(2,1)S(1)} %collective-permute-done.42.refs_1_, f32[384]{0:T(512)S(1)} %copy-done.8), custom_call_target="tpu_custom_call" | custom-call | flops 1000 | bytes 1000 | tf_op jit(solution)/shard_map/unpack_ffn/pallas_call | solution.py:53
  (125 shorter events, 55.5 us)
Async XLA Ops:
  2.3 15.4 %collective-permute-start.1 = (bf16[288,768]{1,0:T(8,128)(2,1)S(1)}, bf16[288,768]{1,0:T(8,128)(2,1)S(1)}, u32[]{:S(2)}, u32[]{:S(2)}) collective-permute-start(bf16[288,768]{1,0:T(8,128)(2,1)S(1)} %get-tuple-element.148), channel_id=1, source_target_pairs={{0,1},{1,0},{2,3},{3,2},{4,5},{5,4},{6,7},{7,6},{8,9},{9,8},{10,11... | collective-permute-start | bytes 1327112 | tf_op jit(solution)/shard_map/ppermute | solution.py:539
  5.3 17.3 %collective-permute-start = (bf16[288,512]{1,0:T(8,128)(2,1)S(1)}, bf16[288,512]{1,0:T(8,128)(2,1)S(1)}, u32[]{:S(2)}, u32[]{:S(2)}) collective-permute-start(bf16[288,512]{1,0:T(8,128)(2,1)S(1)} %get-tuple-element.134.refs_16_), channel_id=1, source_target_pairs={{0,1},{1,0},{2,3},{3,2},{4,5},{5,4},{6,7},{7,6},{8,9},{9,8},{10,11... | collective-permute-start | bytes 884744 | tf_op jit(solution)/shard_map/ppermute | solution.py:539
  5.4 22.7 %collective-permute-start.3 = (bf16[288,512]{1,0:T(8,128)(2,1)S(1)}, bf16[288,512]{1,0:T(8,128)(2,1)S(1)}, u32[]{:S(2)}, u32[]{:S(2)}) collective-permute-start(bf16[288,512]{1,0:T(8,128)(2,1)S(1)} %get-tuple-element.159.refs_13_.refs_9_), channel_id=1, source_target_pairs={{0,1},{1,0},{2,3},{3,2},{4,5},{5,4},{6,7},{7,6},{8,9},{9,8},{10,11... | collective-permute-start | bytes 884744 | tf_op jit(solution)/shard_map/ppermute | solution.py:539
  24.7 22.0 %collective-permute-start.8 = (bf16[16,288,128]{2,1,0:T(8,128)(2,1)S(1)}, bf16[16,288,128]{2,1,0:T(8,128)(2,1)S(1)}, u32[]{:S(2)}, u32[]{:S(2)}) collective-permute-start(bf16[16,288,128]{2,1,0:T(8,128)(2,1)S(1)} %get-tuple-element.186), channel_id=1, source_target_pairs={{0,2},{1,3},{2,0},{3,1},{4,6},{5,7},{6,4},{7,5},{8,10},{9,11},{10,... | collective-permute-start | bytes 3538952 | tf_op jit(solution)/shard_map/columns2/ppermute | solution.py:539
  39.8 13.1 %collective-permute-start.6 = (bf16[8,208,128]{2,1,0:T(8,128)(2,1)S(1)}, bf16[8,208,128]{2,1,0:T(8,128)(2,1)S(1)}, u32[]{:S(2)}, u32[]{:S(2)}) collective-permute-start(bf16[8,208,128]{2,1,0:T(8,128)(2,1)S(1)} %get-tuple-element.183), channel_id=1, source_target_pairs={{0,4},{1,5},{2,6},{3,7},{4,0},{5,1},{6,2},{7,3},{8,12},{9,13},{10,... | collective-permute-start | bytes 1277960 | tf_op jit(solution)/shard_map/ffn4/ppermute | solution.py:539
  41.6 14.1 %collective-permute-start.5 = (bf16[8,240,128]{2,1,0:T(8,128)(2,1)S(1)}, bf16[8,240,128]{2,1,0:T(8,128)(2,1)S(1)}, u32[]{:S(2)}, u32[]{:S(2)}) collective-permute-start(bf16[8,240,128]{2,1,0:T(8,128)(2,1)S(1)} %get-tuple-element.182), channel_id=1, source_target_pairs={{0,1},{1,0},{2,3},{3,2},{4,5},{5,4},{6,7},{7,6},{8,9},{9,8},{10,11... | collective-permute-start | bytes 1474568 | tf_op jit(solution)/shard_map/ffn1/ppermute | solution.py:539
  50.2 12.0 %collective-permute-start.11 = (bf16[8,192,128]{2,1,0:T(8,128)(2,1)S(1)}, bf16[8,192,128]{2,1,0:T(8,128)(2,1)S(1)}, u32[]{:S(2)}, u32[]{:S(2)}) collective-permute-start(bf16[8,192,128]{2,1,0:T(8,128)(2,1)S(1)} %get-tuple-element.194), channel_id=1, source_target_pairs={{0,4},{1,5},{2,6},{3,7},{4,0},{5,1},{6,2},{7,3},{8,12},{9,13},{10,... | collective-permute-start | bytes 1179656 | tf_op jit(solution)/shard_map/tokens4/ppermute | solution.py:539
  50.7 11.2 %collective-permute-start.10 = (bf16[8,160,128]{2,1,0:T(8,128)(2,1)S(1)}, bf16[8,160,128]{2,1,0:T(8,128)(2,1)S(1)}, u32[]{:S(2)}, u32[]{:S(2)}) collective-permute-start(bf16[8,160,128]{2,1,0:T(8,128)(2,1)S(1)} %get-tuple-element.192), channel_id=1, source_target_pairs={{0,1},{1,0},{2,3},{3,2},{4,5},{5,4},{6,7},{7,6},{8,9},{9,8},{10,11... | collective-permute-start | bytes 983048 | tf_op jit(solution)/shard_map/tokens1/ppermute | solution.py:539
  51.0 20.8 %collective-permute-start.14 = (bf16[8,288,128]{2,1,0:T(8,128)(2,1)S(1)}, bf16[8,288,128]{2,1,0:T(8,128)(2,1)S(1)}, u32[]{:S(2)}, u32[]{:S(2)}) collective-permute-start(bf16[8,288,128]{2,1,0:T(8,128)(2,1)S(1)} %get-tuple-element.200), channel_id=1, source_target_pairs={{0,8},{1,9},{2,10},{3,11},{4,12},{5,13},{6,14},{7,15},{8,0},{9,1},... | collective-permute-start | bytes 1769480 | tf_op jit(solution)/shard_map/columns8/ppermute | solution.py:539
  55.9 22.5 %collective-permute-start.18 = (bf16[4,208,128]{2,1,0:T(8,128)(2,1)S(1)}, bf16[4,208,128]{2,1,0:T(8,128)(2,1)S(1)}, u32[]{:S(2)}, u32[]{:S(2)}) collective-permute-start(bf16[4,208,128]{2,1,0:T(8,128)(2,1)S(1)} %get-tuple-element.208), channel_id=1, source_target_pairs={{0,16},{1,17},{2,18},{3,19},{4,20},{5,21},{6,22},{7,23},{8,24},{9,... | collective-permute-start | bytes 638984 | tf_op jit(solution)/shard_map/ffn16/ppermute | solution.py:539
  58.5 21.5 %collective-permute-start.17 = (bf16[4,240,128]{2,1,0:T(8,128)(2,1)S(1)}, bf16[4,240,128]{2,1,0:T(8,128)(2,1)S(1)}, u32[]{:S(2)}, u32[]{:S(2)}) collective-permute-start(bf16[4,240,128]{2,1,0:T(8,128)(2,1)S(1)} %get-tuple-element.207), channel_id=1, source_target_pairs={{0,4},{1,5},{2,6},{3,7},{4,0},{5,1},{6,2},{7,3},{8,12},{9,13},{10,... | collective-permute-start | bytes 737288 | tf_op jit(solution)/shard_map/ffn4/ppermute | solution.py:539
  63.1 13.6 %collective-permute-start.13 = (bf16[4,192,128]{2,1,0:T(8,128)(2,1)S(1)}, bf16[4,192,128]{2,1,0:T(8,128)(2,1)S(1)}, u32[]{:S(2)}, u32[]{:S(2)}) collective-permute-start(bf16[4,192,128]{2,1,0:T(8,128)(2,1)S(1)} %get-tuple-element.199), channel_id=1, source_target_pairs={{0,1},{1,0},{2,3},{3,2},{4,5},{5,4},{6,7},{7,6},{8,9},{9,8},{10,11... | collective-permute-start | bytes 589832 | tf_op jit(solution)/shard_map/tokens1/ppermute | solution.py:539
  71.8 16.0 %collective-permute-start.9 = (bf16[288,512]{1,0:T(8,128)(2,1)S(1)}, bf16[288,512]{1,0:T(8,128)(2,1)S(1)}, u32[]{:S(2)}, u32[]{:S(2)}) collective-permute-start(bf16[288,512]{1,0:T(8,128)(2,1)S(1)} %get-tuple-element.191), channel_id=1, source_target_pairs={{0,1},{1,0},{2,3},{3,2},{4,5},{5,4},{6,7},{7,6},{8,9},{9,8},{10,11... | collective-permute-start | bytes 884744 | tf_op jit(solution)/shard_map/ppermute | solution.py:539
  74.0 18.1 %collective-permute-start.22 = (bf16[4,288,128]{2,1,0:T(8,128)(2,1)S(1)}, bf16[4,288,128]{2,1,0:T(8,128)(2,1)S(1)}, u32[]{:S(2)}, u32[]{:S(2)}) collective-permute-start(bf16[4,288,128]{2,1,0:T(8,128)(2,1)S(1)} %get-tuple-element.213), channel_id=1, source_target_pairs={{0,16},{1,17},{2,18},{3,19},{4,20},{5,21},{6,22},{7,23},{8,24},{9,... | collective-permute-start | bytes 884744 | tf_op jit(solution)/shard_map/columns16/ppermute | solution.py:539
  80.1 13.3 %collective-permute-start.21 = (bf16[2,208,128]{2,1,0:T(8,128)(2,1)S(1)}, bf16[2,208,128]{2,1,0:T(8,128)(2,1)S(1)}, u32[]{:S(2)}, u32[]{:S(2)}) collective-permute-start(bf16[2,208,128]{2,1,0:T(8,128)(2,1)S(1)} %get-tuple-element.212), channel_id=1, source_target_pairs={{0,1},{1,0},{2,3},{3,2},{4,5},{5,4},{6,7},{7,6},{8,9},{9,8},{10,11... | collective-permute-start | bytes 319496 | tf_op jit(solution)/shard_map/ffn1/ppermute | solution.py:539
  81.7 11.8 %collective-permute-start.20 = (bf16[2,240,128]{2,1,0:T(8,128)(2,1)S(1)}, bf16[2,240,128]{2,1,0:T(8,128)(2,1)S(1)}, u32[]{:S(2)}, u32[]{:S(2)}) collective-permute-start(bf16[2,240,128]{2,1,0:T(8,128)(2,1)S(1)} %get-tuple-element.211), channel_id=1, source_target_pairs={{0,8},{1,9},{2,10},{3,11},{4,12},{5,13},{6,14},{7,15},{8,0},{9,1},... | collective-permute-start | bytes 368648 | tf_op jit(solution)/shard_map/ffn8/ppermute | solution.py:539
  86.2 13.6 %collective-permute-start.19 = (bf16[2,352,128]{2,1,0:T(8,128)(2,1)S(1)}, bf16[2,352,128]{2,1,0:T(8,128)(2,1)S(1)}, u32[]{:S(2)}, u32[]{:S(2)}) collective-permute-start(bf16[2,352,128]{2,1,0:T(8,128)(2,1)S(1)} %add_kernel.23.refs_2_.refs_0_), channel_id=1, source_target_pairs={{0,16},{1,17},{2,18},{3,19},{4,20},{5,21},{6,22},{7,23},{8,24},{9,... | collective-permute-start | bytes 540680 | tf_op jit(solution)/shard_map/tokens16/ppermute | solution.py:539
  107.0 10.8 %collective-permute-start.27 = (bf16[4,160,128]{2,1,0:T(8,128)(2,1)S(1)}, bf16[4,160,128]{2,1,0:T(8,128)(2,1)S(1)}, u32[]{:S(2)}, u32[]{:S(2)}) collective-permute-start(bf16[4,160,128]{2,1,0:T(8,128)(2,1)S(1)} %get-tuple-element.220.refs_2_.refs_0_), channel_id=1, source_target_pairs={{0,8},{1,9},{2,10},{3,11},{4,12},{5,13},{6,14},{7,15},{8,0},{9,1},... | collective-permute-start | bytes 491528 | tf_op jit(solution)/shard_map/tokens8/ppermute | solution.py:539
  110.1 17.5 %collective-permute-start.37 = (bf16[4,208,128]{2,1,0:T(8,128)(2,1)S(1)}, bf16[4,208,128]{2,1,0:T(8,128)(2,1)S(1)}, u32[]{:S(2)}, u32[]{:S(2)}) collective-permute-start(bf16[4,208,128]{2,1,0:T(8,128)(2,1)S(1)} %get-tuple-element.224.refs_2_), channel_id=1, source_target_pairs={{0,16},{1,17},{2,18},{3,19},{4,20},{5,21},{6,22},{7,23},{8,24},{9,... | collective-permute-start | bytes 638984 | tf_op jit(solution)/shard_map/ffn16/ppermute | solution.py:539
  114.3 13.3 %collective-permute-start.36 = (bf16[4,240,128]{2,1,0:T(8,128)(2,1)S(1)}, bf16[4,240,128]{2,1,0:T(8,128)(2,1)S(1)}, u32[]{:S(2)}, u32[]{:S(2)}) collective-permute-start(bf16[4,240,128]{2,1,0:T(8,128)(2,1)S(1)} %get-tuple-element.227.refs_0_), channel_id=1, source_target_pairs={{0,4},{1,5},{2,6},{3,7},{4,0},{5,1},{6,2},{7,3},{8,12},{9,13},{10,... | collective-permute-start | bytes 737288 | tf_op jit(solution)/shard_map/ffn4/ppermute | solution.py:539
  115.8 13.4 %collective-permute-start.35 = (bf16[2,288,128]{2,1,0:T(8,128)(2,1)S(1)}, bf16[2,288,128]{2,1,0:T(8,128)(2,1)S(1)}, u32[]{:S(2)}, u32[]{:S(2)}) collective-permute-start(bf16[2,288,128]{2,1,0:T(8,128)(2,1)S(1)} %add_kernel.29.refs_4_.refs_0_), channel_id=1, source_target_pairs={{0,16},{1,17},{2,18},{3,19},{4,20},{5,21},{6,22},{7,23},{8,24},{9,... | collective-permute-start | bytes 442376 | tf_op jit(solution)/shard_map/columns16/ppermute | solution.py:539
  117.8 11.4 %collective-permute-start.33 = (bf16[8,160,128]{2,1,0:T(8,128)(2,1)S(1)}, bf16[8,160,128]{2,1,0:T(8,128)(2,1)S(1)}, u32[]{:S(2)}, u32[]{:S(2)}) collective-permute-start(bf16[8,160,128]{2,1,0:T(8,128)(2,1)S(1)} %get-tuple-element.225.refs_4_.refs_0_), channel_id=1, source_target_pairs={{0,1},{1,0},{2,3},{3,2},{4,5},{5,4},{6,7},{7,6},{8,9},{9,8},{10,11... | collective-permute-start | bytes 983048 | tf_op jit(solution)/shard_map/tokens1/ppermute | solution.py:539
  119.8 10.8 %collective-permute-start.34 = (bf16[8,192,128]{2,1,0:T(8,128)(2,1)S(1)}, bf16[8,192,128]{2,1,0:T(8,128)(2,1)S(1)}, u32[]{:S(2)}, u32[]{:S(2)}) collective-permute-start(bf16[8,192,128]{2,1,0:T(8,128)(2,1)S(1)} %get-tuple-element.226.refs_2_), channel_id=1, source_target_pairs={{0,4},{1,5},{2,6},{3,7},{4,0},{5,1},{6,2},{7,3},{8,12},{9,13},{10,... | collective-permute-start | bytes 1179656 | tf_op jit(solution)/shard_map/tokens4/ppermute | solution.py:539
  127.7 10.4 %collective-permute-start.41 = (bf16[8,208,128]{2,1,0:T(8,128)(2,1)S(1)}, bf16[8,208,128]{2,1,0:T(8,128)(2,1)S(1)}, u32[]{:S(2)}, u32[]{:S(2)}) collective-permute-start(bf16[8,208,128]{2,1,0:T(8,128)(2,1)S(1)} %get-tuple-element.228.refs_2_), channel_id=1, source_target_pairs={{0,4},{1,5},{2,6},{3,7},{4,0},{5,1},{6,2},{7,3},{8,12},{9,13},{10,... | collective-permute-start | bytes 1277960 | tf_op jit(solution)/shard_map/ffn4/ppermute | solution.py:539
  (31 other events, 183.1 us)

commit v3 on v2

--- a/solution.py
+++ b/solution.py
@@ -17,7 +17,7 @@
 WIDE = 256
 AXES = ("wide", "narrow")
 MIB = 1 << 20
-COSTS = {31: 20000000000, 20: 6000000000, 12: 30000000000, 19: 30000000000, 35: 20000000000, 27: 30000000000, 5: 10000000000, 16: 3000000000, 21: 10000000000, 28: 6000000000, 23: 30000000000, 29: 6000000000, 32: 30000000000, 26: 10000000000, 10: 3000000000, 8: 20000000000, 38: 10000000000}
+COSTS = {31: 15000000000, 20: 6000000000, 12: 30000000000, 19: 30000000000, 35: 20000000000, 27: 30000000000, 5: 10000000000, 21: 10000000000, 28: 6000000000, 23: 30000000000, 29: 6000000000, 32: 30000000000, 26: 10000000000, 10: 3000000000, 8: 20000000000, 38: 10000000000}
 
 
 def dot(a, b):
@@ -116,29 +116,23 @@
     return out
 
 
-def prepare_kernel(count, rows, bias, cot, whz, wrs, *refs):
-    cots, (own, mine, short) = refs[:count - 1], refs[count - 1:count + 2]
-    wide_cots, shortcut, offsets, sems = refs[count + 2:]
+def prepare_kernel(count, rows, cot, whz, *refs):
+    cots, (own, mine) = refs[:count - 1], refs[count - 1:count + 1]
+    wide_cots, sems = refs[count + 1:]
     narrow = lax.axis_index("narrow")
     core = lax.axis_index("wide") % 2
-    width, dim = mine.shape[1], shortcut.shape[1]
+    width = mine.shape[1]
 
     def tokens(r):
         return cot.at[:, pl.ds(pl.multiple_of((narrow ^ r) * rows, 128), rows)]
 
     copies = [
-        pltpu.make_async_copy(bias, offsets, sems.at[0]),
-        pltpu.make_async_copy(wrs, shortcut, sems.at[1]),
-        pltpu.make_async_copy(whz.at[:, pl.ds(pl.multiple_of(core * width, 128), width)], mine, sems.at[2]),
-        pltpu.make_async_copy(tokens(0), own, sems.at[3]),
-    ] + [pltpu.make_async_copy(tokens(r), wide_cots.at[r - 1], sems.at[3 + r]) for r in range(1, count)]
+        pltpu.make_async_copy(whz.at[:, pl.ds(pl.multiple_of(core * width, 128), width)], mine, sems.at[0]),
+        pltpu.make_async_copy(tokens(0), own, sems.at[1]),
+    ] + [pltpu.make_async_copy(tokens(r), wide_cots.at[r - 1], sems.at[1 + r]) for r in range(1, count)]
     for c in copies:
         c.start()
-    for c in copies[:2]:
-        c.wait()
-    short[:, :dim] = shortcut[...]
-    short[:, dim:] = dot_tn(offsets[...].astype(f32)[None, :].astype(bf), jnp.ones((1, 128), bf)).astype(bf)
-    for c in copies[2:]:
+    for c in copies:
         c.wait()
     for r in range(1, count):
         cots[r - 1][...] = wide_cots[r - 1].astype(bf)
@@ -491,15 +485,17 @@
     refs = refs[7:]
     mats, refs = refs[:count], refs[count:]
     short, refs = refs[:count], refs[count:]
+    offsets, refs = refs[:count], refs[count:]
     cots, refs = refs[:count], refs[count:]
     preds, series_grad = refs[:count], refs[count]
     sg = sigma_row[...]
     ct = center_row[...]
     st = states[...]
-    dim = st.shape[1]
+    ones = jnp.ones((1, 128), bf)
     row_c, row_s = 0.0, 0.0
     for r in range(count):
-        raw = dot_nt(mats[r][...], hid[...]) + dot_nt(short[r][:, :dim], st) + short[r][:, dim:dim + 1].astype(f32)
+        added_bias = dot_tn(offsets[r][...].astype(f32)[None, :].astype(bf), ones)[:, :1]
+        raw = dot_nt(mats[r][...], hid[...]) + dot_nt(short[r][...], st) + added_bias
         preds[r][...] = (raw * sg + ct).astype(preds[r].dtype)
         c = cots[r][...].astype(f32)
         row_c = row_c + jnp.sum(c, axis=0, keepdims=True)
@@ -772,14 +768,14 @@
     prepared = chain(
         functools.partial(prepare_kernel, count, rows),
         [((cols, rows), bf)] * (count - 1)
-        + [((cols, rows), f32), ((cols, width // 2), bf), ((cols, dim + 128), bf)],
-        [], raw=[bro, cot_t, whz_t, wrs_t],
-        scratch=[vmem((max(count - 1, 1), cols, rows), f32), vmem((cols, dim), bf), vmem((cols,), bf),
-                 pltpu.SemaphoreType.DMA((count + 3,))], limit=24)
-    own_cot, mine, short = prepared[count - 1:]
+        + [((cols, rows), f32), ((cols, width // 2), bf)],
+        [], raw=[cot_t, whz_t],
+        scratch=[vmem((max(count - 1, 1), cols, rows), f32), pltpu.SemaphoreType.DMA((count + 1,))], limit=24)
+    own_cot, mine = prepared[count - 1:]
     cots = [own_cot] + [xor_send(prepared[r - 1], r, total) for r in range(1, count)]
     far = [xor_send(mine, r, total) for r in range(1, count)]
-    shorts = [short] + [xor_send(short, r, total) for r in range(1, count)]
+    shorts = [wrs_t] + [xor_send(wrs_t, r, total) for r in range(1, count)]
+    offsets = [bro] + [xor_send(bro, r, total) for r in range(1, count)]
 
     weights = [wi, wfin, wskip, wq, wk, wv, wm, we, wc, wri, whz_t]
     out = chain(
@@ -856,7 +852,7 @@
         out = chain(
             functools.partial(forecast_kernel, count, patch),
             [((cols, rows), f32)] + [((cols, rows), bf)] * (count - 1) + [((series, points), f32)],
-            [signal_samples, present_mask, gpatches, hidh, states, sigma, center] + mats + shorts + cots)
+            [signal_samples, present_mask, gpatches, hidh, states, sigma, center] + mats + shorts + offsets + cots)
         return [out[0]] + [xor_send(out[r], r, total) for r in range(1, count)], out[count]
 
     def place():
@@ -890,19 +886,19 @@
     one.step()
     three.step()
     two.step()
-    preds, g_series = forecast()
     three.step()
     one.step()
     three.step()
+    preds, g_series = forecast()
     two.step()
     three.step()
+    one.step()
+    two.step()
     prediction = place()
+    three.step()
     one.step()
     two.step()
     three.step()
-    two.step()
-    three.step()
-    one.step()
     two.step()
     one.step()
     three.step()

time: 149 us -> 147 us (0.987)
  starting transfers between devices: 57.4 us -> 52.8 us
  waiting for transfers between devices: 42 us -> 45.1 us
    ppermute x44 -> x45, starting transfers between devices: 57.4 us -> 52.8 us  [xor_send(): return lax.ppermute(v, AXES, [(i, i ^ mask) for i in range(total)])]
    ppermute x44 -> x45, waiting for transfers between devices: 42 us -> 45.1 us  [xor_send(): return lax.ppermute(v, AXES, [(i, i ^ mask) for i in range(total)])]
    unnamed x22 -> x26, local copies, waits for them, and re-layouts: 3.43 us -> 3.43 us
  transfers between devices with their start and end apart: 44 -> 45, of which waited for: 16 -> 14; matrix products, arithmetic and copies ran while one was open for 0% -> 0% of each run, Pallas kernels for 28% -> 28%
where the time goes in v3:
time: 147 us
  starting transfers between devices  52.8 us (36%)
  waiting for transfers between devices  45.1 us (31%)
  Pallas kernels  44.4 us (30%)
  local copies, waits for them, and re-layouts  3.43 us (2%)
    ppermute x45, starting transfers between devices, xor_send(): return lax.ppermute(v, AXES, [(i, i ^ mask) for i in range(total)])  52.8 us
    ppermute x45, waiting for transfers between devices, xor_send(): return lax.ppermute(v, AXES, [(i, i ^ mask) for i in range(total)])  45.1 us
    pallas_call x39, Pallas kernels, __call__(): pl.pallas_call(body, name=name, out_shape=[jax.ShapeDtypeStruct(s, d) for...  44.4 us
    unnamed x26, local copies, waits for them, and re-layouts  3.43 us
  transfers between devices with their start and end apart: 45, of which 14 were waited for; matrix products, arithmetic and copies ran while one was open for 0% of the time, Pallas kernels for 28%

profile of v3, /device:TPU:0, one launch (start us, length us, event | category | flops | bytes accessed | tf_op | source)
XLA Modules:
  0.0 146.8 jit_solution(3036941138322981985)
XLA Ops:
  2.3 3.0 %collective-permute-start.1 = (bf16[288,768]{1,0:T(8,128)(2,1)S(1)}, bf16[288,768]{1,0:T(8,128)(2,1)S(1)}, u32[]{:S(2)}, u32[]{:S(2)}) collective-permute-start(bf16[288,768]{1,0:T(8,128)(2,1)S(1)} %get-tuple-element.147), channel_id=1, source_target_pairs={{0,1},{1,0},{2,3},{3,2},{4,5},{5,4},{6,7},{7,6},{8,9},{9,8},{10,11... | collective-permute-start | bytes 1327112 | tf_op jit(solution)/shard_map/ppermute | solution.py:535
  7.3 5.3 %tokens_kernel.1 = (bf16[512,32]{1,0:T(8,128)(2,1)S(1)}, bf16[512,1536]{1,0:T(8,128)(2,1)S(1)}, bf16[512,1536]{1,0:T(8,128)(2,1)S(1)}, f32[512,384]{1,0:T(8,128)...) custom-call(f32[16,512]{1,0:T(8,128)S(1)} %copy-done.2, ...), custom_call_target="tpu_custom_call" | custom-call | flops 1000 | bytes 1000 | tf_op jit(solution)/shard_map/tokens_kernel/pallas_call | solution.py:53
  14.1 3.6 %ffn_kernel.1 = (f32[512,384]{1,0:T(8,128)S(1)}, bf16[512,384]{1,0:T(8,128)(2,1)S(1)}, bf16[512,1536]{1,0:T(8,128)(2,1)S(1)}, bf16[512,1536]{1,0:T(8,128)(2,1)S(...) custom-call(f32[512,384]{1,0:T(8,128)S(1)} %get-tuple-element.134.refs_0_.refs_4_, ...), custom_call_target="tpu_custom_call" | custom-call | flops 1000 | bytes 1000 | tf_op jit(solution)/shard_map/ffn_kernel/pallas_call | solution.py:53
  17.8 4.8 %collective-permute-done.refs_4_.refs_3_.refs_14_ = bf16[288,512]{1,0:T(8,128)(2,1)S(1)} collective-permute-done((bf16[288,512]{1,0:T(8,128)(2,1)S(1)}, bf16[288,512]{1,0:T(8,128)(2,1)S(1)}, u32[]{:S(2)}, u32[]{:S(2)}) %collective-permute-start) | collective-permute-done | bytes 294944 | tf_op jit(solution)/shard_map/ppermute | solution.py:535
  26.7 6.7 %ffn_back_kernel.1 = (bf16[512,384]{1,0:T(8,128)(2,1)S(1)}, bf16[16,448,128]{2,1,0:T(8,128)(2,1)S(1)}, bf16[16,448,128]{2,1,0:T(8,128)(2,1)S(1)}) custom-call(bf16[512,384]{1,0:T(8,128)(2,1)S(1)} %get-tuple-element.143.refs_0_.refs_4_, bf16[512,1536]{1,0:T(8,128)(2,1)S(1)} %get-tuple-element.151.refs_1_, f32[1,1536]{1,0:T(1,128)S(1)} %get-tuple-element.152.refs_2_, ...), custom_call_target="tpu_custom_call" | custom-call | flops 1000 | bytes 1000 | tf_op jit(solution)/shard_map/ffn_back_kernel/pallas_call | solution.py:53
  34.0 2.1 %attend_back_kernel.1.refs_0_ = bf16[512,1536]{1,0:T(8,128)(2,1)S(1)} custom-call(bf16[512,384]{1,0:T(8,128)(2,1)S(1)} %get-tuple-element.158.refs_0_.refs_1_, bf16[512,384]{1,0:T(8,128)(2,1)S(1)} %get-tuple-element.138.refs_2_.refs_1_, bf16[512,1536]{1,0:T(8,128)(2,1)S(1)} %get-tuple-element.135.refs_0_.refs_2_, ...), custom_call_target="tpu_custom_call" | custom-call | flops 20000000000 | bytes 1000 | tf_op jit(solution)/shard_map/attend_back_kernel/pallas_call | solution.py:53
  36.1 2.3 %project_back_kernel.1 = (bf16[512,384]{1,0:T(8,128)(2,1)S(1)}, f32[1,384]{1,0:T(1,128)S(1)}, bf16[32,160,128]{2,1,0:T(8,128)(2,1)S(1)}, bf16[32,192,128]{2,1,0:T(8,128)(2,1)S(1)}) custom-call(bf16[512,1536]{1,0:T(8,128)(2,1)S(1)} %attend_back_kernel.1.refs_0_, bf16[512,384]{1,0:T(8,128)(2,1)S(1)} %get-tuple-element.158.refs_0_.refs_1_, ...), custom_call_target="tpu_custom_call" | custom-call | flops 1000 | bytes 1000 | tf_op jit(solution)/shard_map/project_back_kernel/pallas_call | solution.py:53
  38.8 3.5 %tokens_back_kernel.1 = (f32[512,32]{1,0:T(8,128)S(1)}, bf16[16,352,128]{2,1,0:T(8,128)(2,1)S(1)}, bf16[16,352,128]{2,1,0:T(8,128)(2,1)S(1)}) custom-call(bf16[512,384]{1,0:T(8,128)(2,1)S(1)} %get-tuple-element.163.refs_0_, bf16[512,1536]{1,0:T(8,128)(2,1)S(1)} %get-tuple-element.164.refs_1_, bf16[512,1536]{1,0:T(8,128)(2,1)S(1)} %get-tuple-element.165.refs_2_, ...), custom_call_target="tpu_custom_call" | custom-call | flops 1000 | bytes 1000 | tf_op jit(solution)/shard_map/tokens_back_kernel/pallas_call | solution.py:53
  42.4 2.1 %collective-permute-start.10 = (bf16[8,240,128]{2,1,0:T(8,128)(2,1)S(1)}, bf16[8,240,128]{2,1,0:T(8,128)(2,1)S(1)}, u32[]{:S(2)}, u32[]{:S(2)}) collective-permute-start(bf16[8,240,128]{2,1,0:T(8,128)(2,1)S(1)} %get-tuple-element.188), channel_id=1, source_target_pairs={{0,1},{1,0},{2,3},{3,2},{4,5},{5,4},{6,7},{7,6},{8,9},{9,8},{10,11... | collective-permute-start | bytes 1474568 | tf_op jit(solution)/shard_map/ffn1/ppermute | solution.py:535
  49.5 7.6 %collective-permute-done.11.refs_3_ = bf16[8,208,128]{2,1,0:T(8,128)(2,1)S(1)} collective-permute-done((bf16[8,208,128]{2,1,0:T(8,128)(2,1)S(1)}, bf16[8,208,128]{2,1,0:T(8,128)(2,1)S(1)}, u32[]{:S(2)}, u32[]{:S(2)}) %collective-permute-start.11) | collective-permute-done | bytes 426016 | tf_op jit(solution)/shard_map/ffn4/ppermute | solution.py:535
  59.0 2.6 %collective-permute-start.17 = (bf16[4,208,128]{2,1,0:T(8,128)(2,1)S(1)}, bf16[4,208,128]{2,1,0:T(8,128)(2,1)S(1)}, u32[]{:S(2)}, u32[]{:S(2)}) collective-permute-start(bf16[4,208,128]{2,1,0:T(8,128)(2,1)S(1)} %get-tuple-element.202), channel_id=1, source_target_pairs={{0,16},{1,17},{2,18},{3,19},{4,20},{5,21},{6,22},{7,23},{8,24},{9,... | collective-permute-start | bytes 638984 | tf_op jit(solution)/shard_map/ffn16/ppermute | solution.py:535
  63.3 2.3 %collective-permute-done.9.refs_3_ = bf16[8,192,128]{2,1,0:T(8,128)(2,1)S(1)} collective-permute-done((bf16[8,192,128]{2,1,0:T(8,128)(2,1)S(1)}, bf16[8,192,128]{2,1,0:T(8,128)(2,1)S(1)}, u32[]{:S(2)}, u32[]{:S(2)}) %collective-permute-start.9) | collective-permute-done | bytes 393248 | tf_op jit(solution)/shard_map/tokens4/ppermute | solution.py:535
  69.6 3.5 %collective-permute-done.12.refs_1_ = bf16[4,160,128]{2,1,0:T(8,128)(2,1)S(1)} collective-permute-done((bf16[4,160,128]{2,1,0:T(8,128)(2,1)S(1)}, bf16[4,160,128]{2,1,0:T(8,128)(2,1)S(1)}, u32[]{:S(2)}, u32[]{:S(2)}) %collective-permute-start.12) | collective-permute-done | bytes 163872 | tf_op jit(solution)/shard_map/tokens8/ppermute | solution.py:535
  73.1 2.5 %collective-permute-start.20 = (bf16[4,288,128]{2,1,0:T(8,128)(2,1)S(1)}, bf16[4,288,128]{2,1,0:T(8,128)(2,1)S(1)}, u32[]{:S(2)}, u32[]{:S(2)}) collective-permute-start(bf16[4,288,128]{2,1,0:T(8,128)(2,1)S(1)} %get-tuple-element.208), channel_id=1, source_target_pairs={{0,16},{1,17},{2,18},{3,19},{4,20},{5,21},{6,22},{7,23},{8,24},{9,... | collective-permute-start | bytes 884744 | tf_op jit(solution)/shard_map/columns16/ppermute | solution.py:535
  75.6 2.5 %collective-permute-start.22 = (bf16[2,192,128]{2,1,0:T(8,128)(2,1)S(1)}, bf16[2,192,128]{2,1,0:T(8,128)(2,1)S(1)}, u32[]{:S(2)}, u32[]{:S(2)}) collective-permute-start(bf16[2,192,128]{2,1,0:T(8,128)(2,1)S(1)} %get-tuple-element.211), channel_id=1, source_target_pairs={{0,8},{1,9},{2,10},{3,11},{4,12},{5,13},{6,14},{7,15},{8,0},{9,1},... | collective-permute-start | bytes 294920 | tf_op jit(solution)/shard_map/tokens8/ppermute | solution.py:535
  78.7 2.6 %forecast_kernel.1 = (f32[288,512]{1,0:T(8,128)S(1)}, bf16[288,512]{1,0:T(8,128)(2,1)S(1)}, f32[16,512]{1,0:T(8,128)}) custom-call(f32[16,512]{1,0:T(8,128)S(1)} %copy-done.2, s32[16,512]{1,0:T(8,128)S(1)} %copy-done.3, f32[512,32]{1,0:T(8,128)S(1)} %get-tuple-element.176.refs_2_, bf16[512,1536]{1,0:T(8,128)(2,1)S(1)} %get-tuple-element.149.refs_1_.refs_3_, ...), custom_call_target="tpu_custom_call" | custom-call | flops 1000 | bytes 1000 | tf_op jit(solution)/shard_map/forecast_kernel/pallas_call | solution.py:53
  85.1 3.0 %collective-permute-start.23 = (bf16[2,352,128]{2,1,0:T(8,128)(2,1)S(1)}, bf16[2,352,128]{2,1,0:T(8,128)(2,1)S(1)}, u32[]{:S(2)}, u32[]{:S(2)}) collective-permute-start(bf16[2,352,128]{2,1,0:T(8,128)(2,1)S(1)} %add_kernel.23.refs_2_.refs_0_), channel_id=1, source_target_pairs={{0,16},{1,17},{2,18},{3,19},{4,20},{5,21},{6,22},{7,23},{8,24},{9,... | collective-permute-start | bytes 540680 | tf_op jit(solution)/shard_map/tokens16/ppermute | solution.py:535
  88.1 6.0 %collective-permute-done.20.refs_1_ = bf16[4,288,128]{2,1,0:T(8,128)(2,1)S(1)} collective-permute-done((bf16[4,288,128]{2,1,0:T(8,128)(2,1)S(1)}, bf16[4,288,128]{2,1,0:T(8,128)(2,1)S(1)}, u32[]{:S(2)}, u32[]{:S(2)}) %collective-permute-start.20) | collective-permute-done | bytes 294944 | tf_op jit(solution)/shard_map/columns16/ppermute | solution.py:535
  94.2 2.3 %collective-permute-start.28 = (bf16[2,288,128]{2,1,0:T(8,128)(2,1)S(1)}, bf16[2,288,128]{2,1,0:T(8,128)(2,1)S(1)}, u32[]{:S(2)}, u32[]{:S(2)}) collective-permute-start(bf16[2,288,128]{2,1,0:T(8,128)(2,1)S(1)} %get-tuple-element.217), channel_id=1, source_target_pairs={{0,1},{1,0},{2,3},{3,2},{4,5},{5,4},{6,7},{7,6},{8,9},{9,8},{10,11... | collective-permute-start | bytes 442376 | tf_op jit(solution)/shard_map/columns1/ppermute | solution.py:535
  96.7 3.5 %collective-permute-start.27 = (bf16[2,208,128]{2,1,0:T(8,128)(2,1)S(1)}, bf16[2,208,128]{2,1,0:T(8,128)(2,1)S(1)}, u32[]{:S(2)}, u32[]{:S(2)}) collective-permute-start(bf16[2,208,128]{2,1,0:T(8,128)(2,1)S(1)} %get-tuple-element.213.refs_2_), channel_id=1, source_target_pairs={{0,8},{1,9},{2,10},{3,11},{4,12},{5,13},{6,14},{7,15},{8,0},{9,1},... | collective-permute-start | bytes 319496 | tf_op jit(solution)/shard_map/ffn8/ppermute | solution.py:535
  118.0 8.3 %collective-permute-done.38.refs_3_ = bf16[4,208,128]{2,1,0:T(8,128)(2,1)S(1)} collective-permute-done((bf16[4,208,128]{2,1,0:T(8,128)(2,1)S(1)}, bf16[4,208,128]{2,1,0:T(8,128)(2,1)S(1)}, u32[]{:S(2)}, u32[]{:S(2)}) %collective-permute-start.38) | collective-permute-done | bytes 213024 | tf_op jit(solution)/shard_map/ffn16/ppermute | solution.py:535
  129.3 6.0 %collective-permute-done.42.refs_3_ = bf16[8,208,128]{2,1,0:T(8,128)(2,1)S(1)} collective-permute-done((bf16[8,208,128]{2,1,0:T(8,128)(2,1)S(1)}, bf16[8,208,128]{2,1,0:T(8,128)(2,1)S(1)}, u32[]{:S(2)}, u32[]{:S(2)}) %collective-permute-start.42) | collective-permute-done | bytes 426016 | tf_op jit(solution)/shard_map/ffn4/ppermute | solution.py:535
  137.3 2.8 %unpack_tokens.1 = (f32[384,512]{1,0:T(8,128)}, f32[384,512]{1,0:T(8,128)}, f32[384,512]{1,0:T(8,128)}, f32[512,384]{1,0:T(8,128)}, f32[1536,384]{1,0:T(8,128)},...) custom-call(bf16[16,352,128]{2,1,0:T(8,128)(2,1)S(1)} %join_kernel.13.refs_4_.refs_0_, ...), custom_call_target="tpu_custom_call" | custom-call | flops 1000 | bytes 1000 | tf_op jit(solution)/shard_map/unpack_tokens/pallas_call | solution.py:53
  141.2 3.4 %unpack_ffn.1 = (f32[384,1536]{1,0:T(8,128)}, f32[384,1536]{1,0:T(8,128)}, f32[1536,384]{1,0:T(8,128)}, f32[1536]{0:T(1024)}, f32[384]{0:T(512)}) custom-call(bf16[16,448,128]{2,1,0:T(8,128)(2,1)S(1)} %join_kernel.14.refs_2_.refs_0_, bf16[16,448,128]{2,1,0:T(8,128)(2,1)S(1)} %collective-permute-done.43.refs_1_, f32[384]{0:T(512)S(1)} %copy-done.9), custom_call_target="tpu_custom_call" | custom-call | flops 1000 | bytes 1000 | tf_op jit(solution)/shard_map/unpack_ffn/pallas_call | solution.py:53
  (131 shorter events, 53.7 us)
Async XLA Ops:
  2.3 15.4 %collective-permute-start.1 = (bf16[288,768]{1,0:T(8,128)(2,1)S(1)}, bf16[288,768]{1,0:T(8,128)(2,1)S(1)}, u32[]{:S(2)}, u32[]{:S(2)}) collective-permute-start(bf16[288,768]{1,0:T(8,128)(2,1)S(1)} %get-tuple-element.147), channel_id=1, source_target_pairs={{0,1},{1,0},{2,3},{3,2},{4,5},{5,4},{6,7},{7,6},{8,9},{9,8},{10,11... | collective-permute-start | bytes 1327112 | tf_op jit(solution)/shard_map/ppermute | solution.py:535
  5.3 17.3 %collective-permute-start = (bf16[288,512]{1,0:T(8,128)(2,1)S(1)}, bf16[288,512]{1,0:T(8,128)(2,1)S(1)}, u32[]{:S(2)}, u32[]{:S(2)}) collective-permute-start(bf16[288,512]{1,0:T(8,128)(2,1)S(1)} %get-tuple-element.133.refs_16_), channel_id=1, source_target_pairs={{0,1},{1,0},{2,3},{3,2},{4,5},{5,4},{6,7},{7,6},{8,9},{9,8},{10,11... | collective-permute-start | bytes 884744 | tf_op jit(solution)/shard_map/ppermute | solution.py:535
  5.4 21.3 %collective-permute-start.3 = (bf16[288,384]{1,0:T(8,128)(2,1)S(1)}, bf16[288,384]{1,0:T(8,128)(2,1)S(1)}, u32[]{:S(2)}, u32[]{:S(2)}) collective-permute-start(bf16[288,384]{1,0:T(8,128)(2,1)S(1)} %bitcast.7), channel_id=1, source_target_pairs={{0,1},{1,0},{2,3},{3,2},{4,5},{5,4},{6,7},{7,6},{8,9},{9,8},{10,11... | collective-permute-start | bytes 663560 | tf_op jit(solution)/shard_map/ppermute | solution.py:535
  24.6 21.4 %collective-permute-start.7 = (bf16[16,288,128]{2,1,0:T(8,128)(2,1)S(1)}, bf16[16,288,128]{2,1,0:T(8,128)(2,1)S(1)}, u32[]{:S(2)}, u32[]{:S(2)}) collective-permute-start(bf16[16,288,128]{2,1,0:T(8,128)(2,1)S(1)} %get-tuple-element.181), channel_id=1, source_target_pairs={{0,2},{1,3},{2,0},{3,1},{4,6},{5,7},{6,4},{7,5},{8,10},{9,11},{10,... | collective-permute-start | bytes 3538952 | tf_op jit(solution)/shard_map/columns2/ppermute | solution.py:535
  42.4 14.8 %collective-permute-start.10 = (bf16[8,240,128]{2,1,0:T(8,128)(2,1)S(1)}, bf16[8,240,128]{2,1,0:T(8,128)(2,1)S(1)}, u32[]{:S(2)}, u32[]{:S(2)}) collective-permute-start(bf16[8,240,128]{2,1,0:T(8,128)(2,1)S(1)} %get-tuple-element.188), channel_id=1, source_target_pairs={{0,1},{1,0},{2,3},{3,2},{4,5},{5,4},{6,7},{7,6},{8,9},{9,8},{10,11... | collective-permute-start | bytes 1474568 | tf_op jit(solution)/shard_map/ffn1/ppermute | solution.py:535
  44.5 12.7 %collective-permute-start.11 = (bf16[8,208,128]{2,1,0:T(8,128)(2,1)S(1)}, bf16[8,208,128]{2,1,0:T(8,128)(2,1)S(1)}, u32[]{:S(2)}, u32[]{:S(2)}) collective-permute-start(bf16[8,208,128]{2,1,0:T(8,128)(2,1)S(1)} %get-tuple-element.189), channel_id=1, source_target_pairs={{0,4},{1,5},{2,6},{3,7},{4,0},{5,1},{6,2},{7,3},{8,12},{9,13},{10,... | collective-permute-start | bytes 1277960 | tf_op jit(solution)/shard_map/ffn4/ppermute | solution.py:535
  46.3 21.6 %collective-permute-start.14 = (bf16[8,288,128]{2,1,0:T(8,128)(2,1)S(1)}, bf16[8,288,128]{2,1,0:T(8,128)(2,1)S(1)}, u32[]{:S(2)}, u32[]{:S(2)}) collective-permute-start(bf16[8,288,128]{2,1,0:T(8,128)(2,1)S(1)} %get-tuple-element.195), channel_id=1, source_target_pairs={{0,8},{1,9},{2,10},{3,11},{4,12},{5,13},{6,14},{7,15},{8,0},{9,1},... | collective-permute-start | bytes 1769480 | tf_op jit(solution)/shard_map/columns8/ppermute | solution.py:535
  48.3 17.3 %collective-permute-start.9 = (bf16[8,192,128]{2,1,0:T(8,128)(2,1)S(1)}, bf16[8,192,128]{2,1,0:T(8,128)(2,1)S(1)}, u32[]{:S(2)}, u32[]{:S(2)}) collective-permute-start(bf16[8,192,128]{2,1,0:T(8,128)(2,1)S(1)} %get-tuple-element.186), channel_id=1, source_target_pairs={{0,4},{1,5},{2,6},{3,7},{4,0},{5,1},{6,2},{7,3},{8,12},{9,13},{10,... | collective-permute-start | bytes 1179656 | tf_op jit(solution)/shard_map/tokens4/ppermute | solution.py:535
  48.9 14.4 %collective-permute-start.8 = (bf16[8,160,128]{2,1,0:T(8,128)(2,1)S(1)}, bf16[8,160,128]{2,1,0:T(8,128)(2,1)S(1)}, u32[]{:S(2)}, u32[]{:S(2)}) collective-permute-start(bf16[8,160,128]{2,1,0:T(8,128)(2,1)S(1)} %get-tuple-element.184), channel_id=1, source_target_pairs={{0,1},{1,0},{2,3},{3,2},{4,5},{5,4},{6,7},{7,6},{8,9},{9,8},{10,11... | collective-permute-start | bytes 983048 | tf_op jit(solution)/shard_map/tokens1/ppermute | solution.py:535
  57.4 23.9 %collective-permute-start.16 = (bf16[4,240,128]{2,1,0:T(8,128)(2,1)S(1)}, bf16[4,240,128]{2,1,0:T(8,128)(2,1)S(1)}, u32[]{:S(2)}, u32[]{:S(2)}) collective-permute-start(bf16[4,240,128]{2,1,0:T(8,128)(2,1)S(1)} %get-tuple-element.201), channel_id=1, source_target_pairs={{0,4},{1,5},{2,6},{3,7},{4,0},{5,1},{6,2},{7,3},{8,12},{9,13},{10,... | collective-permute-start | bytes 737288 | tf_op jit(solution)/shard_map/ffn4/ppermute | solution.py:535
  59.0 22.3 %collective-permute-start.17 = (bf16[4,208,128]{2,1,0:T(8,128)(2,1)S(1)}, bf16[4,208,128]{2,1,0:T(8,128)(2,1)S(1)}, u32[]{:S(2)}, u32[]{:S(2)}) collective-permute-start(bf16[4,208,128]{2,1,0:T(8,128)(2,1)S(1)} %get-tuple-element.202), channel_id=1, source_target_pairs={{0,16},{1,17},{2,18},{3,19},{4,20},{5,21},{6,22},{7,23},{8,24},{9,... | collective-permute-start | bytes 638984 | tf_op jit(solution)/shard_map/ffn16/ppermute | solution.py:535
  67.9 10.3 %collective-permute-start.5 = (bf16[288]{0:T(512)(128)(2,1)S(1)}, bf16[288]{0:T(512)(128)(2,1)S(1)}, u32[]{:S(2)}, u32[]{:S(2)}) collective-permute-start(bf16[288]{0:T(512)(128)(2,1)S(1)} %copy-done.10), channel_id=1, source_target_pairs={{0,1},{1,0},{2,3},{3,2},{4,5},{5,4},{6,7},{7,6},{8,9},{9,8},{10,11... | collective-permute-start | bytes 1736 | tf_op jit(solution)/shard_map/ppermute | solution.py:535
  73.1 21.0 %collective-permute-start.20 = (bf16[4,288,128]{2,1,0:T(8,128)(2,1)S(1)}, bf16[4,288,128]{2,1,0:T(8,128)(2,1)S(1)}, u32[]{:S(2)}, u32[]{:S(2)}) collective-permute-start(bf16[4,288,128]{2,1,0:T(8,128)(2,1)S(1)} %get-tuple-element.208), channel_id=1, source_target_pairs={{0,16},{1,17},{2,18},{3,19},{4,20},{5,21},{6,22},{7,23},{8,24},{9,... | collective-permute-start | bytes 884744 | tf_op jit(solution)/shard_map/columns16/ppermute | solution.py:535
  82.1 14.4 %collective-permute-start.18 = (bf16[2,240,128]{2,1,0:T(8,128)(2,1)S(1)}, bf16[2,240,128]{2,1,0:T(8,128)(2,1)S(1)}, u32[]{:S(2)}, u32[]{:S(2)}) collective-permute-start(bf16[2,240,128]{2,1,0:T(8,128)(2,1)S(1)} %get-tuple-element.205), channel_id=1, source_target_pairs={{0,8},{1,9},{2,10},{3,11},{4,12},{5,13},{6,14},{7,15},{8,0},{9,1},... | collective-permute-start | bytes 368648 | tf_op jit(solution)/shard_map/ffn8/ppermute | solution.py:535
  82.3 14.2 %collective-permute-start.19 = (bf16[2,208,128]{2,1,0:T(8,128)(2,1)S(1)}, bf16[2,208,128]{2,1,0:T(8,128)(2,1)S(1)}, u32[]{:S(2)}, u32[]{:S(2)}) collective-permute-start(bf16[2,208,128]{2,1,0:T(8,128)(2,1)S(1)} %get-tuple-element.207), channel_id=1, source_target_pairs={{0,1},{1,0},{2,3},{3,2},{4,5},{5,4},{6,7},{7,6},{8,9},{9,8},{10,11... | collective-permute-start | bytes 319496 | tf_op jit(solution)/shard_map/ffn1/ppermute | solution.py:535
  83.7 16.5 %collective-permute-start.15 = (bf16[288,512]{1,0:T(8,128)(2,1)S(1)}, bf16[288,512]{1,0:T(8,128)(2,1)S(1)}, u32[]{:S(2)}, u32[]{:S(2)}) collective-permute-start(bf16[288,512]{1,0:T(8,128)(2,1)S(1)} %get-tuple-element.199), channel_id=1, source_target_pairs={{0,1},{1,0},{2,3},{3,2},{4,5},{5,4},{6,7},{7,6},{8,9},{9,8},{10,11... | collective-permute-start | bytes 884744 | tf_op jit(solution)/shard_map/ppermute | solution.py:535
  85.1 16.1 %collective-permute-start.23 = (bf16[2,352,128]{2,1,0:T(8,128)(2,1)S(1)}, bf16[2,352,128]{2,1,0:T(8,128)(2,1)S(1)}, u32[]{:S(2)}, u32[]{:S(2)}) collective-permute-start(bf16[2,352,128]{2,1,0:T(8,128)(2,1)S(1)} %add_kernel.23.refs_2_.refs_0_), channel_id=1, source_target_pairs={{0,16},{1,17},{2,18},{3,19},{4,20},{5,21},{6,22},{7,23},{8,24},{9,... | collective-permute-start | bytes 540680 | tf_op jit(solution)/shard_map/tokens16/ppermute | solution.py:535
  102.8 11.0 %collective-permute-start.31 = (bf16[2,288,128]{2,1,0:T(8,128)(2,1)S(1)}, bf16[2,288,128]{2,1,0:T(8,128)(2,1)S(1)}, u32[]{:S(2)}, u32[]{:S(2)}) collective-permute-start(bf16[2,288,128]{2,1,0:T(8,128)(2,1)S(1)} %add_kernel.27.refs_4_.refs_0_), channel_id=1, source_target_pairs={{0,4},{1,5},{2,6},{3,7},{4,0},{5,1},{6,2},{7,3},{8,12},{9,13},{10,... | collective-permute-start | bytes 442376 | tf_op jit(solution)/shard_map/columns4/ppermute | solution.py:535
  111.9 14.4 %collective-permute-start.37 = (bf16[4,240,128]{2,1,0:T(8,128)(2,1)S(1)}, bf16[4,240,128]{2,1,0:T(8,128)(2,1)S(1)}, u32[]{:S(2)}, u32[]{:S(2)}) collective-permute-start(bf16[4,240,128]{2,1,0:T(8,128)(2,1)S(1)} %get-tuple-element.225.refs_0_), channel_id=1, source_target_pairs={{0,4},{1,5},{2,6},{3,7},{4,0},{5,1},{6,2},{7,3},{8,12},{9,13},{10,... | collective-permute-start | bytes 737288 | tf_op jit(solution)/shard_map/ffn4/ppermute | solution.py:535
  112.3 14.0 %collective-permute-start.38 = (bf16[4,208,128]{2,1,0:T(8,128)(2,1)S(1)}, bf16[4,208,128]{2,1,0:T(8,128)(2,1)S(1)}, u32[]{:S(2)}, u32[]{:S(2)}) collective-permute-start(bf16[4,208,128]{2,1,0:T(8,128)(2,1)S(1)} %get-tuple-element.222.refs_2_), channel_id=1, source_target_pairs={{0,16},{1,17},{2,18},{3,19},{4,20},{5,21},{6,22},{7,23},{8,24},{9,... | collective-permute-start | bytes 638984 | tf_op jit(solution)/shard_map/ffn16/ppermute | solution.py:535
  113.9 14.8 %collective-permute-start.36 = (bf16[2,288,128]{2,1,0:T(8,128)(2,1)S(1)}, bf16[2,288,128]{2,1,0:T(8,128)(2,1)S(1)}, u32[]{:S(2)}, u32[]{:S(2)}) collective-permute-start(bf16[2,288,128]{2,1,0:T(8,128)(2,1)S(1)} %add_kernel.29.refs_4_.refs_0_), channel_id=1, source_target_pairs={{0,16},{1,17},{2,18},{3,19},{4,20},{5,21},{6,22},{7,23},{8,24},{9,... | collective-permute-start | bytes 442376 | tf_op jit(solution)/shard_map/columns16/ppermute | solution.py:535
  115.4 13.7 %collective-permute-start.35 = (bf16[8,192,128]{2,1,0:T(8,128)(2,1)S(1)}, bf16[8,192,128]{2,1,0:T(8,128)(2,1)S(1)}, u32[]{:S(2)}, u32[]{:S(2)}) collective-permute-start(bf16[8,192,128]{2,1,0:T(8,128)(2,1)S(1)} %get-tuple-element.224.refs_2_), channel_id=1, source_target_pairs={{0,4},{1,5},{2,6},{3,7},{4,0},{5,1},{6,2},{7,3},{8,12},{9,13},{10,... | collective-permute-start | bytes 1179656 | tf_op jit(solution)/shard_map/tokens4/ppermute | solution.py:535
  117.2 11.9 %collective-permute-start.34 = (bf16[8,160,128]{2,1,0:T(8,128)(2,1)S(1)}, bf16[8,160,128]{2,1,0:T(8,128)(2,1)S(1)}, u32[]{:S(2)}, u32[]{:S(2)}) collective-permute-start(bf16[8,160,128]{2,1,0:T(8,128)(2,1)S(1)} %get-tuple-element.223.refs_4_.refs_0_), channel_id=1, source_target_pairs={{0,1},{1,0},{2,3},{3,2},{4,5},{5,4},{6,7},{7,6},{8,9},{9,8},{10,11... | collective-permute-start | bytes 983048 | tf_op jit(solution)/shard_map/tokens1/ppermute | solution.py:535
  126.4 10.2 %collective-permute-start.41 = (bf16[8,240,128]{2,1,0:T(8,128)(2,1)S(1)}, bf16[8,240,128]{2,1,0:T(8,128)(2,1)S(1)}, u32[]{:S(2)}, u32[]{:S(2)}) collective-permute-start(bf16[8,240,128]{2,1,0:T(8,128)(2,1)S(1)} %get-tuple-element.227.refs_0_), channel_id=1, source_target_pairs={{0,1},{1,0},{2,3},{3,2},{4,5},{5,4},{6,7},{7,6},{8,9},{9,8},{10,11... | collective-permute-start | bytes 1474568 | tf_op jit(solution)/shard_map/ffn1/ppermute | solution.py:535
  (34 other events, 201.5 us)

commit v4 on v3

--- a/solution.py
+++ b/solution.py
@@ -327,9 +327,9 @@
                 at = at * 2 + (r % 2 if axis == "x" else others.pop(0))
             scr[at] = v
 
-        for j in range(0, width, TILE):
-            v = dot(turned, hidh[:, j:j + TILE]).astype(bf)
-            for i in range(TILE // 128):
+        for j in range(0, width, 2 * WIDE):
+            v = dot(turned, hidh[:, j:j + 2 * WIDE]).astype(bf)
+            for i in range(2 * WIDE // 128):
                 put(j // 128 + i, v[:, 128 * i:128 * i + 128])
         v = dot(turned, st).astype(bf)
         for i in range(st.shape[1] // 128):

time: 147 us -> 147 us (level)
  transfers between devices with their start and end apart: 45 -> 45, of which waited for: 14 -> 15; matrix products, arithmetic and copies ran while one was open for 0% -> 0% of each run, Pallas kernels for 28% -> 28%
where the time goes in v4:
time: 147 us; the launch traced here: 146 us
  starting transfers between devices  52.9 us (36%)
  waiting for transfers between devices  45.1 us (31%)
  Pallas kernels  44.1 us (30%)
  local copies, waits for them, and re-layouts  3.43 us (2%)
    ppermute x45, starting transfers between devices, xor_send(): return lax.ppermute(v, AXES, [(i, i ^ mask) for i in range(total)])  52.9 us
    ppermute x45, waiting for transfers between devices, xor_send(): return lax.ppermute(v, AXES, [(i, i ^ mask) for i in range(total)])  45.1 us
    pallas_call x39, Pallas kernels, __call__(): pl.pallas_call(body, name=name, out_shape=[jax.ShapeDtypeStruct(s, d) for...  44.1 us
    unnamed x26, local copies, waits for them, and re-layouts  3.43 us
  transfers between devices with their start and end apart: 45, of which 15 were waited for; matrix products, arithmetic and copies ran while one was open for 0% of the time, Pallas kernels for 28%

profile of v4, /device:TPU:0, one launch (start us, length us, event | category | flops | bytes accessed | tf_op | source)
XLA Modules:
  0.0 146.5 jit_solution(18399896920080808263)
XLA Ops:
  2.3 3.0 %collective-permute-start.1 = (bf16[288,768]{1,0:T(8,128)(2,1)S(1)}, bf16[288,768]{1,0:T(8,128)(2,1)S(1)}, u32[]{:S(2)}, u32[]{:S(2)}) collective-permute-start(bf16[288,768]{1,0:T(8,128)(2,1)S(1)} %get-tuple-element.147), channel_id=1, source_target_pairs={{0,1},{1,0},{2,3},{3,2},{4,5},{5,4},{6,7},{7,6},{8,9},{9,8},{10,11... | collective-permute-start | bytes 1327112 | tf_op jit(solution)/shard_map/ppermute | solution.py:535
  7.3 5.3 %tokens_kernel.1 = (bf16[512,32]{1,0:T(8,128)(2,1)S(1)}, bf16[512,1536]{1,0:T(8,128)(2,1)S(1)}, bf16[512,1536]{1,0:T(8,128)(2,1)S(1)}, f32[512,384]{1,0:T(8,128)...) custom-call(f32[16,512]{1,0:T(8,128)S(1)} %copy-done.2, ...), custom_call_target="tpu_custom_call" | custom-call | flops 1000 | bytes 1000 | tf_op jit(solution)/shard_map/tokens_kernel/pallas_call | solution.py:53
  14.1 3.6 %ffn_kernel.1 = (f32[512,384]{1,0:T(8,128)S(1)}, bf16[512,384]{1,0:T(8,128)(2,1)S(1)}, bf16[512,1536]{1,0:T(8,128)(2,1)S(1)}, bf16[512,1536]{1,0:T(8,128)(2,1)S(...) custom-call(f32[512,384]{1,0:T(8,128)S(1)} %get-tuple-element.134.refs_0_.refs_4_, ...), custom_call_target="tpu_custom_call" | custom-call | flops 1000 | bytes 1000 | tf_op jit(solution)/shard_map/ffn_kernel/pallas_call | solution.py:53
  17.8 4.8 %collective-permute-done.refs_4_.refs_3_.refs_14_ = bf16[288,512]{1,0:T(8,128)(2,1)S(1)} collective-permute-done((bf16[288,512]{1,0:T(8,128)(2,1)S(1)}, bf16[288,512]{1,0:T(8,128)(2,1)S(1)}, u32[]{:S(2)}, u32[]{:S(2)}) %collective-permute-start) | collective-permute-done | bytes 294944 | tf_op jit(solution)/shard_map/ppermute | solution.py:535
  26.5 6.7 %ffn_back_kernel.1 = (bf16[512,384]{1,0:T(8,128)(2,1)S(1)}, bf16[16,448,128]{2,1,0:T(8,128)(2,1)S(1)}, bf16[16,448,128]{2,1,0:T(8,128)(2,1)S(1)}) custom-call(bf16[512,384]{1,0:T(8,128)(2,1)S(1)} %get-tuple-element.143.refs_0_.refs_4_, bf16[512,1536]{1,0:T(8,128)(2,1)S(1)} %get-tuple-element.151.refs_1_, f32[1,1536]{1,0:T(1,128)S(1)} %get-tuple-element.152.refs_2_, ...), custom_call_target="tpu_custom_call" | custom-call | flops 1000 | bytes 1000 | tf_op jit(solution)/shard_map/ffn_back_kernel/pallas_call | solution.py:53
  33.8 2.1 %attend_back_kernel.1.refs_0_ = bf16[512,1536]{1,0:T(8,128)(2,1)S(1)} custom-call(bf16[512,384]{1,0:T(8,128)(2,1)S(1)} %get-tuple-element.158.refs_0_.refs_1_, bf16[512,384]{1,0:T(8,128)(2,1)S(1)} %get-tuple-element.138.refs_2_.refs_1_, bf16[512,1536]{1,0:T(8,128)(2,1)S(1)} %get-tuple-element.135.refs_0_.refs_2_, ...), custom_call_target="tpu_custom_call" | custom-call | flops 20000000000 | bytes 1000 | tf_op jit(solution)/shard_map/attend_back_kernel/pallas_call | solution.py:53
  35.9 2.3 %project_back_kernel.1 = (bf16[512,384]{1,0:T(8,128)(2,1)S(1)}, f32[1,384]{1,0:T(1,128)S(1)}, bf16[32,160,128]{2,1,0:T(8,128)(2,1)S(1)}, bf16[32,192,128]{2,1,0:T(8,128)(2,1)S(1)}) custom-call(bf16[512,1536]{1,0:T(8,128)(2,1)S(1)} %attend_back_kernel.1.refs_0_, bf16[512,384]{1,0:T(8,128)(2,1)S(1)} %get-tuple-element.158.refs_0_.refs_1_, ...), custom_call_target="tpu_custom_call" | custom-call | flops 1000 | bytes 1000 | tf_op jit(solution)/shard_map/project_back_kernel/pallas_call | solution.py:53
  38.6 3.4 %tokens_back_kernel.1 = (f32[512,32]{1,0:T(8,128)S(1)}, bf16[16,352,128]{2,1,0:T(8,128)(2,1)S(1)}, bf16[16,352,128]{2,1,0:T(8,128)(2,1)S(1)}) custom-call(bf16[512,384]{1,0:T(8,128)(2,1)S(1)} %get-tuple-element.163.refs_0_, bf16[512,1536]{1,0:T(8,128)(2,1)S(1)} %get-tuple-element.164.refs_1_, bf16[512,1536]{1,0:T(8,128)(2,1)S(1)} %get-tuple-element.165.refs_2_, ...), custom_call_target="tpu_custom_call" | custom-call | flops 1000 | bytes 1000 | tf_op jit(solution)/shard_map/tokens_back_kernel/pallas_call | solution.py:53
  49.3 7.6 %collective-permute-done.11.refs_3_ = bf16[8,208,128]{2,1,0:T(8,128)(2,1)S(1)} collective-permute-done((bf16[8,208,128]{2,1,0:T(8,128)(2,1)S(1)}, bf16[8,208,128]{2,1,0:T(8,128)(2,1)S(1)}, u32[]{:S(2)}, u32[]{:S(2)}) %collective-permute-start.11) | collective-permute-done | bytes 426016 | tf_op jit(solution)/shard_map/ffn4/ppermute | solution.py:535
  58.7 2.6 %collective-permute-start.17 = (bf16[4,208,128]{2,1,0:T(8,128)(2,1)S(1)}, bf16[4,208,128]{2,1,0:T(8,128)(2,1)S(1)}, u32[]{:S(2)}, u32[]{:S(2)}) collective-permute-start(bf16[4,208,128]{2,1,0:T(8,128)(2,1)S(1)} %get-tuple-element.202), channel_id=1, source_target_pairs={{0,16},{1,17},{2,18},{3,19},{4,20},{5,21},{6,22},{7,23},{8,24},{9,... | collective-permute-start | bytes 638984 | tf_op jit(solution)/shard_map/ffn16/ppermute | solution.py:535
  63.1 2.3 %collective-permute-done.9.refs_3_ = bf16[8,192,128]{2,1,0:T(8,128)(2,1)S(1)} collective-permute-done((bf16[8,192,128]{2,1,0:T(8,128)(2,1)S(1)}, bf16[8,192,128]{2,1,0:T(8,128)(2,1)S(1)}, u32[]{:S(2)}, u32[]{:S(2)}) %collective-permute-start.9) | collective-permute-done | bytes 393248 | tf_op jit(solution)/shard_map/tokens4/ppermute | solution.py:535
  65.6 2.1 %collective-permute-start.12 = (bf16[4,160,128]{2,1,0:T(8,128)(2,1)S(1)}, bf16[4,160,128]{2,1,0:T(8,128)(2,1)S(1)}, u32[]{:S(2)}, u32[]{:S(2)}) collective-permute-start(bf16[4,160,128]{2,1,0:T(8,128)(2,1)S(1)} %get-tuple-element.192), channel_id=1, source_target_pairs={{0,8},{1,9},{2,10},{3,11},{4,12},{5,13},{6,14},{7,15},{8,0},{9,1},... | collective-permute-start | bytes 491528 | tf_op jit(solution)/shard_map/tokens8/ppermute | solution.py:535
  69.3 3.5 %collective-permute-done.12.refs_1_ = bf16[4,160,128]{2,1,0:T(8,128)(2,1)S(1)} collective-permute-done((bf16[4,160,128]{2,1,0:T(8,128)(2,1)S(1)}, bf16[4,160,128]{2,1,0:T(8,128)(2,1)S(1)}, u32[]{:S(2)}, u32[]{:S(2)}) %collective-permute-start.12) | collective-permute-done | bytes 163872 | tf_op jit(solution)/shard_map/tokens8/ppermute | solution.py:535
  72.8 2.5 %collective-permute-start.20 = (bf16[4,288,128]{2,1,0:T(8,128)(2,1)S(1)}, bf16[4,288,128]{2,1,0:T(8,128)(2,1)S(1)}, u32[]{:S(2)}, u32[]{:S(2)}) collective-permute-start(bf16[4,288,128]{2,1,0:T(8,128)(2,1)S(1)} %get-tuple-element.208), channel_id=1, source_target_pairs={{0,16},{1,17},{2,18},{3,19},{4,20},{5,21},{6,22},{7,23},{8,24},{9,... | collective-permute-start | bytes 884744 | tf_op jit(solution)/shard_map/columns16/ppermute | solution.py:535
  75.4 2.5 %collective-permute-start.22 = (bf16[2,192,128]{2,1,0:T(8,128)(2,1)S(1)}, bf16[2,192,128]{2,1,0:T(8,128)(2,1)S(1)}, u32[]{:S(2)}, u32[]{:S(2)}) collective-permute-start(bf16[2,192,128]{2,1,0:T(8,128)(2,1)S(1)} %get-tuple-element.211), channel_id=1, source_target_pairs={{0,8},{1,9},{2,10},{3,11},{4,12},{5,13},{6,14},{7,15},{8,0},{9,1},... | collective-permute-start | bytes 294920 | tf_op jit(solution)/shard_map/tokens8/ppermute | solution.py:535
  78.5 2.5 %forecast_kernel.1 = (f32[288,512]{1,0:T(8,128)S(1)}, bf16[288,512]{1,0:T(8,128)(2,1)S(1)}, f32[16,512]{1,0:T(8,128)}) custom-call(f32[16,512]{1,0:T(8,128)S(1)} %copy-done.2, s32[16,512]{1,0:T(8,128)S(1)} %copy-done.3, f32[512,32]{1,0:T(8,128)S(1)} %get-tuple-element.176.refs_2_, bf16[512,1536]{1,0:T(8,128)(2,1)S(1)} %get-tuple-element.149.refs_1_.refs_3_, ...), custom_call_target="tpu_custom_call" | custom-call | flops 1000 | bytes 1000 | tf_op jit(solution)/shard_map/forecast_kernel/pallas_call | solution.py:53
  84.9 3.0 %collective-permute-start.23 = (bf16[2,352,128]{2,1,0:T(8,128)(2,1)S(1)}, bf16[2,352,128]{2,1,0:T(8,128)(2,1)S(1)}, u32[]{:S(2)}, u32[]{:S(2)}) collective-permute-start(bf16[2,352,128]{2,1,0:T(8,128)(2,1)S(1)} %add_kernel.23.refs_2_.refs_0_), channel_id=1, source_target_pairs={{0,16},{1,17},{2,18},{3,19},{4,20},{5,21},{6,22},{7,23},{8,24},{9,... | collective-permute-start | bytes 540680 | tf_op jit(solution)/shard_map/tokens16/ppermute | solution.py:535
  87.9 5.9 %collective-permute-done.20.refs_1_ = bf16[4,288,128]{2,1,0:T(8,128)(2,1)S(1)} collective-permute-done((bf16[4,288,128]{2,1,0:T(8,128)(2,1)S(1)}, bf16[4,288,128]{2,1,0:T(8,128)(2,1)S(1)}, u32[]{:S(2)}, u32[]{:S(2)}) %collective-permute-start.20) | collective-permute-done | bytes 294944 | tf_op jit(solution)/shard_map/columns16/ppermute | solution.py:535
  93.9 2.4 %collective-permute-start.28 = (bf16[2,288,128]{2,1,0:T(8,128)(2,1)S(1)}, bf16[2,288,128]{2,1,0:T(8,128)(2,1)S(1)}, u32[]{:S(2)}, u32[]{:S(2)}) collective-permute-start(bf16[2,288,128]{2,1,0:T(8,128)(2,1)S(1)} %get-tuple-element.217), channel_id=1, source_target_pairs={{0,1},{1,0},{2,3},{3,2},{4,5},{5,4},{6,7},{7,6},{8,9},{9,8},{10,11... | collective-permute-start | bytes 442376 | tf_op jit(solution)/shard_map/columns1/ppermute | solution.py:535
  96.4 3.5 %collective-permute-start.27 = (bf16[2,208,128]{2,1,0:T(8,128)(2,1)S(1)}, bf16[2,208,128]{2,1,0:T(8,128)(2,1)S(1)}, u32[]{:S(2)}, u32[]{:S(2)}) collective-permute-start(bf16[2,208,128]{2,1,0:T(8,128)(2,1)S(1)} %get-tuple-element.213.refs_2_), channel_id=1, source_target_pairs={{0,8},{1,9},{2,10},{3,11},{4,12},{5,13},{6,14},{7,15},{8,0},{9,1},... | collective-permute-start | bytes 319496 | tf_op jit(solution)/shard_map/ffn8/ppermute | solution.py:535
  117.7 8.3 %collective-permute-done.38.refs_3_ = bf16[4,208,128]{2,1,0:T(8,128)(2,1)S(1)} collective-permute-done((bf16[4,208,128]{2,1,0:T(8,128)(2,1)S(1)}, bf16[4,208,128]{2,1,0:T(8,128)(2,1)S(1)}, u32[]{:S(2)}, u32[]{:S(2)}) %collective-permute-start.38) | collective-permute-done | bytes 213024 | tf_op jit(solution)/shard_map/ffn16/ppermute | solution.py:535
  129.0 6.0 %collective-permute-done.42.refs_3_ = bf16[8,208,128]{2,1,0:T(8,128)(2,1)S(1)} collective-permute-done((bf16[8,208,128]{2,1,0:T(8,128)(2,1)S(1)}, bf16[8,208,128]{2,1,0:T(8,128)(2,1)S(1)}, u32[]{:S(2)}, u32[]{:S(2)}) %collective-permute-start.42) | collective-permute-done | bytes 426016 | tf_op jit(solution)/shard_map/ffn4/ppermute | solution.py:535
  137.1 2.8 %unpack_tokens.1 = (f32[384,512]{1,0:T(8,128)}, f32[384,512]{1,0:T(8,128)}, f32[384,512]{1,0:T(8,128)}, f32[512,384]{1,0:T(8,128)}, f32[1536,384]{1,0:T(8,128)},...) custom-call(bf16[16,352,128]{2,1,0:T(8,128)(2,1)S(1)} %join_kernel.13.refs_4_.refs_0_, ...), custom_call_target="tpu_custom_call" | custom-call | flops 1000 | bytes 1000 | tf_op jit(solution)/shard_map/unpack_tokens/pallas_call | solution.py:53
  140.9 3.4 %unpack_ffn.1 = (f32[384,1536]{1,0:T(8,128)}, f32[384,1536]{1,0:T(8,128)}, f32[1536,384]{1,0:T(8,128)}, f32[1536]{0:T(1024)}, f32[384]{0:T(512)}) custom-call(bf16[16,448,128]{2,1,0:T(8,128)(2,1)S(1)} %join_kernel.14.refs_2_.refs_0_, bf16[16,448,128]{2,1,0:T(8,128)(2,1)S(1)} %collective-permute-done.43.refs_1_, f32[384]{0:T(512)S(1)} %copy-done.9), custom_call_target="tpu_custom_call" | custom-call | flops 1000 | bytes 1000 | tf_op jit(solution)/shard_map/unpack_ffn/pallas_call | solution.py:53
  (131 shorter events, 53.5 us)
Async XLA Ops:
  2.3 15.4 %collective-permute-start.1 = (bf16[288,768]{1,0:T(8,128)(2,1)S(1)}, bf16[288,768]{1,0:T(8,128)(2,1)S(1)}, u32[]{:S(2)}, u32[]{:S(2)}) collective-permute-start(bf16[288,768]{1,0:T(8,128)(2,1)S(1)} %get-tuple-element.147), channel_id=1, source_target_pairs={{0,1},{1,0},{2,3},{3,2},{4,5},{5,4},{6,7},{7,6},{8,9},{9,8},{10,11... | collective-permute-start | bytes 1327112 | tf_op jit(solution)/shard_map/ppermute | solution.py:535
  5.3 17.3 %collective-permute-start = (bf16[288,512]{1,0:T(8,128)(2,1)S(1)}, bf16[288,512]{1,0:T(8,128)(2,1)S(1)}, u32[]{:S(2)}, u32[]{:S(2)}) collective-permute-start(bf16[288,512]{1,0:T(8,128)(2,1)S(1)} %get-tuple-element.133.refs_16_), channel_id=1, source_target_pairs={{0,1},{1,0},{2,3},{3,2},{4,5},{5,4},{6,7},{7,6},{8,9},{9,8},{10,11... | collective-permute-start | bytes 884744 | tf_op jit(solution)/shard_map/ppermute | solution.py:535
  5.4 21.1 %collective-permute-start.3 = (bf16[288,384]{1,0:T(8,128)(2,1)S(1)}, bf16[288,384]{1,0:T(8,128)(2,1)S(1)}, u32[]{:S(2)}, u32[]{:S(2)}) collective-permute-start(bf16[288,384]{1,0:T(8,128)(2,1)S(1)} %bitcast.7), channel_id=1, source_target_pairs={{0,1},{1,0},{2,3},{3,2},{4,5},{5,4},{6,7},{7,6},{8,9},{9,8},{10,11... | collective-permute-start | bytes 663560 | tf_op jit(solution)/shard_map/ppermute | solution.py:535
  24.4 21.4 %collective-permute-start.7 = (bf16[16,288,128]{2,1,0:T(8,128)(2,1)S(1)}, bf16[16,288,128]{2,1,0:T(8,128)(2,1)S(1)}, u32[]{:S(2)}, u32[]{:S(2)}) collective-permute-start(bf16[16,288,128]{2,1,0:T(8,128)(2,1)S(1)} %get-tuple-element.181), channel_id=1, source_target_pairs={{0,2},{1,3},{2,0},{3,1},{4,6},{5,7},{6,4},{7,5},{8,10},{9,11},{10,... | collective-permute-start | bytes 3538952 | tf_op jit(solution)/shard_map/columns2/ppermute | solution.py:535
  42.1 14.7 %collective-permute-start.10 = (bf16[8,240,128]{2,1,0:T(8,128)(2,1)S(1)}, bf16[8,240,128]{2,1,0:T(8,128)(2,1)S(1)}, u32[]{:S(2)}, u32[]{:S(2)}) collective-permute-start(bf16[8,240,128]{2,1,0:T(8,128)(2,1)S(1)} %get-tuple-element.188), channel_id=1, source_target_pairs={{0,1},{1,0},{2,3},{3,2},{4,5},{5,4},{6,7},{7,6},{8,9},{9,8},{10,11... | collective-permute-start | bytes 1474568 | tf_op jit(solution)/shard_map/ffn1/ppermute | solution.py:535
  44.2 12.7 %collective-permute-start.11 = (bf16[8,208,128]{2,1,0:T(8,128)(2,1)S(1)}, bf16[8,208,128]{2,1,0:T(8,128)(2,1)S(1)}, u32[]{:S(2)}, u32[]{:S(2)}) collective-permute-start(bf16[8,208,128]{2,1,0:T(8,128)(2,1)S(1)} %get-tuple-element.189), channel_id=1, source_target_pairs={{0,4},{1,5},{2,6},{3,7},{4,0},{5,1},{6,2},{7,3},{8,12},{9,13},{10,... | collective-permute-start | bytes 1277960 | tf_op jit(solution)/shard_map/ffn4/ppermute | solution.py:535
  46.1 21.6 %collective-permute-start.14 = (bf16[8,288,128]{2,1,0:T(8,128)(2,1)S(1)}, bf16[8,288,128]{2,1,0:T(8,128)(2,1)S(1)}, u32[]{:S(2)}, u32[]{:S(2)}) collective-permute-start(bf16[8,288,128]{2,1,0:T(8,128)(2,1)S(1)} %get-tuple-element.195), channel_id=1, source_target_pairs={{0,8},{1,9},{2,10},{3,11},{4,12},{5,13},{6,14},{7,15},{8,0},{9,1},... | collective-permute-start | bytes 1769480 | tf_op jit(solution)/shard_map/columns8/ppermute | solution.py:535
  48.0 17.3 %collective-permute-start.9 = (bf16[8,192,128]{2,1,0:T(8,128)(2,1)S(1)}, bf16[8,192,128]{2,1,0:T(8,128)(2,1)S(1)}, u32[]{:S(2)}, u32[]{:S(2)}) collective-permute-start(bf16[8,192,128]{2,1,0:T(8,128)(2,1)S(1)} %get-tuple-element.186), channel_id=1, source_target_pairs={{0,4},{1,5},{2,6},{3,7},{4,0},{5,1},{6,2},{7,3},{8,12},{9,13},{10,... | collective-permute-start | bytes 1179656 | tf_op jit(solution)/shard_map/tokens4/ppermute | solution.py:535
  48.6 14.5 %collective-permute-start.8 = (bf16[8,160,128]{2,1,0:T(8,128)(2,1)S(1)}, bf16[8,160,128]{2,1,0:T(8,128)(2,1)S(1)}, u32[]{:S(2)}, u32[]{:S(2)}) collective-permute-start(bf16[8,160,128]{2,1,0:T(8,128)(2,1)S(1)} %get-tuple-element.184), channel_id=1, source_target_pairs={{0,1},{1,0},{2,3},{3,2},{4,5},{5,4},{6,7},{7,6},{8,9},{9,8},{10,11... | collective-permute-start | bytes 983048 | tf_op jit(solution)/shard_map/tokens1/ppermute | solution.py:535
  57.1 23.9 %collective-permute-start.16 = (bf16[4,240,128]{2,1,0:T(8,128)(2,1)S(1)}, bf16[4,240,128]{2,1,0:T(8,128)(2,1)S(1)}, u32[]{:S(2)}, u32[]{:S(2)}) collective-permute-start(bf16[4,240,128]{2,1,0:T(8,128)(2,1)S(1)} %get-tuple-element.201), channel_id=1, source_target_pairs={{0,4},{1,5},{2,6},{3,7},{4,0},{5,1},{6,2},{7,3},{8,12},{9,13},{10,... | collective-permute-start | bytes 737288 | tf_op jit(solution)/shard_map/ffn4/ppermute | solution.py:535
  58.7 22.3 %collective-permute-start.17 = (bf16[4,208,128]{2,1,0:T(8,128)(2,1)S(1)}, bf16[4,208,128]{2,1,0:T(8,128)(2,1)S(1)}, u32[]{:S(2)}, u32[]{:S(2)}) collective-permute-start(bf16[4,208,128]{2,1,0:T(8,128)(2,1)S(1)} %get-tuple-element.202), channel_id=1, source_target_pairs={{0,16},{1,17},{2,18},{3,19},{4,20},{5,21},{6,22},{7,23},{8,24},{9,... | collective-permute-start | bytes 638984 | tf_op jit(solution)/shard_map/ffn16/ppermute | solution.py:535
  67.7 10.3 %collective-permute-start.5 = (bf16[288]{0:T(512)(128)(2,1)S(1)}, bf16[288]{0:T(512)(128)(2,1)S(1)}, u32[]{:S(2)}, u32[]{:S(2)}) collective-permute-start(bf16[288]{0:T(512)(128)(2,1)S(1)} %copy-done.10), channel_id=1, source_target_pairs={{0,1},{1,0},{2,3},{3,2},{4,5},{5,4},{6,7},{7,6},{8,9},{9,8},{10,11... | collective-permute-start | bytes 1736 | tf_op jit(solution)/shard_map/ppermute | solution.py:535
  72.8 21.0 %collective-permute-start.20 = (bf16[4,288,128]{2,1,0:T(8,128)(2,1)S(1)}, bf16[4,288,128]{2,1,0:T(8,128)(2,1)S(1)}, u32[]{:S(2)}, u32[]{:S(2)}) collective-permute-start(bf16[4,288,128]{2,1,0:T(8,128)(2,1)S(1)} %get-tuple-element.208), channel_id=1, source_target_pairs={{0,16},{1,17},{2,18},{3,19},{4,20},{5,21},{6,22},{7,23},{8,24},{9,... | collective-permute-start | bytes 884744 | tf_op jit(solution)/shard_map/columns16/ppermute | solution.py:535
  81.9 14.4 %collective-permute-start.18 = (bf16[2,240,128]{2,1,0:T(8,128)(2,1)S(1)}, bf16[2,240,128]{2,1,0:T(8,128)(2,1)S(1)}, u32[]{:S(2)}, u32[]{:S(2)}) collective-permute-start(bf16[2,240,128]{2,1,0:T(8,128)(2,1)S(1)} %get-tuple-element.205), channel_id=1, source_target_pairs={{0,8},{1,9},{2,10},{3,11},{4,12},{5,13},{6,14},{7,15},{8,0},{9,1},... | collective-permute-start | bytes 368648 | tf_op jit(solution)/shard_map/ffn8/ppermute | solution.py:535
  82.0 14.2 %collective-permute-start.19 = (bf16[2,208,128]{2,1,0:T(8,128)(2,1)S(1)}, bf16[2,208,128]{2,1,0:T(8,128)(2,1)S(1)}, u32[]{:S(2)}, u32[]{:S(2)}) collective-permute-start(bf16[2,208,128]{2,1,0:T(8,128)(2,1)S(1)} %get-tuple-element.207), channel_id=1, source_target_pairs={{0,1},{1,0},{2,3},{3,2},{4,5},{5,4},{6,7},{7,6},{8,9},{9,8},{10,11... | collective-permute-start | bytes 319496 | tf_op jit(solution)/shard_map/ffn1/ppermute | solution.py:535
  83.4 16.5 %collective-permute-start.15 = (bf16[288,512]{1,0:T(8,128)(2,1)S(1)}, bf16[288,512]{1,0:T(8,128)(2,1)S(1)}, u32[]{:S(2)}, u32[]{:S(2)}) collective-permute-start(bf16[288,512]{1,0:T(8,128)(2,1)S(1)} %get-tuple-element.199), channel_id=1, source_target_pairs={{0,1},{1,0},{2,3},{3,2},{4,5},{5,4},{6,7},{7,6},{8,9},{9,8},{10,11... | collective-permute-start | bytes 884744 | tf_op jit(solution)/shard_map/ppermute | solution.py:535
  84.9 16.1 %collective-permute-start.23 = (bf16[2,352,128]{2,1,0:T(8,128)(2,1)S(1)}, bf16[2,352,128]{2,1,0:T(8,128)(2,1)S(1)}, u32[]{:S(2)}, u32[]{:S(2)}) collective-permute-start(bf16[2,352,128]{2,1,0:T(8,128)(2,1)S(1)} %add_kernel.23.refs_2_.refs_0_), channel_id=1, source_target_pairs={{0,16},{1,17},{2,18},{3,19},{4,20},{5,21},{6,22},{7,23},{8,24},{9,... | collective-permute-start | bytes 540680 | tf_op jit(solution)/shard_map/tokens16/ppermute | solution.py:535
  102.5 11.0 %collective-permute-start.31 = (bf16[2,288,128]{2,1,0:T(8,128)(2,1)S(1)}, bf16[2,288,128]{2,1,0:T(8,128)(2,1)S(1)}, u32[]{:S(2)}, u32[]{:S(2)}) collective-permute-start(bf16[2,288,128]{2,1,0:T(8,128)(2,1)S(1)} %add_kernel.27.refs_4_.refs_0_), channel_id=1, source_target_pairs={{0,4},{1,5},{2,6},{3,7},{4,0},{5,1},{6,2},{7,3},{8,12},{9,13},{10,... | collective-permute-start | bytes 442376 | tf_op jit(solution)/shard_map/columns4/ppermute | solution.py:535
  111.7 14.4 %collective-permute-start.37 = (bf16[4,240,128]{2,1,0:T(8,128)(2,1)S(1)}, bf16[4,240,128]{2,1,0:T(8,128)(2,1)S(1)}, u32[]{:S(2)}, u32[]{:S(2)}) collective-permute-start(bf16[4,240,128]{2,1,0:T(8,128)(2,1)S(1)} %get-tuple-element.225.refs_0_), channel_id=1, source_target_pairs={{0,4},{1,5},{2,6},{3,7},{4,0},{5,1},{6,2},{7,3},{8,12},{9,13},{10,... | collective-permute-start | bytes 737288 | tf_op jit(solution)/shard_map/ffn4/ppermute | solution.py:535
  112.0 14.0 %collective-permute-start.38 = (bf16[4,208,128]{2,1,0:T(8,128)(2,1)S(1)}, bf16[4,208,128]{2,1,0:T(8,128)(2,1)S(1)}, u32[]{:S(2)}, u32[]{:S(2)}) collective-permute-start(bf16[4,208,128]{2,1,0:T(8,128)(2,1)S(1)} %get-tuple-element.222.refs_2_), channel_id=1, source_target_pairs={{0,16},{1,17},{2,18},{3,19},{4,20},{5,21},{6,22},{7,23},{8,24},{9,... | collective-permute-start | bytes 638984 | tf_op jit(solution)/shard_map/ffn16/ppermute | solution.py:535
  113.6 14.9 %collective-permute-start.36 = (bf16[2,288,128]{2,1,0:T(8,128)(2,1)S(1)}, bf16[2,288,128]{2,1,0:T(8,128)(2,1)S(1)}, u32[]{:S(2)}, u32[]{:S(2)}) collective-permute-start(bf16[2,288,128]{2,1,0:T(8,128)(2,1)S(1)} %add_kernel.29.refs_4_.refs_0_), channel_id=1, source_target_pairs={{0,16},{1,17},{2,18},{3,19},{4,20},{5,21},{6,22},{7,23},{8,24},{9,... | collective-permute-start | bytes 442376 | tf_op jit(solution)/shard_map/columns16/ppermute | solution.py:535
  115.1 13.7 %collective-permute-start.35 = (bf16[8,192,128]{2,1,0:T(8,128)(2,1)S(1)}, bf16[8,192,128]{2,1,0:T(8,128)(2,1)S(1)}, u32[]{:S(2)}, u32[]{:S(2)}) collective-permute-start(bf16[8,192,128]{2,1,0:T(8,128)(2,1)S(1)} %get-tuple-element.224.refs_2_), channel_id=1, source_target_pairs={{0,4},{1,5},{2,6},{3,7},{4,0},{5,1},{6,2},{7,3},{8,12},{9,13},{10,... | collective-permute-start | bytes 1179656 | tf_op jit(solution)/shard_map/tokens4/ppermute | solution.py:535
  116.9 11.9 %collective-permute-start.34 = (bf16[8,160,128]{2,1,0:T(8,128)(2,1)S(1)}, bf16[8,160,128]{2,1,0:T(8,128)(2,1)S(1)}, u32[]{:S(2)}, u32[]{:S(2)}) collective-permute-start(bf16[8,160,128]{2,1,0:T(8,128)(2,1)S(1)} %get-tuple-element.223.refs_4_.refs_0_), channel_id=1, source_target_pairs={{0,1},{1,0},{2,3},{3,2},{4,5},{5,4},{6,7},{7,6},{8,9},{9,8},{10,11... | collective-permute-start | bytes 983048 | tf_op jit(solution)/shard_map/tokens1/ppermute | solution.py:535
  126.1 10.2 %collective-permute-start.41 = (bf16[8,240,128]{2,1,0:T(8,128)(2,1)S(1)}, bf16[8,240,128]{2,1,0:T(8,128)(2,1)S(1)}, u32[]{:S(2)}, u32[]{:S(2)}) collective-permute-start(bf16[8,240,128]{2,1,0:T(8,128)(2,1)S(1)} %get-tuple-element.227.refs_0_), channel_id=1, source_target_pairs={{0,1},{1,0},{2,3},{3,2},{4,5},{5,4},{6,7},{7,6},{8,9},{9,8},{10,11... | collective-permute-start | bytes 1474568 | tf_op jit(solution)/shard_map/ffn1/ppermute | solution.py:535
  (34 other events, 201.1 us)
